TPU v7x, 128 devices: a whole 4x4x4 slice. The times are simulated.
128 devices in a mesh: chan: 4 (over z_lo, core), blk: 32 (over x, z_hi, y).
Axes of the slice: x: 4, y: 4, z: 4 (z_hi: 2, z_lo: 2; z = z_hi * 2 + z_lo), core: 2. Of those that a mesh axis runs over, the one named last changes fastest.
Arguments:
- voltages: bfloat16 [4096, 2, 2, 4336], P(('blk', 'chan')), may hold values from -6 to 6
- filter_taps: float32 [16, 16], replicated, may hold values from -1.5 to 1.5
- sample_counts: int32 [4096, 2], P(('blk', 'chan')), may hold values from 1084 to 4336
- keep_list: int32 [128, 4, 24], P(('blk', 'chan')), may hold values from 0 to 32, as said below
Outputs:
- visibility: float32 [2, 32, 4096, 2176], P(None, 'chan', 'blk')
Inputs may be any that keep to these rules, and one draw needn't show every extreme that they name: keep_list[s, g, :] holds, in increasing order, distinct indices within source block s (below 32) of the inputs unflagged for channel group g, then 32 in every unused slot; each list has 12 to 24 indices, and in every draw, for some channel group, the 4 source blocks s with the same s // 4 all list 24 indices.
All inputs are finite; a program needn't handle non-finite values.
Results may differ from a plain program's by a relative error of at most 0.0035.
Values may be sent and summed in bfloat16 or wider, within the bound.
No kernel may reach another device: no remote copies, remote signals or barrier semaphores. Data moves between devices by JAX's collectives and lax.ppermute only.
A program may use at most 320 MiB of HBM per device.

v0:
```python
import math

import jax
import jax.numpy as jnp
from jax import lax
from jax.sharding import PartitionSpec as P


def shifted(value, axis, steps):
    count = lax.axis_size(axis)
    pairs = [(source, (source + steps) % count) for source in range(count)]
    return lax.ppermute(value, axis, pairs)


def filter_bank(voltages, filter_taps, sample_counts, spectra_len):
    in_count, coarse, _, samples = voltages.shape
    tap_count, fft_len = filter_taps.shape
    frames = voltages.astype(jnp.float32).reshape(in_count, coarse, 2, samples // fft_len, fft_len)
    filtered = frames[:, :, :, 0:spectra_len, :] * filter_taps[0]
    for tap_index in range(1, tap_count):
        filtered = (
            filtered
            + frames[:, :, :, tap_index : tap_index + spectra_len, :] * filter_taps[tap_index]
        )
    bin_index = jnp.arange(fft_len, dtype=jnp.int32)
    phase_angle = (
        2.0
        * math.pi
        / fft_len
        * (bin_index[:, None] * bin_index[None, :] % fft_len).astype(jnp.float32)
    )
    cosine = jnp.cos(phase_angle)
    sine_table = jnp.sin(phase_angle)
    cosine_component_source = filtered[:, :, 0]
    imaginary_input = filtered[:, :, 1]
    highest = lax.Precision.HIGHEST
    real_out = jnp.einsum(
        "ictp,fp->icft", cosine_component_source, cosine, precision=highest
    ) + jnp.einsum("ictp,fp->icft", imaginary_input, sine_table, precision=highest)
    imag_out = jnp.einsum("ictp,fp->icft", imaginary_input, cosine, precision=highest) - jnp.einsum(
        "ictp,fp->icft", cosine_component_source, sine_table, precision=highest
    )
    rescale = jnp.sqrt(samples / (fft_len * sample_counts.astype(jnp.float32)))
    spectra = jnp.stack([real_out, imag_out], axis=3) * rescale[:, :, None, None, None]
    return spectra.reshape(in_count, coarse * fft_len, 2, spectra_len).astype(jnp.bfloat16)


def shards(voltages, filter_taps, sample_counts, keep_list):
    chan_count = lax.axis_size("chan")
    blk_count = lax.axis_size("blk")
    in_count = voltages.shape[0]
    fft_len = filter_taps.shape[1]
    tap_count = filter_taps.shape[0]
    spectra_len = voltages.shape[3] // fft_len - tap_count + 1
    spectra = filter_bank(voltages, filter_taps, sample_counts, spectra_len)
    fine_channel_count = spectra.shape[1]
    group_fine = fine_channel_count // chan_count
    row_width = group_fine * 2 * spectra_len
    grouped = spectra.reshape(in_count, chan_count, row_width)
    flag_lists = keep_list[0]
    positions = jnp.arange(in_count, dtype=jnp.int32)
    picked = (flag_lists[:, :, None] == positions).astype(jnp.bfloat16)
    outgoing = jnp.einsum(
        "gsi,igl->gsl", picked, grouped, preferred_element_type=jnp.float32
    ).astype(jnp.bfloat16)
    incoming, arrived = (
        lax.all_to_all(outgoing, "chan", split_axis=0, concat_axis=0, tiled=True),
        lax.all_to_all(flag_lists, "chan", split_axis=0, concat_axis=0, tiled=True),
    )
    placing = (arrived[:, :, None] == positions).astype(jnp.bfloat16)
    own_rows = jnp.einsum(
        "csi,csl->cil", placing, incoming, preferred_element_type=jnp.float32
    ).astype(jnp.bfloat16)
    own_block = own_rows.reshape(chan_count * in_count, group_fine, 2 * spectra_len)
    block_inputs = own_block.shape[0]
    half_count = blk_count // 2 + 1
    normalize = 1.0 / math.sqrt(spectra_len)

    def products(remote):
        halves = remote.reshape(block_inputs, group_fine, 2, spectra_len)
        turned = jnp.concatenate([-halves[:, :, 1:2], halves[:, :, 0:1]], axis=2).reshape(
            block_inputs, group_fine, 2 * spectra_len
        )
        paired = jnp.stack([remote, turned])
        return (
            jnp.einsum("ifk,rjfk->rfij", own_block, paired, preferred_element_type=jnp.float32)
            * normalize
        )

    first_tile = products(own_block)[None]

    def advance(travel, unused):
        travel = shifted(travel, "blk", -1)
        return (travel, products(travel))

    _, later_tiles = lax.scan(advance, own_block, None, length=half_count - 1)
    all_tiles = jnp.concatenate([first_tile, later_tiles], axis=0)
    visible = jnp.transpose(all_tiles, (1, 2, 3, 0, 4)).reshape(
        2, group_fine, block_inputs, half_count * block_inputs
    )
    return visible


def solution(mesh):
    in_specs = (
        P(("blk", "chan"), None, None, None),
        P(),
        P(("blk", "chan"), None),
        P(("blk", "chan"), None, None),
    )
    out_specs = P(None, "chan", "blk", None)
    return jax.shard_map(shards, mesh=mesh, in_specs=in_specs, out_specs=out_specs, check_vma=False)
```

profile of v0, /device:TPU:0, one launch (start us, length us, event | category | flops | bytes accessed | tf_op | source)
XLA Modules:
  0.0 829.7 jit_solution(9367300770322787714)
XLA Ops:
  10.0 88.2 %fusion.65 = (f32[32,2,2,256,16]{0,4,3,2,1:T(8,128)}, f32[32,2,2,256,16]{0,4,3,2,1:T(8,128)}, f32[32,2,2,256,16]{0,4,3,2,1:T(8,128)}, f32[32,2,2,256,16]{0,4,3,2...) fusion(f32[32,2,2,271,16]{0,4,3,2,1:T(8,128)} %bitcast.106), kind=kLoop, calls=%fused_computation.86 | loop fusion | bytes 67108864 | tf_op jit(solution)/shard_map/slice | solution.py:19
  160.0 8.3 copy.86
  223.0 11.6 %multiply_add_fusion = f32[32,2,2,256,16]{3,4,1,0,2:T(8,128)S(1)} fusion(f32[32,2,2,256,16]{3,4,1,0,2:T(8,128)} %copy.93, f32[32,2,2,256,16]{3,4,1,0,2:T(8,128)} %copy.92, f32[32,2,2,256,16]{3,4,1,0,2:T(8,128)} %copy.91, f32[32,2,2,256,16]{3,4,1,0,2:T(8,128)} %copy.90, f32[32,2,2,256,16]{3,4,1,0,2:T(8,128)} %copy.89, f32[32,2,2,256,16]{3,4,1,0,2:T(8,128)} %copy.88, ...), kind=kLoop, calls=%fused_computation.20 | loop fusion | flops 16252928 | bytes 35652608 | tf_op jit(solution)/shard_map/add | solution.py:22
  249.9 11.6 %all-to-all-done.1 = bf16[4,24,4096]{2,1,0:T(8,128)(2,1)S(1)} async-done(((bf16[4,24,4096]{2,1,0:T(8,128)(2,1)}), bf16[4,24,4096]{2,1,0:T(8,128)(2,1)S(1)}, u32[]{:S(2)}, u32[]{:S(2)}) %all-to-all-start.1) | async-done | bytes 786464 | tf_op jit(solution)/shard_map/all_to_all | solution.py:67
  272.6 525.2 %while.12 = (s32[]{:T(128)}, bf16[128,8,512]{2,0,1:T(8,128)(2,1)S(1)}, f32[16,2,8,128,128]{3,4,1,2,0:T(8,128)}, bf16[128,8,512]{2,0,1:T(8,128)(2,1)}, s32[]{:T(128)}) while((s32[]{:T(128)}, bf16[128,8,512]{2,0,1:T(8,128)(2,1)S(1)}, f32[16,2,8,128,128]{3,4,1,2,0:T(8,128)}, bf16[128,8,512]{2,0,1:T(8,128)(2,1)}, s32[]{:T(128)}) %tuple.58), condition=%wide.region_1.2_spmd, body=%wide.region_0.1_spmd.sunk | while | flops 272105472 | bytes 18874480 | solution.py:96
  272.6 8.6 %collective-permute-start = (bf16[128,8,512]{2,0,1:T(8,128)(2,1)S(1)}, bf16[128,8,512]{2,0,1:T(8,128)(2,1)S(1)}, u32[]{:S(2)}, u32[]{:S(2)}) collective-permute-start(bf16[128,8,512]{2,0,1:T(8,128)(2,1)S(1)} %get-tuple-element.119), channel_id=1, source_target_pairs={{0,31},{1,0},{2,1},{3,2},{4,3},{5,4},{6,5},{7,6},{8,7},{9,8},{10,9... | collective-permute-start | bytes 3145736 | tf_op jit(solution)/shard_map/while/body/eval_jaxpr/ppermute | solution.py:12
  281.1 22.2 %collective-permute-done = bf16[128,8,512]{2,0,1:T(8,128)(2,1)S(1)} collective-permute-done((bf16[128,8,512]{2,0,1:T(8,128)(2,1)S(1)}, bf16[128,8,512]{2,0,1:T(8,128)(2,1)S(1)}, u32[]{:S(2)}, u32[]{:S(2)}) %collective-permute-start) | collective-permute-done | bytes 1048608 | tf_op jit(solution)/shard_map/while/body/eval_jaxpr/ppermute | solution.py:12
  320.2 21.3 %collective-permute-done = bf16[128,8,512]{2,0,1:T(8,128)(2,1)S(1)} collective-permute-done((bf16[128,8,512]{2,0,1:T(8,128)(2,1)S(1)}, bf16[128,8,512]{2,0,1:T(8,128)(2,1)S(1)}, u32[]{:S(2)}, u32[]{:S(2)}) %collective-permute-start) | collective-permute-done | bytes 1048608 | tf_op jit(solution)/shard_map/while/body/eval_jaxpr/ppermute | solution.py:12
  358.4 20.4 %collective-permute-done = bf16[128,8,512]{2,0,1:T(8,128)(2,1)S(1)} collective-permute-done((bf16[128,8,512]{2,0,1:T(8,128)(2,1)S(1)}, bf16[128,8,512]{2,0,1:T(8,128)(2,1)S(1)}, u32[]{:S(2)}, u32[]{:S(2)}) %collective-permute-start) | collective-permute-done | bytes 1048608 | tf_op jit(solution)/shard_map/while/body/eval_jaxpr/ppermute | solution.py:12
  395.6 19.5 %collective-permute-done = bf16[128,8,512]{2,0,1:T(8,128)(2,1)S(1)} collective-permute-done((bf16[128,8,512]{2,0,1:T(8,128)(2,1)S(1)}, bf16[128,8,512]{2,0,1:T(8,128)(2,1)S(1)}, u32[]{:S(2)}, u32[]{:S(2)}) %collective-permute-start) | collective-permute-done | bytes 1048608 | tf_op jit(solution)/shard_map/while/body/eval_jaxpr/ppermute | solution.py:12
  431.9 18.5 %collective-permute-done = bf16[128,8,512]{2,0,1:T(8,128)(2,1)S(1)} collective-permute-done((bf16[128,8,512]{2,0,1:T(8,128)(2,1)S(1)}, bf16[128,8,512]{2,0,1:T(8,128)(2,1)S(1)}, u32[]{:S(2)}, u32[]{:S(2)}) %collective-permute-start) | collective-permute-done | bytes 1048608 | tf_op jit(solution)/shard_map/while/body/eval_jaxpr/ppermute | solution.py:12
  459.0 8.3 collective-permute-start
  467.3 17.6 %collective-permute-done = bf16[128,8,512]{2,0,1:T(8,128)(2,1)S(1)} collective-permute-done((bf16[128,8,512]{2,0,1:T(8,128)(2,1)S(1)}, bf16[128,8,512]{2,0,1:T(8,128)(2,1)S(1)}, u32[]{:S(2)}, u32[]{:S(2)}) %collective-permute-start) | collective-permute-done | bytes 1048608 | tf_op jit(solution)/shard_map/while/body/eval_jaxpr/ppermute | solution.py:12
  501.8 16.7 %collective-permute-done = bf16[128,8,512]{2,0,1:T(8,128)(2,1)S(1)} collective-permute-done((bf16[128,8,512]{2,0,1:T(8,128)(2,1)S(1)}, bf16[128,8,512]{2,0,1:T(8,128)(2,1)S(1)}, u32[]{:S(2)}, u32[]{:S(2)}) %collective-permute-start) | collective-permute-done | bytes 1048608 | tf_op jit(solution)/shard_map/while/body/eval_jaxpr/ppermute | solution.py:12
  535.3 15.8 %collective-permute-done = bf16[128,8,512]{2,0,1:T(8,128)(2,1)S(1)} collective-permute-done((bf16[128,8,512]{2,0,1:T(8,128)(2,1)S(1)}, bf16[128,8,512]{2,0,1:T(8,128)(2,1)S(1)}, u32[]{:S(2)}, u32[]{:S(2)}) %collective-permute-start) | collective-permute-done | bytes 1048608 | tf_op jit(solution)/shard_map/while/body/eval_jaxpr/ppermute | solution.py:12
  567.9 14.8 %collective-permute-done = bf16[128,8,512]{2,0,1:T(8,128)(2,1)S(1)} collective-permute-done((bf16[128,8,512]{2,0,1:T(8,128)(2,1)S(1)}, bf16[128,8,512]{2,0,1:T(8,128)(2,1)S(1)}, u32[]{:S(2)}, u32[]{:S(2)}) %collective-permute-start) | collective-permute-done | bytes 1048608 | tf_op jit(solution)/shard_map/while/body/eval_jaxpr/ppermute | solution.py:12
  599.6 13.9 %collective-permute-done = bf16[128,8,512]{2,0,1:T(8,128)(2,1)S(1)} collective-permute-done((bf16[128,8,512]{2,0,1:T(8,128)(2,1)S(1)}, bf16[128,8,512]{2,0,1:T(8,128)(2,1)S(1)}, u32[]{:S(2)}, u32[]{:S(2)}) %collective-permute-start) | collective-permute-done | bytes 1048608 | tf_op jit(solution)/shard_map/while/body/eval_jaxpr/ppermute | solution.py:12
  630.3 13.0 %collective-permute-done = bf16[128,8,512]{2,0,1:T(8,128)(2,1)S(1)} collective-permute-done((bf16[128,8,512]{2,0,1:T(8,128)(2,1)S(1)}, bf16[128,8,512]{2,0,1:T(8,128)(2,1)S(1)}, u32[]{:S(2)}, u32[]{:S(2)}) %collective-permute-start) | collective-permute-done | bytes 1048608 | tf_op jit(solution)/shard_map/while/body/eval_jaxpr/ppermute | solution.py:12
  660.2 12.3 %collective-permute-done = bf16[128,8,512]{2,0,1:T(8,128)(2,1)S(1)} collective-permute-done((bf16[128,8,512]{2,0,1:T(8,128)(2,1)S(1)}, bf16[128,8,512]{2,0,1:T(8,128)(2,1)S(1)}, u32[]{:S(2)}, u32[]{:S(2)}) %collective-permute-start) | collective-permute-done | bytes 1048608 | tf_op jit(solution)/shard_map/while/body/eval_jaxpr/ppermute | solution.py:12
  689.3 12.3 %collective-permute-done = bf16[128,8,512]{2,0,1:T(8,128)(2,1)S(1)} collective-permute-done((bf16[128,8,512]{2,0,1:T(8,128)(2,1)S(1)}, bf16[128,8,512]{2,0,1:T(8,128)(2,1)S(1)}, u32[]{:S(2)}, u32[]{:S(2)}) %collective-permute-start) | collective-permute-done | bytes 1048608 | tf_op jit(solution)/shard_map/while/body/eval_jaxpr/ppermute | solution.py:12
  718.5 12.3 %collective-permute-done = bf16[128,8,512]{2,0,1:T(8,128)(2,1)S(1)} collective-permute-done((bf16[128,8,512]{2,0,1:T(8,128)(2,1)S(1)}, bf16[128,8,512]{2,0,1:T(8,128)(2,1)S(1)}, u32[]{:S(2)}, u32[]{:S(2)}) %collective-permute-start) | collective-permute-done | bytes 1048608 | tf_op jit(solution)/shard_map/while/body/eval_jaxpr/ppermute | solution.py:12
  747.7 12.3 %collective-permute-done = bf16[128,8,512]{2,0,1:T(8,128)(2,1)S(1)} collective-permute-done((bf16[128,8,512]{2,0,1:T(8,128)(2,1)S(1)}, bf16[128,8,512]{2,0,1:T(8,128)(2,1)S(1)}, u32[]{:S(2)}, u32[]{:S(2)}) %collective-permute-start) | collective-permute-done | bytes 1048608 | tf_op jit(solution)/shard_map/while/body/eval_jaxpr/ppermute | solution.py:12
  776.9 12.3 %collective-permute-done = bf16[128,8,512]{2,0,1:T(8,128)(2,1)S(1)} collective-permute-done((bf16[128,8,512]{2,0,1:T(8,128)(2,1)S(1)}, bf16[128,8,512]{2,0,1:T(8,128)(2,1)S(1)}, u32[]{:S(2)}, u32[]{:S(2)}) %collective-permute-start) | collective-permute-done | bytes 1048608 | tf_op jit(solution)/shard_map/while/body/eval_jaxpr/ppermute | solution.py:12
  811.5 18.0 %copy.69 = f32[2,8,128,2176]{3,2,1,0:T(8,128)} copy(f32[2,8,128,2176]{2,3,1,0:T(8,128)} %bitcast.108) | data formatting | bytes 35651584 | tf_op jit(solution)/shard_map/reshape | solution.py:98
  (164 shorter events, 418.7 us)
Async XLA Ops:
  0.0 246.2 %all-to-all-start = ((s32[4,1,24]{2,1,0:T(1,128)}), s32[4,1,24]{2,1,0:T(1,128)S(1)}, u32[]{:S(2)}, u32[]{:S(2)}) async-start(s32[4,1,24]{2,1,0:T(1,128)} %bitcast.116), calls=%async_computation | async-start | bytes 4096 | tf_op jit(solution)/shard_map/all_to_all | solution.py:68
  215.2 7.8 copy-start.1
  238.8 2.2 copy-start.3
  241.1 2.9 copy-start.2
  246.2 15.3 %all-to-all-start.1 = ((bf16[4,24,4096]{2,1,0:T(8,128)(2,1)}), bf16[4,24,4096]{2,1,0:T(8,128)(2,1)S(1)}, u32[]{:S(2)}, u32[]{:S(2)}) async-start(bf16[4,24,4096]{2,1,0:T(8,128)(2,1)} %convolution_convert_fusion.1), calls=%async_computation.1 | async-start | bytes 1572864 | tf_op jit(solution)/shard_map/all_to_all | solution.py:67
  269.8 1.0 copy-start
  272.6 30.8 %collective-permute-start = (bf16[128,8,512]{2,0,1:T(8,128)(2,1)S(1)}, bf16[128,8,512]{2,0,1:T(8,128)(2,1)S(1)}, u32[]{:S(2)}, u32[]{:S(2)}) collective-permute-start(bf16[128,8,512]{2,0,1:T(8,128)(2,1)S(1)} %get-tuple-element.119), channel_id=1, source_target_pairs={{0,31},{1,0},{2,1},{3,2},{4,3},{5,4},{6,5},{7,6},{8,7},{9,8},{10,9... | collective-permute-start | bytes 3145736 | tf_op jit(solution)/shard_map/while/body/eval_jaxpr/ppermute | solution.py:12
  311.9 29.6 %collective-permute-start = (bf16[128,8,512]{2,0,1:T(8,128)(2,1)S(1)}, bf16[128,8,512]{2,0,1:T(8,128)(2,1)S(1)}, u32[]{:S(2)}, u32[]{:S(2)}) collective-permute-start(bf16[128,8,512]{2,0,1:T(8,128)(2,1)S(1)} %get-tuple-element.119), channel_id=1, source_target_pairs={{0,31},{1,0},{2,1},{3,2},{4,3},{5,4},{6,5},{7,6},{8,7},{9,8},{10,9... | collective-permute-start | bytes 3145736 | tf_op jit(solution)/shard_map/while/body/eval_jaxpr/ppermute | solution.py:12
  350.1 28.7 %collective-permute-start = (bf16[128,8,512]{2,0,1:T(8,128)(2,1)S(1)}, bf16[128,8,512]{2,0,1:T(8,128)(2,1)S(1)}, u32[]{:S(2)}, u32[]{:S(2)}) collective-permute-start(bf16[128,8,512]{2,0,1:T(8,128)(2,1)S(1)} %get-tuple-element.119), channel_id=1, source_target_pairs={{0,31},{1,0},{2,1},{3,2},{4,3},{5,4},{6,5},{7,6},{8,7},{9,8},{10,9... | collective-permute-start | bytes 3145736 | tf_op jit(solution)/shard_map/while/body/eval_jaxpr/ppermute | solution.py:12
  387.3 27.7 %collective-permute-start = (bf16[128,8,512]{2,0,1:T(8,128)(2,1)S(1)}, bf16[128,8,512]{2,0,1:T(8,128)(2,1)S(1)}, u32[]{:S(2)}, u32[]{:S(2)}) collective-permute-start(bf16[128,8,512]{2,0,1:T(8,128)(2,1)S(1)} %get-tuple-element.119), channel_id=1, source_target_pairs={{0,31},{1,0},{2,1},{3,2},{4,3},{5,4},{6,5},{7,6},{8,7},{9,8},{10,9... | collective-permute-start | bytes 3145736 | tf_op jit(solution)/shard_map/while/body/eval_jaxpr/ppermute | solution.py:12
  423.6 26.8 %collective-permute-start = (bf16[128,8,512]{2,0,1:T(8,128)(2,1)S(1)}, bf16[128,8,512]{2,0,1:T(8,128)(2,1)S(1)}, u32[]{:S(2)}, u32[]{:S(2)}) collective-permute-start(bf16[128,8,512]{2,0,1:T(8,128)(2,1)S(1)} %get-tuple-element.119), channel_id=1, source_target_pairs={{0,31},{1,0},{2,1},{3,2},{4,3},{5,4},{6,5},{7,6},{8,7},{9,8},{10,9... | collective-permute-start | bytes 3145736 | tf_op jit(solution)/shard_map/while/body/eval_jaxpr/ppermute | solution.py:12
  459.0 25.9 %collective-permute-start = (bf16[128,8,512]{2,0,1:T(8,128)(2,1)S(1)}, bf16[128,8,512]{2,0,1:T(8,128)(2,1)S(1)}, u32[]{:S(2)}, u32[]{:S(2)}) collective-permute-start(bf16[128,8,512]{2,0,1:T(8,128)(2,1)S(1)} %get-tuple-element.119), channel_id=1, source_target_pairs={{0,31},{1,0},{2,1},{3,2},{4,3},{5,4},{6,5},{7,6},{8,7},{9,8},{10,9... | collective-permute-start | bytes 3145736 | tf_op jit(solution)/shard_map/while/body/eval_jaxpr/ppermute | solution.py:12
  493.5 25.0 %collective-permute-start = (bf16[128,8,512]{2,0,1:T(8,128)(2,1)S(1)}, bf16[128,8,512]{2,0,1:T(8,128)(2,1)S(1)}, u32[]{:S(2)}, u32[]{:S(2)}) collective-permute-start(bf16[128,8,512]{2,0,1:T(8,128)(2,1)S(1)} %get-tuple-element.119), channel_id=1, source_target_pairs={{0,31},{1,0},{2,1},{3,2},{4,3},{5,4},{6,5},{7,6},{8,7},{9,8},{10,9... | collective-permute-start | bytes 3145736 | tf_op jit(solution)/shard_map/while/body/eval_jaxpr/ppermute | solution.py:12
  527.0 24.0 %collective-permute-start = (bf16[128,8,512]{2,0,1:T(8,128)(2,1)S(1)}, bf16[128,8,512]{2,0,1:T(8,128)(2,1)S(1)}, u32[]{:S(2)}, u32[]{:S(2)}) collective-permute-start(bf16[128,8,512]{2,0,1:T(8,128)(2,1)S(1)} %get-tuple-element.119), channel_id=1, source_target_pairs={{0,31},{1,0},{2,1},{3,2},{4,3},{5,4},{6,5},{7,6},{8,7},{9,8},{10,9... | collective-permute-start | bytes 3145736 | tf_op jit(solution)/shard_map/while/body/eval_jaxpr/ppermute | solution.py:12
  559.6 23.1 %collective-permute-start = (bf16[128,8,512]{2,0,1:T(8,128)(2,1)S(1)}, bf16[128,8,512]{2,0,1:T(8,128)(2,1)S(1)}, u32[]{:S(2)}, u32[]{:S(2)}) collective-permute-start(bf16[128,8,512]{2,0,1:T(8,128)(2,1)S(1)} %get-tuple-element.119), channel_id=1, source_target_pairs={{0,31},{1,0},{2,1},{3,2},{4,3},{5,4},{6,5},{7,6},{8,7},{9,8},{10,9... | collective-permute-start | bytes 3145736 | tf_op jit(solution)/shard_map/while/body/eval_jaxpr/ppermute | solution.py:12
  591.3 22.2 %collective-permute-start = (bf16[128,8,512]{2,0,1:T(8,128)(2,1)S(1)}, bf16[128,8,512]{2,0,1:T(8,128)(2,1)S(1)}, u32[]{:S(2)}, u32[]{:S(2)}) collective-permute-start(bf16[128,8,512]{2,0,1:T(8,128)(2,1)S(1)} %get-tuple-element.119), channel_id=1, source_target_pairs={{0,31},{1,0},{2,1},{3,2},{4,3},{5,4},{6,5},{7,6},{8,7},{9,8},{10,9... | collective-permute-start | bytes 3145736 | tf_op jit(solution)/shard_map/while/body/eval_jaxpr/ppermute | solution.py:12
  622.1 21.3 %collective-permute-start = (bf16[128,8,512]{2,0,1:T(8,128)(2,1)S(1)}, bf16[128,8,512]{2,0,1:T(8,128)(2,1)S(1)}, u32[]{:S(2)}, u32[]{:S(2)}) collective-permute-start(bf16[128,8,512]{2,0,1:T(8,128)(2,1)S(1)} %get-tuple-element.119), channel_id=1, source_target_pairs={{0,31},{1,0},{2,1},{3,2},{4,3},{5,4},{6,5},{7,6},{8,7},{9,8},{10,9... | collective-permute-start | bytes 3145736 | tf_op jit(solution)/shard_map/while/body/eval_jaxpr/ppermute | solution.py:12
  651.9 20.6 %collective-permute-start = (bf16[128,8,512]{2,0,1:T(8,128)(2,1)S(1)}, bf16[128,8,512]{2,0,1:T(8,128)(2,1)S(1)}, u32[]{:S(2)}, u32[]{:S(2)}) collective-permute-start(bf16[128,8,512]{2,0,1:T(8,128)(2,1)S(1)} %get-tuple-element.119), channel_id=1, source_target_pairs={{0,31},{1,0},{2,1},{3,2},{4,3},{5,4},{6,5},{7,6},{8,7},{9,8},{10,9... | collective-permute-start | bytes 3145736 | tf_op jit(solution)/shard_map/while/body/eval_jaxpr/ppermute | solution.py:12
  681.1 20.6 %collective-permute-start = (bf16[128,8,512]{2,0,1:T(8,128)(2,1)S(1)}, bf16[128,8,512]{2,0,1:T(8,128)(2,1)S(1)}, u32[]{:S(2)}, u32[]{:S(2)}) collective-permute-start(bf16[128,8,512]{2,0,1:T(8,128)(2,1)S(1)} %get-tuple-element.119), channel_id=1, source_target_pairs={{0,31},{1,0},{2,1},{3,2},{4,3},{5,4},{6,5},{7,6},{8,7},{9,8},{10,9... | collective-permute-start | bytes 3145736 | tf_op jit(solution)/shard_map/while/body/eval_jaxpr/ppermute | solution.py:12
  710.2 20.6 %collective-permute-start = (bf16[128,8,512]{2,0,1:T(8,128)(2,1)S(1)}, bf16[128,8,512]{2,0,1:T(8,128)(2,1)S(1)}, u32[]{:S(2)}, u32[]{:S(2)}) collective-permute-start(bf16[128,8,512]{2,0,1:T(8,128)(2,1)S(1)} %get-tuple-element.119), channel_id=1, source_target_pairs={{0,31},{1,0},{2,1},{3,2},{4,3},{5,4},{6,5},{7,6},{8,7},{9,8},{10,9... | collective-permute-start | bytes 3145736 | tf_op jit(solution)/shard_map/while/body/eval_jaxpr/ppermute | solution.py:12
  739.4 20.6 %collective-permute-start = (bf16[128,8,512]{2,0,1:T(8,128)(2,1)S(1)}, bf16[128,8,512]{2,0,1:T(8,128)(2,1)S(1)}, u32[]{:S(2)}, u32[]{:S(2)}) collective-permute-start(bf16[128,8,512]{2,0,1:T(8,128)(2,1)S(1)} %get-tuple-element.119), channel_id=1, source_target_pairs={{0,31},{1,0},{2,1},{3,2},{4,3},{5,4},{6,5},{7,6},{8,7},{9,8},{10,9... | collective-permute-start | bytes 3145736 | tf_op jit(solution)/shard_map/while/body/eval_jaxpr/ppermute | solution.py:12
  768.6 20.6 %collective-permute-start = (bf16[128,8,512]{2,0,1:T(8,128)(2,1)S(1)}, bf16[128,8,512]{2,0,1:T(8,128)(2,1)S(1)}, u32[]{:S(2)}, u32[]{:S(2)}) collective-permute-start(bf16[128,8,512]{2,0,1:T(8,128)(2,1)S(1)} %get-tuple-element.119), channel_id=1, source_target_pairs={{0,31},{1,0},{2,1},{3,2},{4,3},{5,4},{6,5},{7,6},{8,7},{9,8},{10,9... | collective-permute-start | bytes 3145736 | tf_op jit(solution)/shard_map/while/body/eval_jaxpr/ppermute | solution.py:12
where the time goes:
time: 841 us; the launch traced here: 830 us
  local copies, waits for them, and re-layouts  268 us (32%)
  waiting for transfers between devices  267 us (32%)
  starting transfers between devices  140 us (17%)
  other arithmetic  98.8 us (12%)
  matrix products  55.2 us (7%)
    ppermute x16, waiting for transfers between devices, shifted(): return lax.ppermute(value, axis, pairs)  255 us
    ppermute x16, starting transfers between devices, shifted(): return lax.ppermute(value, axis, pairs)  133 us
    unnamed x26, local copies, waits for them, and re-layouts  126 us
    slice x1, local copies, waits for them, and re-layouts, filter_bank(): filtered = frames[:, :, :, 0:spectra_len, :] * filter_taps[0]  88.2 us
    dot_general x17, matrix products, products(): jnp.einsum('ifk,rjfk->rfij', own_block, paired, preferred_element_type=jn...  48.3 us
    neg x17, other arithmetic, products(): -halves[:, :, 1:2]  39.9 us
    concatenate x17, other arithmetic, products(): jnp.concatenate([-halves[:, :, 1:2], halves[:, :, 0:1]], axis=2)  38 us
    reshape x1, local copies, waits for them, and re-layouts, shards(): jnp.transpose(all_tiles, (1, 2, 3, 0, 4))  18 us
  transfers between devices with their start and end apart: 18, of which 17 were waited for; matrix products, arithmetic and copies ran while one was open for 29% of the time, Pallas kernels for 0%

commit v1 on v0

v1 whole, which is shorter than its diff:
```python
import math

import jax
import jax.numpy as jnp
import numpy as np
from jax import lax
from jax.experimental import pallas as pl
from jax.experimental.pallas import tpu as pltpu
from jax.sharding import Mesh
from jax.sharding import PartitionSpec as P

TAPS = 16
FFT = 16
STEP = 8
LANES = 128
CHUNKS = LANES // STEP


def trig_table():
    table = np.zeros((2, 2, LANES, 8, 2, STEP), np.float64)
    point = np.arange(LANES) % FFT
    for half in range(2):
        for fine in range(8):
            angle = 2.0 * math.pi * ((8 * half + fine) * point % FFT) / FFT
            cosine, sine = np.cos(angle)[:, None], np.sin(angle)[:, None]
            table[half, 0, :, fine, 0] = cosine
            table[half, 0, :, fine, 1] = -sine
            table[half, 1, :, fine, 0] = sine
            table[half, 1, :, fine, 1] = cosine
    return table.reshape(2, 2 * LANES, LANES).astype(np.float32)


def channelize_kernel(spectra_len, cap, volt, rows, scale, taps, trig, out, frames, weights):
    samples = volt.shape[1]
    tiles = -(-samples // LANES)
    listed = 2 * cap
    point_row = lax.broadcasted_iota(jnp.int32, (LANES, LANES), 0) // FFT
    spec_lane = lax.broadcasted_iota(jnp.int32, (LANES, LANES), 1) % STEP
    lag = point_row - spec_lane
    column = [jnp.broadcast_to(taps[:, m : m + 1], (LANES, LANES)) for m in range(TAPS)]
    for part in range(3):
        shaped = jnp.zeros((LANES, LANES), jnp.float32)
        for m in range(TAPS):
            shaped = jnp.where(lag == m - STEP * part, column[m], shaped)
        both = jnp.concatenate([shaped, shaped], axis=0)
        for half in range(2):
            exact = both * trig[half]
            high = exact.astype(jnp.bfloat16)
            low = (exact - high.astype(jnp.float32)).astype(jnp.bfloat16)
            weights[half, part, :, 0:LANES] = high
            weights[half, part, :, LANES : 2 * LANES] = low
    wanted = rows[...] == lax.broadcasted_iota(jnp.int32, (4 * listed, LANES), 1)
    pick = wanted.astype(jnp.bfloat16)
    for tile in range(tiles):
        width = min(LANES, samples - tile * LANES)
        piece = volt[:, tile * LANES : tile * LANES + width]
        if width < LANES:
            piece = jnp.concatenate([piece, jnp.zeros((LANES, LANES - width), piece.dtype)], axis=1)
        got = jnp.dot(pick, piece, preferred_element_type=jnp.float32).astype(jnp.bfloat16)
        for half in range(2):
            base = 2 * half * listed
            here = slice(tile * listed, (tile + 1) * listed)
            frames[half, here, 0:LANES] = got[base : base + listed]
            frames[half, here, LANES : 2 * LANES] = got[base + listed : base + 2 * listed]
    factor = jnp.sum(jnp.where(wanted, scale[...], 0.0), axis=1, keepdims=True)
    chunk = lax.broadcasted_iota(jnp.int32, (listed, LANES), 1) // STEP
    for half in range(2):
        gain = factor[2 * half * listed : (2 * half + 1) * listed]
        for quarter in range(spectra_len // LANES):
            total = None
            for part in range(3):
                first = (quarter * CHUNKS + part) * listed
                term = jnp.dot(
                    frames[half, first : first + CHUNKS * listed, :],
                    weights[half, part],
                    preferred_element_type=jnp.float32,
                )
                total = term if total is None else total + term
            summed = total[:, 0:LANES] + total[:, LANES : 2 * LANES]
            lines = [summed[n * listed : (n + 1) * listed] * gain for n in range(CHUNKS)]
            bit = 1
            while bit < CHUNKS:
                keep = (chunk & bit) == 0
                fresh = list(lines)
                for n in range(CHUNKS):
                    if n & bit == 0:
                        one, two = lines[n], lines[n | bit]
                        fresh[n] = jnp.where(keep, one, pltpu.roll(two, bit * STEP, 1))
                        fresh[n | bit] = jnp.where(keep, pltpu.roll(one, LANES - bit * STEP, 1), two)
                lines = fresh
                bit *= 2
            for n in range(CHUNKS):
                fine, part = divmod(n, 2)
                lane = (fine * 2 + part) * spectra_len + quarter * LANES
                value = lines[n].astype(jnp.bfloat16)
                out[half, :, lane : lane + LANES] = value[0:cap]
                out[half + 2, :, lane : lane + LANES] = value[cap : 2 * cap]


def channelize(voltages, filter_taps, sample_counts, flag_lists, spectra_len):
    in_count, coarse, _, samples = voltages.shape
    groups, cap = flag_lists.shape
    volt = voltages.reshape(in_count * coarse * 2, samples)
    by_half = jnp.transpose(flag_lists.reshape(2, 2, cap), (1, 0, 2))
    rows = (
        by_half[:, None] * (2 * coarse)
        + 2 * jnp.arange(2, dtype=jnp.int32)[None, None, :, None]
        + jnp.arange(2, dtype=jnp.int32)[None, :, None, None]
    ).reshape(8 * cap, 1)
    gain = jnp.sqrt(samples / (FFT * sample_counts.astype(jnp.float32)))
    gain = jnp.repeat(gain.reshape(-1), 2).reshape(1, -1)
    taps = jnp.tile(filter_taps.T, (LANES // FFT, 1))
    row_width = 8 * 2 * spectra_len
    tiles = -(-samples // LANES)

    def kernel(*refs):
        channelize_kernel(spectra_len, cap, *refs)

    return pl.pallas_call(
        kernel,
        out_shape=jax.ShapeDtypeStruct((groups, cap, row_width), jnp.bfloat16),
        scratch_shapes=[
            pltpu.VMEM((2, tiles * 2 * cap, 2 * LANES), jnp.bfloat16),
            pltpu.VMEM((2, 3, 2 * LANES, 2 * LANES), jnp.bfloat16),
        ],
        compiler_params=pltpu.CompilerParams(vmem_limit_bytes=48 * 1024 * 1024),
        cost_estimate=pl.CostEstimate(flops=4 * 10**9, bytes_accessed=3 * 10**6, transcendentals=0),
        name="channelize",
    )(volt, rows, gain, taps, trig_table())


def place_rows(block, where):
    inputs = LANES
    spots = lax.broadcasted_iota(jnp.int32, (inputs, block.shape[0]), 0)
    one_hot = (spots == where).astype(jnp.bfloat16)
    return jnp.dot(one_hot, block, preferred_element_type=jnp.float32).astype(jnp.bfloat16)


def own_kernel(fine, norm, where_all, block, sides, out):
    width = block.shape[1] // fine
    half = width // 2
    for f in range(fine):
        full = place_rows(block[:, f * width : (f + 1) * width], where_all[0])
        scaled = (full.astype(jnp.float32) * norm).astype(jnp.bfloat16)
        turned = jnp.concatenate([scaled[:, half:], -scaled[:, :half]], axis=1)
        both = jnp.concatenate([scaled, turned], axis=0)
        sides[:, f * width : (f + 1) * width] = both
        got = lax.dot_general(both, full, (((1,), (1,)), ((), ())), preferred_element_type=jnp.float32)
        out[0, f] = got[0:LANES]
        out[1, f] = got[LANES : 2 * LANES]


def pair_kernel(fine, spots, where_all, sides, block, _, out):
    width = block.shape[1] // fine
    for f in range(fine):
        full = place_rows(block[:, f * width : (f + 1) * width], where_all[0])
        got = lax.dot_general(
            sides[:, f * width : (f + 1) * width],
            full,
            (((1,), (1,)), ((), ())),
            preferred_element_type=jnp.float32,
        )
        out[0, f] = got[0:LANES]
        out[1, f] = got[LANES : 2 * LANES]


def correlate_own(block, where_all, own, fine, columns, norm):
    listed, width = block.shape

    def kernel(spot, *refs):
        own_kernel(fine, norm, *refs)

    return pl.pallas_call(
        kernel,
        grid_spec=pltpu.PrefetchScalarGridSpec(
            num_scalar_prefetch=1,
            grid=(1,),
            in_specs=[
                pl.BlockSpec((1, 1, listed), lambda i, s: (s[0], 0, 0)),
                pl.BlockSpec((listed, width), lambda i, s: (0, 0)),
            ],
            out_specs=[
                pl.BlockSpec((2 * LANES, width), lambda i, s: (0, 0)),
                pl.BlockSpec((2, fine, LANES, LANES), lambda i, s: (0, 0, 0, 0)),
            ],
        ),
        out_shape=[
            jax.ShapeDtypeStruct((2 * LANES, width), jnp.bfloat16),
            jax.ShapeDtypeStruct((2, fine, LANES, columns), jnp.float32),
        ],
        compiler_params=pltpu.CompilerParams(vmem_limit_bytes=24 * 1024 * 1024),
        cost_estimate=pl.CostEstimate(flops=10**9, bytes_accessed=4 * 10**6, transcendentals=0),
        name="own_block",
    )(own.reshape(1), where_all, block)


def correlate_pair(result, sides, block, where_all, other, offset, fine):
    listed, width = block.shape
    spots = jnp.stack([other, offset]).astype(jnp.int32)

    def kernel(*refs):
        pair_kernel(fine, *refs)

    return pl.pallas_call(
        kernel,
        grid_spec=pltpu.PrefetchScalarGridSpec(
            num_scalar_prefetch=1,
            grid=(1,),
            in_specs=[
                pl.BlockSpec((1, 1, listed), lambda i, s: (s[0], 0, 0)),
                pl.BlockSpec((2 * LANES, width), lambda i, s: (0, 0)),
                pl.BlockSpec((listed, width), lambda i, s: (0, 0)),
                pl.BlockSpec(memory_space=pl.ANY),
            ],
            out_specs=pl.BlockSpec((2, fine, LANES, LANES), lambda i, s: (0, 0, 0, s[1])),
        ),
        out_shape=jax.ShapeDtypeStruct(result.shape, result.dtype),
        input_output_aliases={4: 0},
        compiler_params=pltpu.CompilerParams(vmem_limit_bytes=24 * 1024 * 1024),
        cost_estimate=pl.CostEstimate(flops=10**9, bytes_accessed=4 * 10**6, transcendentals=0),
        name="pair_block",
    )(spots, where_all, sides, block, result)


def moved(value, axis, steps):
    count = lax.axis_size(axis)
    return lax.ppermute(value, axis, [(s, (s + steps) % count) for s in range(count)])


def shards(voltages, filter_taps, sample_counts, keep_list):
    spectra_len = voltages.shape[3] // FFT - TAPS + 1
    chan_count = lax.axis_size("chan")
    x_count, z_count, y_count = (lax.axis_size(a) for a in ("x", "zh", "y"))
    blocks = x_count * z_count * y_count
    half_count = blocks // 2 + 1
    in_count = voltages.shape[0]
    group, x, z, y = (lax.axis_index(a) for a in ("chan", "x", "zh", "y"))
    cap = keep_list.shape[2]

    every_list = lax.all_gather(keep_list, ("x", "zh", "y", "chan"), axis=0, tiled=True)
    my_lists = lax.dynamic_index_in_dim(every_list, group, 1, keepdims=False)
    my_lists = my_lists.reshape(blocks, chan_count, cap)
    first_row = in_count * jnp.arange(chan_count, dtype=jnp.int32)[:, None]
    where_all = jnp.where(my_lists < in_count, my_lists + first_row, 1 << 20)
    where_all = where_all.reshape(blocks, 1, chan_count * cap)

    outgoing = channelize(voltages, filter_taps, sample_counts, keep_list[0], spectra_len)
    incoming = lax.all_to_all(outgoing, "chan", split_axis=0, concat_axis=0, tiled=True)
    own = incoming.reshape(chan_count * cap, outgoing.shape[2])
    fine = 8

    def number(dx, zz, yy):
        return ((x + dx) % x_count * z_count + zz) * y_count + yy

    me = number(0, z, y)
    sides, result = correlate_own(
        own, where_all, me, fine, half_count * LANES, 1.0 / math.sqrt(spectra_len)
    )

    def pair(result, block, other):
        return correlate_pair(result, sides, block, where_all, other, (other - me) % blocks, fine)

    up, down, far = (y + 1) % y_count, (y + 3) % y_count, (y + 2) % y_count
    flip = 1 - z
    odd = y % 2 == 1
    swap_a = [(0, 1), (1, 0), (2, 3), (3, 2)]
    swap_b = [(0, 3), (3, 0), (1, 2), (2, 1)]

    def relay_a(from_up, from_down):
        return lax.ppermute(jnp.where(odd, from_up, from_down), "y", swap_a)

    def relay_b(from_up, from_down):
        return lax.ppermute(jnp.where(odd, from_down, from_up), "y", swap_b)

    one = moved(own, "x", -1)
    two = moved(one, "x", -1)
    one_up = moved(one, "y", -1)
    one_down = moved(one, "y", 1)
    one_z = moved(one, "zh", 1)
    cross = moved(jnp.where(z == 1, own, two), "zh", 1)
    near_up = moved(jnp.where(y == 0, two, own), "y", -1)
    near_down = moved(jnp.where(y == y_count - 1, own, two), "y", 1)
    cross_up = moved(cross, "y", -1)
    cross_down = moved(cross, "y", 1)
    onez_up = moved(one_up, "zh", 1)
    one_far = relay_b(one_up, one_down)
    near_far = relay_a(near_up, near_down)
    onez_down = moved(one_down, "zh", 1)
    cross_far = relay_b(cross_up, cross_down)
    onez_far = relay_a(onez_up, onez_down)

    def near(yy):
        return number(jnp.where(yy > y, 0, 2), z, yy)

    def crossed(yy):
        return number(jnp.where(z == 0, 0, 2), flip, yy)

    for block, other in (
        (one, number(1, z, y)),
        (two, number(2, z, y)),
        (one_up, number(1, z, up)),
        (one_down, number(1, z, down)),
        (one_z, number(1, flip, y)),
        (near_up, near(up)),
        (near_down, near(down)),
        (cross, crossed(y)),
        (cross_up, crossed(up)),
        (cross_down, crossed(down)),
        (onez_up, number(1, flip, up)),
        (one_far, number(1, z, far)),
        (near_far, near(far)),
        (onez_down, number(1, flip, down)),
        (cross_far, crossed(far)),
        (onez_far, number(1, flip, far)),
    ):
        result = pair(result, block, other)
    return result


def solution(mesh):
    fine_mesh = Mesh(mesh.devices.reshape(4, 4, 2, 4), ("chan", "x", "zh", "y"))
    blk = ("x", "zh", "y")
    in_specs = (
        P(blk + ("chan",), None, None, None),
        P(),
        P(blk + ("chan",), None),
        P(blk + ("chan",), None, None),
    )
    out_specs = P(None, "chan", blk, None)
    return jax.shard_map(
        shards, mesh=fine_mesh, in_specs=in_specs, out_specs=out_specs, check_vma=False
    )
```

time: 841 us -> 344 us (0.41); the launches traced: 830 us -> 344 us
  local copies, waits for them, and re-layouts: 268 us -> 4.58 us
  waiting for transfers between devices: 267 us -> 78.6 us
  blocking collectives: 0 us -> 185 us
  starting transfers between devices: 140 us -> 20.5 us
  other arithmetic: 98.8 us -> 3.24 us
  matrix products: 55.2 us -> 0 us
  Pallas kernels: 0 us -> 51.6 us
    ppermute x16, waiting for transfers between devices: 255 us -> 67.7 us  [the longest x12 67.7 us: moved(): lax.ppermute(value, axis, [(s, (s + steps) % count) for s in range(count)])]
    all_gather x0 -> x1, blocking collectives: none -> 185 us  [shards(): lax.all_gather(keep_list, ('x', 'zh', 'y', 'chan'), axis=0, tiled=True)]
    unnamed x26 -> x4, local copies, waits for them, and re-layouts: 126 us -> 0.95 us
    ppermute x16, starting transfers between devices: 133 us -> 17 us  [the longest x12 15.5 us: moved(): lax.ppermute(value, axis, [(s, (s + steps) % count) for s in range(count)])]
    slice x1 -> x0, local copies, waits for them, and re-layouts: 88.2 us -> none  [filter_bank(): filtered = frames[:, :, :, 0:spectra_len, :] * filter_taps[0]]
    dot_general x23 -> x0, matrix products: 55.2 us -> none  [the longest x17 48.3 us: products(): jnp.einsum('ifk,rjfk->rfij', own_block, paired, preferred_element_type=jn...]
    pallas_call x0 -> x18, Pallas kernels: none -> 51.6 us  [the longest x16 45.9 us: correlate_pair(): pl.pallas_call(kernel, grid_spec=pltpu.PrefetchScalarGridSpec(num_scalar_...]
    concatenate x18 -> x0, other arithmetic: 45.1 us -> none  [the longest x17 38 us: products(): jnp.concatenate([-halves[:, :, 1:2], halves[:, :, 0:1]], axis=2)]
  transfers between devices with their start and end apart: 18 -> 17, of which waited for: 17 -> 9; matrix products, arithmetic and copies ran while one was open for 29% -> 1% of each run, Pallas kernels for 0% -> 13%
where the time goes in v1:
time: 344 us
  blocking collectives  185 us (54%)
  waiting for transfers between devices  78.6 us (23%)
  Pallas kernels  51.6 us (15%)
  starting transfers between devices  20.5 us (6%)
  local copies, waits for them, and re-layouts  4.58 us (1%)
    all_gather x1, blocking collectives, shards(): lax.all_gather(keep_list, ('x', 'zh', 'y', 'chan'), axis=0, tiled=True)  185 us
    ppermute x12, waiting for transfers between devices, moved(): lax.ppermute(value, axis, [(s, (s + steps) % count) for s in range(count)])  67.7 us
    pallas_call x16, Pallas kernels, correlate_pair(): pl.pallas_call(kernel, grid_spec=pltpu.PrefetchScalarGridSpec(num_scalar_...  45.9 us
    ppermute x12, starting transfers between devices, moved(): lax.ppermute(value, axis, [(s, (s + steps) % count) for s in range(count)])  15.5 us
    all_to_all x1, waiting for transfers between devices, shards(): lax.all_to_all(outgoing, 'chan', split_axis=0, concat_axis=0, tiled=True)  10.9 us
  transfers between devices with their start and end apart: 17, of which 9 were waited for; matrix products, arithmetic and copies ran while one was open for 1% of the time, Pallas kernels for 13%

profile of v1, /device:TPU:0, one launch (start us, length us, event | category | flops | bytes accessed | tf_op | source)
XLA Modules:
  0.0 343.9 jit_solution(1276406815816222020)
XLA Ops:
  5.6 3.3 channelize.1
  9.0 3.5 %all-to-all-start = ((bf16[4,24,4096]{2,1,0:T(8,128)(2,1)}), bf16[4,24,4096]{2,1,0:T(8,128)(2,1)S(1)}, u32[]{:S(2)}, u32[]{:S(2)}) async-start(bf16[4,24,4096]{2,1,0:T(8,128)(2,1)} %channelize.1), calls=%async_computation | async-start | bytes 1572864 | tf_op jit(solution)/shard_map/all_to_all | solution.py:248
  13.2 10.9 %all-to-all-done = bf16[4,24,4096]{2,1,0:T(8,128)(2,1)S(1)} async-done(((bf16[4,24,4096]{2,1,0:T(8,128)(2,1)}), bf16[4,24,4096]{2,1,0:T(8,128)(2,1)S(1)}, u32[]{:S(2)}, u32[]{:S(2)}) %all-to-all-start) | async-done | bytes 786464 | tf_op jit(solution)/shard_map/all_to_all | solution.py:248
  27.5 16.1 %collective-permute-done.refs_3_ = bf16[96,4096]{1,0:T(8,128)(2,1)S(1)} collective-permute-done((bf16[96,4096]{1,0:T(8,128)(2,1)S(1)}, bf16[96,4096]{1,0:T(8,128)(2,1)S(1)}, u32[]{:S(2)}, u32[]{:S(2)}) %collective-permute-start) | collective-permute-done | bytes 786464 | tf_op jit(solution)/shard_map/ppermute | solution.py:227
  43.6 3.7 %collective-permute-start.6 = (bf16[96,4096]{1,0:T(8,128)(2,1)S(1)}, bf16[96,4096]{1,0:T(8,128)(2,1)S(1)}, u32[]{:S(2)}, u32[]{:S(2)}) collective-permute-start(bf16[96,4096]{1,0:T(8,128)(2,1)S(1)} %collective-permute-done.refs_3_), channel_id=1, source_target_pairs={{0,24},{8,0},{16,8},{24,16},{1,25},{9,1},{17,9},{25,17},{2,26},{10... | collective-permute-start | bytes 2359304 | tf_op jit(solution)/shard_map/ppermute | solution.py:227
  47.3 185.0 %all_gather.3 = s32[128,4,24]{2,1,0:T(4,128)S(1)} all-gather(s32[1,4,24]{2,1,0:T(4,128)S(1)} %copy-done.1), channel_id=1, replica_groups=mesh['chan'=4,'x'=4,'zh'=2,'y'=4] {'x','zh','y','chan'}, dimensions={0}, use_global_device_ids=true | all-gather | bytes 49536 | tf_op jit(solution)/shard_map/all_gather | solution.py:240
  237.4 2.9 pair_block.16.refs_4_
  242.6 13.2 %collective-permute-done.1.refs_3_ = bf16[96,4096]{1,0:T(8,128)(2,1)S(1)} collective-permute-done((bf16[96,4096]{1,0:T(8,128)(2,1)S(1)}, bf16[96,4096]{1,0:T(8,128)(2,1)S(1)}, u32[]{:S(2)}, u32[]{:S(2)}) %collective-permute-start.1) | collective-permute-done | bytes 786464 | tf_op jit(solution)/shard_map/ppermute | solution.py:227
  257.4 2.9 pair_block.17.refs_4_
  263.1 2.9 pair_block.19.refs_4_
  266.0 3.5 %collective-permute-start.2 = (bf16[96,4096]{1,0:T(8,128)(2,1)S(1)}, bf16[96,4096]{1,0:T(8,128)(2,1)S(1)}, u32[]{:S(2)}, u32[]{:S(2)}) collective-permute-start(bf16[96,4096]{1,0:T(8,128)(2,1)S(1)} %collective-permute-done.1.refs_3_), channel_id=1, source_target_pairs={{0,4},{4,0},{1,5},{5,1},{2,6},{6,2},{3,7},{7,3},{8,12},{12,8},{9,1... | collective-permute-start | bytes 2359304 | tf_op jit(solution)/shard_map/ppermute | solution.py:227
  274.0 3.7 %collective-permute-done.7.refs_3_ = bf16[96,4096]{1,0:T(8,128)(2,1)S(1)} collective-permute-done((bf16[96,4096]{1,0:T(8,128)(2,1)S(1)}, bf16[96,4096]{1,0:T(8,128)(2,1)S(1)}, u32[]{:S(2)}, u32[]{:S(2)}) %collective-permute-start.7) | collective-permute-done | bytes 786464 | tf_op jit(solution)/shard_map/ppermute | solution.py:227
  279.0 15.6 %collective-permute-done.2.refs_3_ = bf16[96,4096]{1,0:T(8,128)(2,1)S(1)} collective-permute-done((bf16[96,4096]{1,0:T(8,128)(2,1)S(1)}, bf16[96,4096]{1,0:T(8,128)(2,1)S(1)}, u32[]{:S(2)}, u32[]{:S(2)}) %collective-permute-start.2) | collective-permute-done | bytes 786464 | tf_op jit(solution)/shard_map/ppermute | solution.py:227
  294.6 14.8 %collective-permute-done.4.refs_3_ = bf16[96,4096]{1,0:T(8,128)(2,1)S(1)} collective-permute-done((bf16[96,4096]{1,0:T(8,128)(2,1)S(1)}, bf16[96,4096]{1,0:T(8,128)(2,1)S(1)}, u32[]{:S(2)}, u32[]{:S(2)}) %collective-permute-start.4) | collective-permute-done | bytes 786464 | tf_op jit(solution)/shard_map/ppermute | solution.py:227
  312.4 2.9 pair_block.21.refs_4_
  315.2 2.9 pair_block.22.refs_4_
  318.1 2.9 pair_block.23.refs_4_
  321.0 2.9 pair_block.24.refs_4_
  323.8 2.9 pair_block.25.refs_4_
  326.7 2.9 pair_block.26.refs_4_
  329.6 2.9 pair_block.27.refs_4_
  332.5 2.9 pair_block.28.refs_4_
  335.3 2.9 pair_block.29.refs_4_
  338.2 2.9 pair_block.30.refs_4_
  (74 shorter events, 32.9 us)
Async XLA Ops:
  0.0 47.3 %copy-start.1 = (s32[1,4,24]{2,1,0:T(4,128)S(1)}, s32[1,4,24]{2,1,0:T(4,128)}, u32[]{:S(2)}) copy-start(s32[1,4,24]{2,1,0:T(4,128)} %param.8) | copy-start | bytes 1156
  4.7 1.0 copy-start
  9.0 15.1 %all-to-all-start = ((bf16[4,24,4096]{2,1,0:T(8,128)(2,1)}), bf16[4,24,4096]{2,1,0:T(8,128)(2,1)S(1)}, u32[]{:S(2)}, u32[]{:S(2)}) async-start(bf16[4,24,4096]{2,1,0:T(8,128)(2,1)} %channelize.1), calls=%async_computation | async-start | bytes 1572864 | tf_op jit(solution)/shard_map/all_to_all | solution.py:248
  24.1 19.4 %collective-permute-start = (bf16[96,4096]{1,0:T(8,128)(2,1)S(1)}, bf16[96,4096]{1,0:T(8,128)(2,1)S(1)}, u32[]{:S(2)}, u32[]{:S(2)}) collective-permute-start(bf16[96,4096]{1,0:T(8,128)(2,1)S(1)} %bitcast.43), channel_id=1, source_target_pairs={{0,24},{8,0},{16,8},{24,16},{1,25},{9,1},{17,9},{25,17},{2,26},{10... | collective-permute-start | bytes 2359304 | tf_op jit(solution)/shard_map/ppermute | solution.py:227
  43.6 196.7 %collective-permute-start.6 = (bf16[96,4096]{1,0:T(8,128)(2,1)S(1)}, bf16[96,4096]{1,0:T(8,128)(2,1)S(1)}, u32[]{:S(2)}, u32[]{:S(2)}) collective-permute-start(bf16[96,4096]{1,0:T(8,128)(2,1)S(1)} %collective-permute-done.refs_3_), channel_id=1, source_target_pairs={{0,24},{8,0},{16,8},{24,16},{1,25},{9,1},{17,9},{25,17},{2,26},{10... | collective-permute-start | bytes 2359304 | tf_op jit(solution)/shard_map/ppermute | solution.py:227
  235.4 20.4 %collective-permute-start.1 = (bf16[96,4096]{1,0:T(8,128)(2,1)S(1)}, bf16[96,4096]{1,0:T(8,128)(2,1)S(1)}, u32[]{:S(2)}, u32[]{:S(2)}) collective-permute-start(bf16[96,4096]{1,0:T(8,128)(2,1)S(1)} %collective-permute-done.refs_3_), channel_id=1, source_target_pairs={{0,3},{1,0},{2,1},{3,2},{4,7},{5,4},{6,5},{7,6},{8,11},{9,8},{10,9... | collective-permute-start | bytes 2359304 | tf_op jit(solution)/shard_map/ppermute | solution.py:227
  235.4 21.6 %collective-permute-start.3 = (bf16[96,4096]{1,0:T(8,128)(2,1)S(1)}, bf16[96,4096]{1,0:T(8,128)(2,1)S(1)}, u32[]{:S(2)}, u32[]{:S(2)}) collective-permute-start(bf16[96,4096]{1,0:T(8,128)(2,1)S(1)} %collective-permute-done.refs_3_), channel_id=1, source_target_pairs={{0,1},{1,2},{2,3},{3,0},{4,5},{5,6},{6,7},{7,4},{8,9},{9,10},{10,1... | collective-permute-start | bytes 2359304 | tf_op jit(solution)/shard_map/ppermute | solution.py:227
  237.4 28.6 %collective-permute-start.15 = (bf16[96,4096]{1,0:T(8,128)(2,1)S(1)}, bf16[96,4096]{1,0:T(8,128)(2,1)S(1)}, u32[]{:S(2)}, u32[]{:S(2)}) collective-permute-start(bf16[96,4096]{1,0:T(8,128)(2,1)S(1)} %collective-permute-done.refs_3_), channel_id=1, source_target_pairs={{0,4},{4,0},{1,5},{5,1},{2,6},{6,2},{3,7},{7,3},{8,12},{12,8},{9,1... | collective-permute-start | bytes 2359304 | tf_op jit(solution)/shard_map/ppermute | solution.py:227
  240.5 31.9 %collective-permute-start.11 = (bf16[96,4096]{1,0:T(8,128)(2,1)S(1)}, bf16[96,4096]{1,0:T(8,128)(2,1)S(1)}, u32[]{:S(2)}, u32[]{:S(2)}) collective-permute-start(bf16[96,4096]{1,0:T(8,128)(2,1)S(1)} %get-tuple-element.10), channel_id=1, source_target_pairs={{0,3},{1,0},{2,1},{3,2},{4,7},{5,4},{6,5},{7,6},{8,11},{9,8},{10,9... | collective-permute-start | bytes 2359304 | tf_op jit(solution)/shard_map/ppermute | solution.py:227
  241.8 32.0 %collective-permute-start.12 = (bf16[96,4096]{1,0:T(8,128)(2,1)S(1)}, bf16[96,4096]{1,0:T(8,128)(2,1)S(1)}, u32[]{:S(2)}, u32[]{:S(2)}) collective-permute-start(bf16[96,4096]{1,0:T(8,128)(2,1)S(1)} %get-tuple-element.9), channel_id=1, source_target_pairs={{0,1},{1,2},{2,3},{3,0},{4,5},{5,6},{6,7},{7,4},{8,9},{9,10},{10,1... | collective-permute-start | bytes 2359304 | tf_op jit(solution)/shard_map/ppermute | solution.py:227
  255.7 22.0 %collective-permute-start.7 = (bf16[96,4096]{1,0:T(8,128)(2,1)S(1)}, bf16[96,4096]{1,0:T(8,128)(2,1)S(1)}, u32[]{:S(2)}, u32[]{:S(2)}) collective-permute-start(bf16[96,4096]{1,0:T(8,128)(2,1)S(1)} %get-tuple-element.11), channel_id=1, source_target_pairs={{0,4},{4,0},{1,5},{5,1},{2,6},{6,2},{3,7},{7,3},{8,12},{12,8},{9,1... | collective-permute-start | bytes 2359304 | tf_op jit(solution)/shard_map/ppermute | solution.py:227
  257.1 72.5 %collective-permute-start.14 = (bf16[96,4096]{1,0:T(8,128)(2,1)S(1)}, bf16[96,4096]{1,0:T(8,128)(2,1)S(1)}, u32[]{:S(2)}, u32[]{:S(2)}) collective-permute-start(bf16[96,4096]{1,0:T(8,128)(2,1)S(1)} %broadcast_select_fusion.3), channel_id=1, source_target_pairs={{0,3},{3,0},{1,2},{2,1},{4,7},{7,4},{5,6},{6,5},{8,11},{11,8},{9,1... | collective-permute-start | bytes 2359304 | tf_op jit(solution)/shard_map/ppermute | solution.py:273
  266.0 28.6 %collective-permute-start.2 = (bf16[96,4096]{1,0:T(8,128)(2,1)S(1)}, bf16[96,4096]{1,0:T(8,128)(2,1)S(1)}, u32[]{:S(2)}, u32[]{:S(2)}) collective-permute-start(bf16[96,4096]{1,0:T(8,128)(2,1)S(1)} %collective-permute-done.1.refs_3_), channel_id=1, source_target_pairs={{0,4},{4,0},{1,5},{5,1},{2,6},{6,2},{3,7},{7,3},{8,12},{12,8},{9,1... | collective-permute-start | bytes 2359304 | tf_op jit(solution)/shard_map/ppermute | solution.py:227
  272.4 37.0 %collective-permute-start.4 = (bf16[96,4096]{1,0:T(8,128)(2,1)S(1)}, bf16[96,4096]{1,0:T(8,128)(2,1)S(1)}, u32[]{:S(2)}, u32[]{:S(2)}) collective-permute-start(bf16[96,4096]{1,0:T(8,128)(2,1)S(1)} %collective-permute-done.3.refs_3_), channel_id=1, source_target_pairs={{0,4},{4,0},{1,5},{5,1},{2,6},{6,2},{3,7},{7,3},{8,12},{12,8},{9,1... | collective-permute-start | bytes 2359304 | tf_op jit(solution)/shard_map/ppermute | solution.py:227
  273.9 58.6 %collective-permute-start.13 = (bf16[96,4096]{1,0:T(8,128)(2,1)S(1)}, bf16[96,4096]{1,0:T(8,128)(2,1)S(1)}, u32[]{:S(2)}, u32[]{:S(2)}) collective-permute-start(bf16[96,4096]{1,0:T(8,128)(2,1)S(1)} %broadcast_select_fusion.4), channel_id=1, source_target_pairs={{0,1},{1,0},{2,3},{3,2},{4,5},{5,4},{6,7},{7,6},{8,9},{9,8},{10,11... | collective-permute-start | bytes 2359304 | tf_op jit(solution)/shard_map/ppermute | solution.py:270
  277.7 31.8 %collective-permute-start.9 = (bf16[96,4096]{1,0:T(8,128)(2,1)S(1)}, bf16[96,4096]{1,0:T(8,128)(2,1)S(1)}, u32[]{:S(2)}, u32[]{:S(2)}) collective-permute-start(bf16[96,4096]{1,0:T(8,128)(2,1)S(1)} %collective-permute-done.7.refs_3_), channel_id=1, source_target_pairs={{0,3},{1,0},{2,1},{3,2},{4,7},{5,4},{6,5},{7,6},{8,11},{9,8},{10,9... | collective-permute-start | bytes 2359304 | tf_op jit(solution)/shard_map/ppermute | solution.py:227
  294.6 16.7 %collective-permute-start.8 = (bf16[96,4096]{1,0:T(8,128)(2,1)S(1)}, bf16[96,4096]{1,0:T(8,128)(2,1)S(1)}, u32[]{:S(2)}, u32[]{:S(2)}) collective-permute-start(bf16[96,4096]{1,0:T(8,128)(2,1)S(1)} %collective-permute-done.7.refs_3_), channel_id=1, source_target_pairs={{0,1},{1,2},{2,3},{3,0},{4,5},{5,6},{6,7},{7,4},{8,9},{9,10},{10,1... | collective-permute-start | bytes 2359304 | tf_op jit(solution)/shard_map/ppermute | solution.py:227
  309.5 31.6 %collective-permute-start.5 = (bf16[96,4096]{1,0:T(8,128)(2,1)S(1)}, bf16[96,4096]{1,0:T(8,128)(2,1)S(1)}, u32[]{:S(2)}, u32[]{:S(2)}) collective-permute-start(bf16[96,4096]{1,0:T(8,128)(2,1)S(1)} %broadcast_select_fusion.6), channel_id=1, source_target_pairs={{0,1},{1,0},{2,3},{3,2},{4,5},{5,4},{6,7},{7,6},{8,9},{9,8},{10,11... | collective-permute-start | bytes 2359304 | tf_op jit(solution)/shard_map/ppermute | solution.py:270
  311.3 26.9 %collective-permute-start.10 = (bf16[96,4096]{1,0:T(8,128)(2,1)S(1)}, bf16[96,4096]{1,0:T(8,128)(2,1)S(1)}, u32[]{:S(2)}, u32[]{:S(2)}) collective-permute-start(bf16[96,4096]{1,0:T(8,128)(2,1)S(1)} %broadcast_select_fusion.5), channel_id=1, source_target_pairs={{0,3},{3,0},{1,2},{2,1},{4,7},{7,4},{5,6},{6,5},{8,11},{11,8},{9,1... | collective-permute-start | bytes 2359304 | tf_op jit(solution)/shard_map/ppermute | solution.py:273

commit v2 on v1

v2 whole, which is shorter than its diff:
```python
import math

import jax
import jax.numpy as jnp
import numpy as np
from jax import lax
from jax.experimental import pallas as pl
from jax.experimental.pallas import tpu as pltpu
from jax.sharding import Mesh
from jax.sharding import PartitionSpec as P

TAPS = 16
FFT = 16
STEP = 8
LANES = 128
CHUNKS = LANES // STEP
UNUSED = 512


def trig_table():
    table = np.zeros((2, 2, LANES, 8, 2, STEP), np.float64)
    point = np.arange(LANES) % FFT
    for half in range(2):
        for fine in range(8):
            angle = 2.0 * math.pi * ((8 * half + fine) * point % FFT) / FFT
            cosine, sine = np.cos(angle)[:, None], np.sin(angle)[:, None]
            table[half, 0, :, fine, 0] = cosine
            table[half, 0, :, fine, 1] = -sine
            table[half, 1, :, fine, 0] = sine
            table[half, 1, :, fine, 1] = cosine
    return table.reshape(2, 2 * LANES, LANES).astype(np.float32)


def channelize_kernel(spectra_len, cap, volt, lists, counts, taps, trig, out, square, frames, weights):
    samples = volt.shape[1]
    in_count = counts.shape[1]
    tiles = -(-samples // LANES)
    listed = 2 * cap
    point_row = lax.broadcasted_iota(jnp.int32, (LANES, LANES), 0) // FFT
    spec_lane = lax.broadcasted_iota(jnp.int32, (LANES, LANES), 1) % STEP
    lag = point_row - spec_lane
    by_row = jnp.concatenate([taps[...]] * (LANES // FFT), axis=1).T
    column = [jnp.broadcast_to(by_row[:, m : m + 1], (LANES, LANES)) for m in range(TAPS)]
    for part in range(3):
        shaped = jnp.zeros((LANES, LANES), jnp.float32)
        for m in range(TAPS):
            shaped = jnp.where(lag == m - STEP * part, column[m], shaped)
        both = jnp.concatenate([shaped, shaped], axis=0)
        for half in range(2):
            exact = both * trig[half]
            high = exact.astype(jnp.bfloat16)
            low = (exact - high.astype(jnp.float32)).astype(jnp.bfloat16)
            weights[half, part, :, 0:LANES] = high
            weights[half, part, :, LANES : 2 * LANES] = low
    square[...] = jnp.zeros(square.shape, square.dtype)
    square[0:4, 0:cap] = lists[0].astype(jnp.float32)
    by_slot = square[...].T
    entry = [by_slot[0:cap, g : g + 1].astype(jnp.int32) for g in range(4)]
    gains = jnp.sqrt(samples / (FFT * counts[...].astype(jnp.float32)))
    inputs = lax.broadcasted_iota(jnp.int32, (cap, in_count), 1)
    lanes = lax.broadcasted_iota(jnp.int32, (cap, LANES), 1)
    picks = []
    for half in range(2):
        for part in range(2):
            for coarse in range(2):
                row = entry[2 * coarse + half] * 4 + (2 * coarse + part)
                picks.append((row == lanes).astype(jnp.float32))
    pick = jnp.concatenate(picks, axis=0).astype(jnp.bfloat16)
    for tile in range(tiles):
        width = min(LANES, samples - tile * LANES)
        piece = volt[:, tile * LANES : tile * LANES + width]
        if width < LANES:
            piece = jnp.concatenate([piece, jnp.zeros((LANES, LANES - width), piece.dtype)], axis=1)
        got = jnp.dot(pick, piece, preferred_element_type=jnp.float32).astype(jnp.bfloat16)
        for half in range(2):
            base = 2 * half * listed
            here = slice(tile * listed, (tile + 1) * listed)
            frames[half, here, 0:LANES] = got[base : base + listed]
            frames[half, here, LANES : 2 * LANES] = got[base + listed : base + 2 * listed]
    chunk = lax.broadcasted_iota(jnp.int32, (listed, LANES), 1) // STEP
    for half in range(2):
        factors = []
        for coarse in range(2):
            spot = entry[2 * coarse + half]
            chosen = jnp.where(spot == inputs, gains[coarse : coarse + 1, :], 0.0)
            factors.append(jnp.sum(chosen, axis=1, keepdims=True))
            told = jnp.where(spot < in_count, spot, UNUSED).astype(jnp.float32)
            told = jnp.broadcast_to(told, (cap, LANES)).astype(jnp.bfloat16)
            out[2 * coarse + half, :, 16 * spectra_len : 16 * spectra_len + LANES] = told
        gain = jnp.concatenate(factors, axis=0)
        for quarter in range(spectra_len // LANES):
            total = None
            for part in range(3):
                first = (quarter * CHUNKS + part) * listed
                term = jnp.dot(
                    frames[half, first : first + CHUNKS * listed, :],
                    weights[half, part],
                    preferred_element_type=jnp.float32,
                )
                total = term if total is None else total + term
            summed = total[:, 0:LANES] + total[:, LANES : 2 * LANES]
            lines = [summed[n * listed : (n + 1) * listed] * gain for n in range(CHUNKS)]
            bit = 1
            while bit < CHUNKS:
                keep = (chunk & bit) == 0
                fresh = list(lines)
                for n in range(CHUNKS):
                    if n & bit == 0:
                        one, two = lines[n], lines[n | bit]
                        fresh[n] = jnp.where(keep, one, pltpu.roll(two, bit * STEP, 1))
                        fresh[n | bit] = jnp.where(keep, pltpu.roll(one, LANES - bit * STEP, 1), two)
                lines = fresh
                bit *= 2
            for n in range(CHUNKS):
                lane = n * spectra_len + quarter * LANES
                value = lines[n].astype(jnp.bfloat16)
                out[half, :, lane : lane + LANES] = value[0:cap]
                out[half + 2, :, lane : lane + LANES] = value[cap : 2 * cap]


def channelize(voltages, filter_taps, sample_counts, keep_list, spectra_len):
    in_count, coarse, _, samples = voltages.shape
    groups, cap = keep_list.shape[1:]
    volt = voltages.reshape(in_count * coarse * 2, samples)
    row_width = 8 * 2 * spectra_len + LANES
    tiles = -(-samples // LANES)

    def kernel(*refs):
        channelize_kernel(spectra_len, cap, *refs)

    return pl.pallas_call(
        kernel,
        out_shape=jax.ShapeDtypeStruct((groups, cap, row_width), jnp.bfloat16),
        scratch_shapes=[
            pltpu.VMEM((LANES, LANES), jnp.float32),
            pltpu.VMEM((2, tiles * 2 * cap, 2 * LANES), jnp.bfloat16),
            pltpu.VMEM((2, 3, 2 * LANES, 2 * LANES), jnp.bfloat16),
        ],
        compiler_params=pltpu.CompilerParams(vmem_limit_bytes=32 * 1024 * 1024),
        cost_estimate=pl.CostEstimate(flops=4 * 10**9, bytes_accessed=3 * 10**6, transcendentals=0),
        name="channelize",
    )(volt, keep_list, sample_counts.T, filter_taps, trig_table())


def row_places(block, in_count, cap, width):
    listed = block.shape[0]
    told = block[:, width : width + 1].astype(jnp.float32).astype(jnp.int32)
    place = told + lax.broadcasted_iota(jnp.int32, (listed, 1), 0) // cap * in_count
    one_hot = lax.broadcasted_iota(jnp.int32, (listed, LANES), 1) == place
    return one_hot.astype(jnp.float32).T.astype(jnp.bfloat16)


def with_turned(value):
    half = value.shape[1] // 2
    turned = jnp.concatenate([value[:, half:], -value[:, :half]], axis=1)
    return jnp.concatenate([value, turned], axis=0)


def group_kernel(fine, cap, in_count, norm, picked, first, *refs):
    refs = list(refs)
    spots = refs.pop(0)
    side = None if first else refs.pop(0)
    arrays = [[refs.pop(0) for _ in range(2 if two else 1)] for two in picked]
    if not first:
        refs.pop(0)
    out = refs.pop(0)
    if first:
        side_out = refs.pop(0)
    else:
        token = refs.pop(0)
    buf, sems = refs
    count = len(picked)
    width = (arrays[0][0].shape[1] - LANES) // fine
    both_numbers = (((1,), (1,)), ((), ()))

    def rows(n, lanes):
        if picked[n]:
            return jnp.where(spots[count + n] == 1, arrays[n][0][:, lanes], arrays[n][1][:, lanes])
        return arrays[n][0][:, lanes]

    copies = []
    every = [row_places(rows(n, slice(fine * width, fine * width + LANES)), in_count, cap, 0) for n in range(count)]
    for f in range(fine):
        lanes = slice(f * width, (f + 1) * width)
        full = [
            jnp.dot(every[n], rows(n, lanes), preferred_element_type=jnp.float32).astype(jnp.bfloat16)
            for n in range(count)
        ]
        if first:
            own = (full[0].astype(jnp.float32) * norm).astype(jnp.bfloat16)
            side_out[:, lanes] = own
        else:
            own = side[:, lanes]
        stacked = jnp.concatenate(full, axis=0) if count > 1 else full[0]
        got = lax.dot_general(with_turned(own), stacked, both_numbers, preferred_element_type=jnp.float32)
        for n in range(count):
            buf[n, 0, f] = got[0:LANES, n * LANES : (n + 1) * LANES]
            buf[n, 1, f] = got[LANES : 2 * LANES, n * LANES : (n + 1) * LANES]
            column = pl.ds(pl.multiple_of(spots[n] * LANES, LANES), LANES)
            copy = pltpu.make_async_copy(buf.at[n, :, f], out.at[:, f, :, column], sems.at[n, f])
            copy.start()
            copies.append(copy)
    if not first:
        token[...] = jnp.zeros(token.shape, token.dtype)
    for copy in copies:
        copy.wait()


def correlate(result, side, blocks, offsets, sizes):
    fine, cap, in_count, columns, norm = sizes
    first = side is None
    picked = [isinstance(block, tuple) for block in blocks]
    flags = [block[0].astype(jnp.int32) if two else jnp.int32(0) for block, two in zip(blocks, picked)]
    arrays = [a for block, two in zip(blocks, picked) for a in (block[1:] if two else (block,))]
    spots = jnp.stack([jnp.int32(o) for o in offsets] + flags)
    count = len(blocks)
    width = arrays[0].shape[1] - LANES
    vmem = pl.BlockSpec(memory_space=pltpu.VMEM)
    anywhere = pl.BlockSpec(memory_space=pl.ANY)

    def kernel(*refs):
        group_kernel(fine, cap, in_count, norm, picked, first, *refs)

    whole = jax.ShapeDtypeStruct((2, fine, LANES, columns), jnp.float32)
    extra = jax.ShapeDtypeStruct((LANES, width), jnp.bfloat16) if first else jax.ShapeDtypeStruct((8, LANES), jnp.float32)
    operands = [spots] + ([] if first else [side]) + arrays + ([] if first else [result])
    return pl.pallas_call(
        kernel,
        in_specs=[pl.BlockSpec(memory_space=pltpu.SMEM)]
        + [vmem] * (len(arrays) + (0 if first else 1))
        + ([] if first else [anywhere]),
        out_specs=[anywhere, vmem],
        out_shape=[whole, extra],
        scratch_shapes=[
            pltpu.VMEM((count, 2, fine, LANES, LANES), jnp.float32),
            pltpu.SemaphoreType.DMA((count, fine)),
        ],
        input_output_aliases={} if first else {len(operands) - 1: 0},
        compiler_params=pltpu.CompilerParams(vmem_limit_bytes=24 * 1024 * 1024),
        cost_estimate=pl.CostEstimate(flops=10**8 * count, bytes_accessed=10**5 * count, transcendentals=0),
        name="own_block" if first else "pair_blocks",
    )(*operands)


def moved(value, axis, steps):
    count = lax.axis_size(axis)
    return lax.ppermute(value, axis, [(s, (s + steps) % count) for s in range(count)])


def down_x(value, rows):
    xs, ys = lax.axis_size("x"), lax.axis_size("y")
    pairs = [(x * ys + y, (x - 1) % xs * ys + y) for x in range(xs) for y in rows]
    return lax.ppermute(value, ("x", "y"), pairs)


def after(value, token):
    return lax.optimization_barrier((value, token))[0]


def shards(voltages, filter_taps, sample_counts, keep_list):
    spectra_len = voltages.shape[3] // FFT - TAPS + 1
    x_count, z_count, y_count = (lax.axis_size(a) for a in ("x", "zh", "y"))
    blocks = x_count * z_count * y_count
    x, z, y = (lax.axis_index(a) for a in ("x", "zh", "y"))
    cap = keep_list.shape[2]

    outgoing = channelize(voltages, filter_taps, sample_counts, keep_list, spectra_len)
    incoming = lax.all_to_all(outgoing, "chan", split_axis=0, concat_axis=0, tiled=True)
    own = incoming.reshape(-1, outgoing.shape[2])
    columns = (blocks // 2 + 1) * LANES
    sizes = (8, cap, voltages.shape[0], columns, 1.0 / math.sqrt(spectra_len))

    def offset(dx, zz, yy):
        other = ((x + dx) % x_count * z_count + zz) * y_count + yy
        return (other - (x * z_count + z) * y_count - y) % blocks

    up, down, far = (y + 1) % y_count, (y + 3) % y_count, (y + 2) % y_count
    flip = 1 - z

    def near(yy):
        return offset(jnp.where(yy > y, 0, 2), z, yy)

    def crossed(yy):
        return offset(jnp.where(z == 0, 0, 2), flip, yy)

    one = moved(own, "x", -1)
    own_up = moved(own, "y", -1)
    own_down = moved(own, "y", 1)
    result, side = correlate(None, None, [own], [jnp.int32(0)], sizes)
    one_up = moved(one, "y", -1)
    one_down = moved(one, "y", 1)
    two = moved(one, "x", -1)
    one_z = moved(one, "zh", 1)
    result, token = correlate(result, side, [one], [offset(1, z, y)], sizes)
    cross = moved(after(jnp.where(z == 1, own, two), token), "zh", 1)
    one_far = moved(after(one_up, token), "y", -1)
    onez_down = moved(after(one_z, token), "y", 1)
    two_down = down_x(after(one_down, token), (1, 2, 3))
    result, token = correlate(
        result,
        side,
        [two, one_up, one_down, one_z],
        [offset(2, z, y), offset(1, z, up), offset(1, z, down), offset(1, flip, y)],
        sizes,
    )
    cross_up = moved(after(cross, token), "y", -1)
    cross_down = moved(after(cross, token), "y", 1)
    onez_up = moved(after(one_up, token), "zh", 1)
    two_up = down_x(after(one_up, token), (3,))
    two_far = down_x(after(one_far, token), (2, 3))
    result, token = correlate(
        result,
        side,
        [one_far, onez_down, cross, (y == 0, own_down, two_down)],
        [offset(1, z, far), offset(1, flip, down), crossed(y), near(down)],
        sizes,
    )
    cross_far = moved(after(cross_up, token), "y", -1)
    own_far = lax.ppermute(after(own_down, token), "y", [(3, 0), (0, 1)])
    onez_far = moved(after(one_far, token), "zh", 1)
    result, token = correlate(
        result,
        side,
        [cross_up, cross_down, onez_up, (y == y_count - 1, two_up, own_up)],
        [crossed(up), crossed(down), offset(1, flip, up), near(up)],
        sizes,
    )
    result, token = correlate(
        result,
        side,
        [cross_far, onez_far, (y < 2, own_far, two_far)],
        [crossed(far), offset(1, flip, far), near(far)],
        sizes,
    )
    return result


def solution(mesh):
    fine_mesh = Mesh(mesh.devices.reshape(4, 4, 2, 4), ("chan", "x", "zh", "y"))
    blk = ("x", "zh", "y")
    in_specs = (
        P(blk + ("chan",), None, None, None),
        P(),
        P(blk + ("chan",), None),
        P(blk + ("chan",), None, None),
    )
    out_specs = P(None, "chan", blk, None)
    return jax.shard_map(
        shards, mesh=fine_mesh, in_specs=in_specs, out_specs=out_specs, check_vma=False
    )
```

time: 344 us -> 161 us (0.47)
  blocking collectives: 185 us -> 15 us
  waiting for transfers between devices: 78.6 us -> 54.8 us
  starting transfers between devices: 20.5 us -> 38.8 us
  Pallas kernels: 51.6 us -> 44.4 us
    all_gather x1 -> x0, blocking collectives: 185 us -> none  [shards(): lax.all_gather(keep_list, ('x', 'zh', 'y', 'chan'), axis=0, tiled=True)]
    ppermute x12 -> x15, starting transfers between devices: 15.5 us -> 32.5 us  [moved(): lax.ppermute(value, axis, [(s, (s + steps) % count) for s in range(count)])]
    ppermute x12 -> x15, waiting for transfers between devices: 67.7 us -> 51.4 us  [moved(): lax.ppermute(value, axis, [(s, (s + steps) % count) for s in range(count)])]
    all_to_all x0 -> x1, blocking collectives: none -> 15 us  [shards(): lax.all_to_all(outgoing, 'chan', split_axis=0, concat_axis=0, tiled=True)]
    all_to_all x1 -> x0, waiting for transfers between devices: 10.9 us -> none  [shards(): lax.all_to_all(outgoing, 'chan', split_axis=0, concat_axis=0, tiled=True)]
    pallas_call x17 -> x6, Pallas kernels: 48.2 us -> 41.6 us  [correlate(): pl.pallas_call(kernel, in_specs=[pl.BlockSpec(memory_space=pltpu.SMEM)] +...]
    ppermute x4, starting transfers between devices: 1.53 us -> 6.25 us  [the longest x3 3.83 us: down_x(): return lax.ppermute(value, ('x', 'y'), pairs)]
    all_to_all x1 -> x0, starting transfers between devices: 3.49 us -> none  [shards(): lax.all_to_all(outgoing, 'chan', split_axis=0, concat_axis=0, tiled=True)]
  transfers between devices with their start and end apart: 17 -> 19, of which waited for: 9 -> 8; matrix products, arithmetic and copies ran while one was open for 1% -> 1% of each run, Pallas kernels for 13% -> 22%
where the time goes in v2:
time: 161 us; the launch traced here: 160 us
  waiting for transfers between devices  54.8 us (34%)
  Pallas kernels  44.4 us (28%)
  starting transfers between devices  38.8 us (24%)
  blocking collectives  15 us (9%)
  local copies, waits for them, and re-layouts  5.22 us (3%)
    ppermute x15, waiting for transfers between devices, moved(): lax.ppermute(value, axis, [(s, (s + steps) % count) for s in range(count)])  51.4 us
    pallas_call x6, Pallas kernels, correlate(): pl.pallas_call(kernel, in_specs=[pl.BlockSpec(memory_space=pltpu.SMEM)] +...  41.6 us
    ppermute x15, starting transfers between devices, moved(): lax.ppermute(value, axis, [(s, (s + steps) % count) for s in range(count)])  32.5 us
    all_to_all x1, blocking collectives, shards(): lax.all_to_all(outgoing, 'chan', split_axis=0, concat_axis=0, tiled=True)  15 us
    ppermute x3, starting transfers between devices, down_x(): return lax.ppermute(value, ('x', 'y'), pairs)  3.83 us
    ppermute x1, waiting for transfers between devices, shards(): own_far = lax.ppermute(after(own_down, token), 'y', [(3, 0), (0, 1)])  3.36 us
  transfers between devices with their start and end apart: 19, of which 8 were waited for; matrix products, arithmetic and copies ran while one was open for 1% of the time, Pallas kernels for 22%

profile of v2, /device:TPU:0, one launch (start us, length us, event | category | flops | bytes accessed | tf_op | source)
XLA Modules:
  0.0 159.6 jit_solution(8409199419978046270)
XLA Ops:
  4.9 2.8 %channelize.1 = bf16[4,24,4224]{2,1,0:T(8,128)(2,1)S(1)} custom-call(bf16[128,4336]{1,0:T(8,128)(2,1)S(1)} %reshape.6.refs_0_, s32[1,4,24]{2,1,0:T(4,128)S(1)} %copy-done.1, s32[2,32]{1,0:T(2,128)S(1)} %bitcast.26, f32[16,16]{1,0:T(8,128)S(1)} %copy-done, f32[2,256,128]{2,1,0:T(8,128)S(1)} %copy-done.3), custom_call_target="tpu_custom_call" | custom-call | flops 4000000000 | bytes 3000000 | tf_op jit(solution)/shard_map/channelize/pallas_call | solution.py:131
  7.7 15.0 %all_to_all.5 = bf16[4,24,4224]{2,1,0:T(8,128)(2,1)S(1)} all-to-all(bf16[4,24,4224]{2,1,0:T(8,128)(2,1)S(1)} %channelize.1), channel_id=1, replica_groups=mesh['chan'=4,'x'=4,'zh'=2,'y'=4] {'chan'}, dimensions={0} | all-to-all | bytes 1622016 | tf_op jit(solution)/shard_map/all_to_all | solution.py:268
  22.6 2.8 %collective-permute-start = (bf16[96,4224]{1,0:T(8,128)(2,1)S(1)}, bf16[96,4224]{1,0:T(8,128)(2,1)}, u32[]{:S(2)}, u32[]{:S(2)}) collective-permute-start(bf16[96,4224]{1,0:T(8,128)(2,1)S(1)} %bitcast.22), channel_id=1, source_target_pairs={{0,24},{8,0},{16,8},{24,16},{1,25},{9,1},{17,9},{25,17},{2,26},{10... | collective-permute-start | bytes 2433032 | tf_op jit(solution)/shard_map/ppermute | solution.py:247
  25.4 17.5 %collective-permute-done.refs_2_ = bf16[96,4224]{1,0:T(8,128)(2,1)} collective-permute-done((bf16[96,4224]{1,0:T(8,128)(2,1)S(1)}, bf16[96,4224]{1,0:T(8,128)(2,1)}, u32[]{:S(2)}, u32[]{:S(2)}) %collective-permute-start) | collective-permute-done | bytes 811040 | tf_op jit(solution)/shard_map/ppermute | solution.py:247
  42.9 3.8 %collective-permute-start.1 = (bf16[96,4224]{1,0:T(8,128)(2,1)}, bf16[96,4224]{1,0:T(8,128)(2,1)S(1)}, u32[]{:S(2)}, u32[]{:S(2)}) collective-permute-start(bf16[96,4224]{1,0:T(8,128)(2,1)} %collective-permute-done.refs_2_), channel_id=1, source_target_pairs={{0,24},{8,0},{16,8},{24,16},{1,25},{9,1},{17,9},{25,17},{2,26},{10... | collective-permute-start | bytes 2433032 | tf_op jit(solution)/shard_map/ppermute | solution.py:247
  46.8 4.7 %own_block.1 = (f32[2,8,128,2176]{3,2,1,0:T(8,128)}, bf16[128,4096]{1,0:T(8,128)(2,1)S(1)}) custom-call(s32[2]{0:T(128)S(1)} %broadcast_3_refs_0_.2.refs_0_, bf16[96,4224]{1,0:T(8,128)(2,1)S(1)} %bitcast.23), custom_call_target="tpu_custom_call" | custom-call | flops 100000000 | bytes 100000 | tf_op jit(solution)/shard_map/own_block/pallas_call | solution.py:227
  51.5 3.1 %collective-permute-start.3 = (bf16[96,4224]{1,0:T(8,128)(2,1)}, bf16[96,4224]{1,0:T(8,128)(2,1)S(1)}, u32[]{:S(2)}, u32[]{:S(2)}) collective-permute-start(bf16[96,4224]{1,0:T(8,128)(2,1)} %collective-permute-done.refs_2_), channel_id=1, source_target_pairs={{0,3},{1,0},{2,1},{3,2},{4,7},{5,4},{6,5},{7,6},{8,11},{9,8},{10,9... | collective-permute-start | bytes 2433032 | tf_op jit(solution)/shard_map/ppermute | solution.py:247
  54.6 3.6 %collective-permute-start.5 = (bf16[96,4224]{1,0:T(8,128)(2,1)}, bf16[96,4224]{1,0:T(8,128)(2,1)}, u32[]{:S(2)}, u32[]{:S(2)}) collective-permute-start(bf16[96,4224]{1,0:T(8,128)(2,1)} %collective-permute-done.refs_2_), channel_id=1, source_target_pairs={{0,4},{4,0},{1,5},{5,1},{2,6},{6,2},{3,7},{7,3},{8,12},{12,8},{9,1... | collective-permute-start | bytes 2433032 | tf_op jit(solution)/shard_map/ppermute | solution.py:247
  58.1 5.9 %pair_blocks.5 = (f32[2,8,128,2176]{3,2,1,0:T(8,128)}, f32[8,128]{1,0:T(8,128)}) custom-call(s32[2]{0:T(128)S(1)} %pad_add_fusion.refs_0_, bf16[128,4096]{1,0:T(8,128)(2,1)S(1)} %get-tuple-element.25.refs_1_, bf16[96,4224]{1,0:T(8,128)(2,1)} %collective-permute-done.refs_2_, ...), custom_call_target="tpu_custom_call", output_to_operand_aliasing={{0}: (3, {})} | custom-call | flops 100000000 | bytes 100000 | tf_op jit(solution)/shard_map/pair_blocks/pallas_call | solution.py:227
  65.2 3.1 %collective-permute-start.2 = (bf16[96,4224]{1,0:T(8,128)(2,1)}, bf16[96,4224]{1,0:T(8,128)(2,1)}, u32[]{:S(2)}, u32[]{:S(2)}) collective-permute-start(bf16[96,4224]{1,0:T(8,128)(2,1)} %broadcast_select_fusion), channel_id=1, source_target_pairs={{0,4},{4,0},{1,5},{5,1},{2,6},{6,2},{3,7},{7,3},{8,12},{12,8},{9,1... | collective-permute-start | bytes 2433032 | tf_op jit(solution)/shard_map/ppermute | solution.py:247
  69.8 7.2 %collective-permute-done.4.refs_4_ = bf16[96,4224]{1,0:T(8,128)(2,1)} collective-permute-done((bf16[96,4224]{1,0:T(8,128)(2,1)}, bf16[96,4224]{1,0:T(8,128)(2,1)}, u32[]{:S(2)}, u32[]{:S(2)}) %collective-permute-start.4) | collective-permute-done | bytes 811040 | tf_op jit(solution)/shard_map/ppermute | solution.py:247
  80.7 7.6 %pair_blocks.6 = (f32[2,8,128,2176]{3,2,1,0:T(8,128)}, f32[8,128]{1,0:T(8,128)}) custom-call(s32[8]{0:T(128)S(1)} %stack.93.refs_0_, bf16[128,4096]{1,0:T(8,128)(2,1)S(1)} %get-tuple-element.25.refs_1_, bf16[96,4224]{1,0:T(8,128)(2,1)S(1)} %collective-permute-done.1.refs_2_, ...), custom_call_target="tpu_custom_call", output_to_operand_aliasing={{0}: (6, {})} | custom-call | flops 400000000 | bytes 400000 | tf_op jit(solution)/shard_map/pair_blocks/pallas_call | solution.py:227
  88.3 4.4 %collective-permute-done.2.refs_4_ = bf16[96,4224]{1,0:T(8,128)(2,1)} collective-permute-done((bf16[96,4224]{1,0:T(8,128)(2,1)}, bf16[96,4224]{1,0:T(8,128)(2,1)}, u32[]{:S(2)}, u32[]{:S(2)}) %collective-permute-start.2) | collective-permute-done | bytes 811040 | tf_op jit(solution)/shard_map/ppermute | solution.py:247
  92.7 2.9 %collective-permute-start.6 = (bf16[96,4224]{1,0:T(8,128)(2,1)}, bf16[96,4224]{1,0:T(8,128)(2,1)}, u32[]{:S(2)}, u32[]{:S(2)}) collective-permute-start(bf16[96,4224]{1,0:T(8,128)(2,1)} %collective-permute-done.2.refs_4_), channel_id=1, source_target_pairs={{0,3},{1,0},{2,1},{3,2},{4,7},{5,4},{6,5},{7,6},{8,11},{9,8},{10,9... | collective-permute-start | bytes 2433032 | tf_op jit(solution)/shard_map/ppermute | solution.py:247
  95.7 3.3 %collective-permute-start.16 = (bf16[96,4224]{1,0:T(8,128)(2,1)S(1)}, bf16[96,4224]{1,0:T(8,128)(2,1)}, u32[]{:S(2)}, u32[]{:S(2)}) collective-permute-start(bf16[96,4224]{1,0:T(8,128)(2,1)S(1)} %collective-permute-done.3.refs_3_), channel_id=1, source_target_pairs={{0,4},{4,0},{1,5},{5,1},{2,6},{6,2},{3,7},{7,3},{8,12},{12,8},{9,1... | collective-permute-start | bytes 2433032 | tf_op jit(solution)/shard_map/ppermute | solution.py:247
  100.6 8.8 %collective-permute-done.8.refs_3_ = bf16[96,4224]{1,0:T(8,128)(2,1)} collective-permute-done((bf16[96,4224]{1,0:T(8,128)(2,1)}, bf16[96,4224]{1,0:T(8,128)(2,1)}, u32[]{:S(2)}, u32[]{:S(2)}) %collective-permute-start.8) | collective-permute-done | bytes 811040 | tf_op jit(solution)/shard_map/ppermute | solution.py:247
  109.4 8.3 %pair_blocks.7 = (f32[2,8,128,2176]{3,2,1,0:T(8,128)}, f32[8,128]{1,0:T(8,128)}) custom-call(s32[8]{0:T(128)S(1)} %stack.100.refs_0_, bf16[128,4096]{1,0:T(8,128)(2,1)S(1)} %get-tuple-element.25.refs_1_, bf16[96,4224]{1,0:T(8,128)(2,1)} %collective-permute-done.7.refs_2_, ...), custom_call_target="tpu_custom_call", output_to_operand_aliasing={{0}: (7, {})} | custom-call | flops 400000000 | bytes 400000 | tf_op jit(solution)/shard_map/pair_blocks/pallas_call | solution.py:227
  118.4 10.3 %collective-permute-done.18.refs_6_ = bf16[96,4224]{1,0:T(8,128)(2,1)} collective-permute-done((bf16[96,4224]{1,0:T(8,128)(2,1)S(1)}, bf16[96,4224]{1,0:T(8,128)(2,1)}, u32[]{:S(2)}, u32[]{:S(2)}) %collective-permute-start.18) | collective-permute-done | bytes 811040 | tf_op jit(solution)/shard_map/ppermute | solution.py:247
  128.7 2.4 %collective-permute-start.13 = (bf16[96,4224]{1,0:T(8,128)(2,1)}, bf16[96,4224]{1,0:T(8,128)(2,1)S(1)}, u32[]{:S(2)}, u32[]{:S(2)}) collective-permute-start(bf16[96,4224]{1,0:T(8,128)(2,1)} %collective-permute-done.9.refs_5_), channel_id=1, source_target_pairs={{3,0},{0,1},{7,4},{4,5},{11,8},{8,9},{15,12},{12,13},{19,16},{16,1... | collective-permute-start | bytes 2433032 | tf_op jit(solution)/shard_map/ppermute | solution.py:319
  131.1 3.2 %collective-permute-start.12 = (bf16[96,4224]{1,0:T(8,128)(2,1)}, bf16[96,4224]{1,0:T(8,128)(2,1)}, u32[]{:S(2)}, u32[]{:S(2)}) collective-permute-start(bf16[96,4224]{1,0:T(8,128)(2,1)} %collective-permute-done.7.refs_2_), channel_id=1, source_target_pairs={{0,4},{4,0},{1,5},{5,1},{2,6},{6,2},{3,7},{7,3},{8,12},{12,8},{9,1... | collective-permute-start | bytes 2433032 | tf_op jit(solution)/shard_map/ppermute | solution.py:247
  134.3 3.2 %collective-permute-start.11 = (bf16[96,4224]{1,0:T(8,128)(2,1)}, bf16[96,4224]{1,0:T(8,128)(2,1)S(1)}, u32[]{:S(2)}, u32[]{:S(2)}) collective-permute-start(bf16[96,4224]{1,0:T(8,128)(2,1)} %collective-permute-done.6.refs_2_), channel_id=1, source_target_pairs={{0,3},{1,0},{2,1},{3,2},{4,7},{5,4},{6,5},{7,6},{8,11},{9,8},{10,9... | collective-permute-start | bytes 2433032 | tf_op jit(solution)/shard_map/ppermute | solution.py:247
  137.7 8.3 %pair_blocks.8 = (f32[2,8,128,2176]{3,2,1,0:T(8,128)}, f32[8,128]{1,0:T(8,128)}) custom-call(s32[8]{0:T(128)S(1)} %stack.107.refs_0_, bf16[128,4096]{1,0:T(8,128)(2,1)S(1)} %get-tuple-element.25.refs_1_, bf16[96,4224]{1,0:T(8,128)(2,1)} %collective-permute-done.6.refs_2_, ...), custom_call_target="tpu_custom_call", output_to_operand_aliasing={{0}: (7, {})} | custom-call | flops 400000000 | bytes 400000 | tf_op jit(solution)/shard_map/pair_blocks/pallas_call | solution.py:227
  146.0 3.4 %collective-permute-done.13.refs_4_ = bf16[96,4224]{1,0:T(8,128)(2,1)S(1)} collective-permute-done((bf16[96,4224]{1,0:T(8,128)(2,1)}, bf16[96,4224]{1,0:T(8,128)(2,1)S(1)}, u32[]{:S(2)}, u32[]{:S(2)}) %collective-permute-start.13) | collective-permute-done | bytes 811040 | tf_op jit(solution)/shard_map/ppermute | solution.py:319
  152.5 6.9 %pair_blocks.9 = (f32[2,8,128,2176]{3,2,1,0:T(8,128)}, f32[8,128]{1,0:T(8,128)}) custom-call(s32[6]{0:T(128)S(1)} %stack.86.refs_0_, bf16[128,4096]{1,0:T(8,128)(2,1)S(1)} %get-tuple-element.25.refs_1_, bf16[96,4224]{1,0:T(8,128)(2,1)S(1)} %collective-permute-done.11.refs_2_, ...), custom_call_target="tpu_custom_call", output_to_operand_aliasing={{0}: (6, {})} | custom-call | flops 300000000 | bytes 300000 | tf_op jit(solution)/shard_map/pair_blocks/pallas_call | solution.py:227
  (39 shorter events, 17.0 us)
Async XLA Ops:
  1.9 0.7 copy-start
  2.6 0.7 copy-start.1
  3.3 0.7 copy-start.2
  4.0 0.9 copy-start.3
  22.6 20.2 %collective-permute-start = (bf16[96,4224]{1,0:T(8,128)(2,1)S(1)}, bf16[96,4224]{1,0:T(8,128)(2,1)}, u32[]{:S(2)}, u32[]{:S(2)}) collective-permute-start(bf16[96,4224]{1,0:T(8,128)(2,1)S(1)} %bitcast.22), channel_id=1, source_target_pairs={{0,24},{8,0},{16,8},{24,16},{1,25},{9,1},{17,9},{25,17},{2,26},{10... | collective-permute-start | bytes 2433032 | tf_op jit(solution)/shard_map/ppermute | solution.py:247
  42.9 21.2 %collective-permute-start.1 = (bf16[96,4224]{1,0:T(8,128)(2,1)}, bf16[96,4224]{1,0:T(8,128)(2,1)S(1)}, u32[]{:S(2)}, u32[]{:S(2)}) collective-permute-start(bf16[96,4224]{1,0:T(8,128)(2,1)} %collective-permute-done.refs_2_), channel_id=1, source_target_pairs={{0,24},{8,0},{16,8},{24,16},{1,25},{9,1},{17,9},{25,17},{2,26},{10... | collective-permute-start | bytes 2433032 | tf_op jit(solution)/shard_map/ppermute | solution.py:247
  51.5 27.2 %collective-permute-start.3 = (bf16[96,4224]{1,0:T(8,128)(2,1)}, bf16[96,4224]{1,0:T(8,128)(2,1)S(1)}, u32[]{:S(2)}, u32[]{:S(2)}) collective-permute-start(bf16[96,4224]{1,0:T(8,128)(2,1)} %collective-permute-done.refs_2_), channel_id=1, source_target_pairs={{0,3},{1,0},{2,1},{3,2},{4,7},{5,4},{6,5},{7,6},{8,11},{9,8},{10,9... | collective-permute-start | bytes 2433032 | tf_op jit(solution)/shard_map/ppermute | solution.py:247
  54.6 22.5 %collective-permute-start.4 = (bf16[96,4224]{1,0:T(8,128)(2,1)}, bf16[96,4224]{1,0:T(8,128)(2,1)}, u32[]{:S(2)}, u32[]{:S(2)}) collective-permute-start(bf16[96,4224]{1,0:T(8,128)(2,1)} %collective-permute-done.refs_2_), channel_id=1, source_target_pairs={{0,1},{1,2},{2,3},{3,0},{4,5},{5,6},{6,7},{7,4},{8,9},{9,10},{10,1... | collective-permute-start | bytes 2433032 | tf_op jit(solution)/shard_map/ppermute | solution.py:247
  54.6 24.1 %collective-permute-start.5 = (bf16[96,4224]{1,0:T(8,128)(2,1)}, bf16[96,4224]{1,0:T(8,128)(2,1)}, u32[]{:S(2)}, u32[]{:S(2)}) collective-permute-start(bf16[96,4224]{1,0:T(8,128)(2,1)} %collective-permute-done.refs_2_), channel_id=1, source_target_pairs={{0,4},{4,0},{1,5},{5,1},{2,6},{6,2},{3,7},{7,3},{8,12},{12,8},{9,1... | collective-permute-start | bytes 2433032 | tf_op jit(solution)/shard_map/ppermute | solution.py:247
  65.2 27.5 %collective-permute-start.2 = (bf16[96,4224]{1,0:T(8,128)(2,1)}, bf16[96,4224]{1,0:T(8,128)(2,1)}, u32[]{:S(2)}, u32[]{:S(2)}) collective-permute-start(bf16[96,4224]{1,0:T(8,128)(2,1)} %broadcast_select_fusion), channel_id=1, source_target_pairs={{0,4},{4,0},{1,5},{5,1},{2,6},{6,2},{3,7},{7,3},{8,12},{12,8},{9,1... | collective-permute-start | bytes 2433032 | tf_op jit(solution)/shard_map/ppermute | solution.py:247
  68.3 27.4 %collective-permute-start.9 = (bf16[96,4224]{1,0:T(8,128)(2,1)S(1)}, bf16[96,4224]{1,0:T(8,128)(2,1)}, u32[]{:S(2)}, u32[]{:S(2)}) collective-permute-start(bf16[96,4224]{1,0:T(8,128)(2,1)S(1)} %bitcast.24), channel_id=1, source_target_pairs={{0,1},{1,2},{2,3},{3,0},{4,5},{5,6},{6,7},{7,4},{8,9},{9,10},{10,1... | collective-permute-start | bytes 2433032 | tf_op jit(solution)/shard_map/ppermute | solution.py:247
  77.1 18.6 %collective-permute-start.10 = (bf16[96,4224]{1,0:T(8,128)(2,1)}, bf16[96,4224]{1,0:T(8,128)(2,1)}, u32[]{:S(2)}, u32[]{:S(2)}) collective-permute-start(bf16[96,4224]{1,0:T(8,128)(2,1)} %collective-permute-done.4.refs_4_), channel_id=1, source_target_pairs={{1,25},{2,26},{3,27},{9,1},{10,2},{11,3},{17,9},{18,10},{19,11},{2... | collective-permute-start | bytes 2433032 | tf_op jit(solution)/shard_map/ppermute | solution.py:253
  78.6 20.3 %collective-permute-start.7 = (bf16[96,4224]{1,0:T(8,128)(2,1)S(1)}, bf16[96,4224]{1,0:T(8,128)(2,1)}, u32[]{:S(2)}, u32[]{:S(2)}) collective-permute-start(bf16[96,4224]{1,0:T(8,128)(2,1)S(1)} %collective-permute-done.3.refs_3_), channel_id=1, source_target_pairs={{0,3},{1,0},{2,1},{3,2},{4,7},{5,4},{6,5},{7,6},{8,11},{9,8},{10,9... | collective-permute-start | bytes 2433032 | tf_op jit(solution)/shard_map/ppermute | solution.py:247
  78.6 30.8 %collective-permute-start.8 = (bf16[96,4224]{1,0:T(8,128)(2,1)}, bf16[96,4224]{1,0:T(8,128)(2,1)}, u32[]{:S(2)}, u32[]{:S(2)}) collective-permute-start(bf16[96,4224]{1,0:T(8,128)(2,1)} %collective-permute-done.5.refs_5_), channel_id=1, source_target_pairs={{0,1},{1,2},{2,3},{3,0},{4,5},{5,6},{6,7},{7,4},{8,9},{9,10},{10,1... | collective-permute-start | bytes 2433032 | tf_op jit(solution)/shard_map/ppermute | solution.py:247
  92.7 25.0 %collective-permute-start.6 = (bf16[96,4224]{1,0:T(8,128)(2,1)}, bf16[96,4224]{1,0:T(8,128)(2,1)}, u32[]{:S(2)}, u32[]{:S(2)}) collective-permute-start(bf16[96,4224]{1,0:T(8,128)(2,1)} %collective-permute-done.2.refs_4_), channel_id=1, source_target_pairs={{0,3},{1,0},{2,1},{3,2},{4,7},{5,4},{6,5},{7,6},{8,11},{9,8},{10,9... | collective-permute-start | bytes 2433032 | tf_op jit(solution)/shard_map/ppermute | solution.py:247
  95.6 33.0 %collective-permute-start.18 = (bf16[96,4224]{1,0:T(8,128)(2,1)S(1)}, bf16[96,4224]{1,0:T(8,128)(2,1)}, u32[]{:S(2)}, u32[]{:S(2)}) collective-permute-start(bf16[96,4224]{1,0:T(8,128)(2,1)S(1)} %bitcast.25), channel_id=1, source_target_pairs={{0,3},{1,0},{2,1},{3,2},{4,7},{5,4},{6,5},{7,6},{8,11},{9,8},{10,9... | collective-permute-start | bytes 2433032 | tf_op jit(solution)/shard_map/ppermute | solution.py:247
  95.7 35.4 %collective-permute-start.16 = (bf16[96,4224]{1,0:T(8,128)(2,1)S(1)}, bf16[96,4224]{1,0:T(8,128)(2,1)}, u32[]{:S(2)}, u32[]{:S(2)}) collective-permute-start(bf16[96,4224]{1,0:T(8,128)(2,1)S(1)} %collective-permute-done.3.refs_3_), channel_id=1, source_target_pairs={{0,4},{4,0},{1,5},{5,1},{2,6},{6,2},{3,7},{7,3},{8,12},{12,8},{9,1... | collective-permute-start | bytes 2433032 | tf_op jit(solution)/shard_map/ppermute | solution.py:247
  98.9 35.4 %collective-permute-start.17 = (bf16[96,4224]{1,0:T(8,128)(2,1)S(1)}, bf16[96,4224]{1,0:T(8,128)(2,1)}, u32[]{:S(2)}, u32[]{:S(2)}) collective-permute-start(bf16[96,4224]{1,0:T(8,128)(2,1)S(1)} %collective-permute-done.3.refs_3_), channel_id=1, source_target_pairs={{3,27},{11,3},{19,11},{27,19},{7,31},{15,7},{23,15},{31,23},{35,59... | collective-permute-start | bytes 2433032 | tf_op jit(solution)/shard_map/ppermute | solution.py:253
  109.4 28.3 %collective-permute-start.15 = (bf16[96,4224]{1,0:T(8,128)(2,1)}, bf16[96,4224]{1,0:T(8,128)(2,1)}, u32[]{:S(2)}, u32[]{:S(2)}) collective-permute-start(bf16[96,4224]{1,0:T(8,128)(2,1)} %collective-permute-done.2.refs_4_), channel_id=1, source_target_pairs={{0,1},{1,2},{2,3},{3,0},{4,5},{5,6},{6,7},{7,4},{8,9},{9,10},{10,1... | collective-permute-start | bytes 2433032 | tf_op jit(solution)/shard_map/ppermute | solution.py:247
  117.7 28.3 %collective-permute-start.14 = (bf16[96,4224]{1,0:T(8,128)(2,1)}, bf16[96,4224]{1,0:T(8,128)(2,1)S(1)}, u32[]{:S(2)}, u32[]{:S(2)}) collective-permute-start(bf16[96,4224]{1,0:T(8,128)(2,1)} %collective-permute-done.7.refs_2_), channel_id=1, source_target_pairs={{2,26},{3,27},{10,2},{11,3},{18,10},{19,11},{26,18},{27,19},{6,30}... | collective-permute-start | bytes 2433032 | tf_op jit(solution)/shard_map/ppermute | solution.py:253
  128.7 20.7 %collective-permute-start.13 = (bf16[96,4224]{1,0:T(8,128)(2,1)}, bf16[96,4224]{1,0:T(8,128)(2,1)S(1)}, u32[]{:S(2)}, u32[]{:S(2)}) collective-permute-start(bf16[96,4224]{1,0:T(8,128)(2,1)} %collective-permute-done.9.refs_5_), channel_id=1, source_target_pairs={{3,0},{0,1},{7,4},{4,5},{11,8},{8,9},{15,12},{12,13},{19,16},{16,1... | collective-permute-start | bytes 2433032 | tf_op jit(solution)/shard_map/ppermute | solution.py:319
  131.1 19.4 %collective-permute-start.12 = (bf16[96,4224]{1,0:T(8,128)(2,1)}, bf16[96,4224]{1,0:T(8,128)(2,1)}, u32[]{:S(2)}, u32[]{:S(2)}) collective-permute-start(bf16[96,4224]{1,0:T(8,128)(2,1)} %collective-permute-done.7.refs_2_), channel_id=1, source_target_pairs={{0,4},{4,0},{1,5},{5,1},{2,6},{6,2},{3,7},{7,3},{8,12},{12,8},{9,1... | collective-permute-start | bytes 2433032 | tf_op jit(solution)/shard_map/ppermute | solution.py:247
  134.3 18.2 %collective-permute-start.11 = (bf16[96,4224]{1,0:T(8,128)(2,1)}, bf16[96,4224]{1,0:T(8,128)(2,1)S(1)}, u32[]{:S(2)}, u32[]{:S(2)}) collective-permute-start(bf16[96,4224]{1,0:T(8,128)(2,1)} %collective-permute-done.6.refs_2_), channel_id=1, source_target_pairs={{0,3},{1,0},{2,1},{3,2},{4,7},{5,4},{6,5},{7,6},{8,11},{9,8},{10,9... | collective-permute-start | bytes 2433032 | tf_op jit(solution)/shard_map/ppermute | solution.py:247

commit v3 on v2

--- a/solution.py
+++ b/solution.py
@@ -31,7 +31,14 @@
     return table.reshape(2, 2 * LANES, LANES).astype(np.float32)
 
 
-def channelize_kernel(spectra_len, cap, volt, lists, counts, taps, trig, out, square, frames, weights):
+def channelize_kernel(spectra_len, cap, volt, lists_far, counts_far, taps_far, trig_far, out, *scratch):
+    lists, counts, taps, trig, sems, square, frames, weights = scratch
+    fars, nears = (lists_far, counts_far, taps_far, trig_far), (lists, counts, taps, trig)
+    copies = [pltpu.make_async_copy(f, n, sems.at[i]) for i, (f, n) in enumerate(zip(fars, nears))]
+    for copy in copies:
+        copy.start()
+    for copy in copies:
+        copy.wait()
     samples = volt.shape[1]
     in_count = counts.shape[1]
     tiles = -(-samples // LANES)
@@ -131,7 +138,13 @@
     return pl.pallas_call(
         kernel,
         out_shape=jax.ShapeDtypeStruct((groups, cap, row_width), jnp.bfloat16),
+        in_specs=[pl.BlockSpec(memory_space=pltpu.VMEM)] + [pl.BlockSpec(memory_space=pl.ANY)] * 4,
         scratch_shapes=[
+            pltpu.VMEM(keep_list.shape, jnp.int32),
+            pltpu.VMEM((coarse, in_count), jnp.int32),
+            pltpu.VMEM(filter_taps.shape, jnp.float32),
+            pltpu.VMEM((2, 2 * LANES, LANES), jnp.float32),
+            pltpu.SemaphoreType.DMA((4,)),
             pltpu.VMEM((LANES, LANES), jnp.float32),
             pltpu.VMEM((2, tiles * 2 * cap, 2 * LANES), jnp.bfloat16),
             pltpu.VMEM((2, 3, 2 * LANES, 2 * LANES), jnp.bfloat16),
@@ -168,7 +181,7 @@
         side_out = refs.pop(0)
     else:
         token = refs.pop(0)
-    buf, sems = refs
+    full, buf, sems = refs
     count = len(picked)
     width = (arrays[0][0].shape[1] - LANES) // fine
     both_numbers = (((1,), (1,)), ((), ()))
@@ -179,20 +192,19 @@
         return arrays[n][0][:, lanes]
 
     copies = []
-    every = [row_places(rows(n, slice(fine * width, fine * width + LANES)), in_count, cap, 0) for n in range(count)]
+    for n in range(count):
+        told = rows(n, slice(fine * width, fine * width + LANES))
+        spread = row_places(told, in_count, cap, 0)
+        placed = jnp.dot(spread, rows(n, slice(0, fine * width)), preferred_element_type=jnp.float32)
+        full[n * LANES : (n + 1) * LANES] = placed.astype(jnp.bfloat16)
     for f in range(fine):
         lanes = slice(f * width, (f + 1) * width)
-        full = [
-            jnp.dot(every[n], rows(n, lanes), preferred_element_type=jnp.float32).astype(jnp.bfloat16)
-            for n in range(count)
-        ]
         if first:
-            own = (full[0].astype(jnp.float32) * norm).astype(jnp.bfloat16)
+            own = (full[0:LANES, lanes].astype(jnp.float32) * norm).astype(jnp.bfloat16)
             side_out[:, lanes] = own
         else:
             own = side[:, lanes]
-        stacked = jnp.concatenate(full, axis=0) if count > 1 else full[0]
-        got = lax.dot_general(with_turned(own), stacked, both_numbers, preferred_element_type=jnp.float32)
+        got = lax.dot_general(with_turned(own), full[:, lanes], both_numbers, preferred_element_type=jnp.float32)
         for n in range(count):
             buf[n, 0, f] = got[0:LANES, n * LANES : (n + 1) * LANES]
             buf[n, 1, f] = got[LANES : 2 * LANES, n * LANES : (n + 1) * LANES]
@@ -232,6 +244,7 @@
         out_specs=[anywhere, vmem],
         out_shape=[whole, extra],
         scratch_shapes=[
+            pltpu.VMEM((count * LANES, width), jnp.bfloat16),
             pltpu.VMEM((count, 2, fine, LANES, LANES), jnp.float32),
             pltpu.SemaphoreType.DMA((count, fine)),
         ],
@@ -253,8 +266,8 @@
     return lax.ppermute(value, ("x", "y"), pairs)
 
 
-def after(value, token):
-    return lax.optimization_barrier((value, token))[0]
+def after(value, *tokens):
+    return lax.optimization_barrier((value,) + tokens)[0]
 
 
 def shards(voltages, filter_taps, sample_counts, keep_list):
@@ -284,52 +297,62 @@
         return offset(jnp.where(z == 0, 0, 2), flip, yy)
 
     one = moved(own, "x", -1)
-    own_up = moved(own, "y", -1)
-    own_down = moved(own, "y", 1)
+    own_z = moved(own, "zh", 1)
+    own_up = lax.ppermute(own, "y", [(1, 0), (2, 1), (3, 2)])
+    own_down = lax.ppermute(own, "y", [(2, 3), (3, 0)])
     result, side = correlate(None, None, [own], [jnp.int32(0)], sizes)
-    one_up = moved(one, "y", -1)
-    one_down = moved(one, "y", 1)
-    two = moved(one, "x", -1)
-    one_z = moved(one, "zh", 1)
-    result, token = correlate(result, side, [one], [offset(1, z, y)], sizes)
-    cross = moved(after(jnp.where(z == 1, own, two), token), "zh", 1)
+    later = after(one, side)
+    one_up = moved(later, "y", -1)
+    one_down = moved(later, "y", 1)
+    beyond = moved(after(own_z, side), "x", -2)
+    one_z = moved(later, "zh", 1)
+    result, token = correlate(result, side, [after(one, own_up, own_down)], [offset(1, z, y)], sizes)
+    cross = jnp.where(z == 0, own_z, beyond)
     one_far = moved(after(one_up, token), "y", -1)
-    onez_down = moved(after(one_z, token), "y", 1)
+    cross_down = moved(after(cross, token), "y", 1)
+    onez_down = moved(after(one_down, token), "zh", 1)
     two_down = down_x(after(one_down, token), (1, 2, 3))
     result, token = correlate(
         result,
         side,
-        [two, one_up, one_down, one_z],
-        [offset(2, z, y), offset(1, z, up), offset(1, z, down), offset(1, flip, y)],
+        [one_up, one_down, one_z, cross],
+        [offset(1, z, up), offset(1, z, down), offset(1, flip, y), crossed(y)],
         sizes,
     )
     cross_up = moved(after(cross, token), "y", -1)
-    cross_down = moved(after(cross, token), "y", 1)
-    onez_up = moved(after(one_up, token), "zh", 1)
+    cross_far = moved(after(cross_down, token), "y", 1)
+    onez_far = moved(after(one_far, token), "zh", 1)
+    two_far = down_x(after(one_far, token), (2, 3))
+    result, token = correlate(
+        result,
+        side,
+        [(y == 0, own_down, two_down), cross_down, one_far, onez_down],
+        [near(down), crossed(down), offset(1, z, far), offset(1, flip, down)],
+        sizes,
+    )
+    onez_up = moved(after(one_z, token), "y", -1)
+    own_far = lax.ppermute(after(own_down, token), "y", [(3, 0), (0, 1)])
+    two = moved(after(beyond, token), "zh", 1)
     two_up = down_x(after(one_up, token), (3,))
-    two_far = down_x(after(one_far, token), (2, 3))
-    result, token = correlate(
-        result,
-        side,
-        [one_far, onez_down, cross, (y == 0, own_down, two_down)],
-        [offset(1, z, far), offset(1, flip, down), crossed(y), near(down)],
-        sizes,
-    )
-    cross_far = moved(after(cross_up, token), "y", -1)
-    own_far = lax.ppermute(after(own_down, token), "y", [(3, 0), (0, 1)])
-    onez_far = moved(after(one_far, token), "zh", 1)
-    result, token = correlate(
-        result,
-        side,
-        [cross_up, cross_down, onez_up, (y == y_count - 1, two_up, own_up)],
-        [crossed(up), crossed(down), offset(1, flip, up), near(up)],
-        sizes,
-    )
-    result, token = correlate(
-        result,
-        side,
-        [cross_far, onez_far, (y < 2, own_far, two_far)],
-        [crossed(far), offset(1, flip, far), near(far)],
+    result, token = correlate(
+        result,
+        side,
+        [after(cross_up, two_far), cross_far, onez_far],
+        [crossed(up), crossed(far), offset(1, flip, far)],
+        sizes,
+    )
+    result, token = correlate(
+        result,
+        side,
+        [onez_up, two],
+        [offset(1, flip, up), offset(2, z, y)],
+        sizes,
+    )
+    result, token = correlate(
+        result,
+        side,
+        [(y == y_count - 1, two_up, own_up), (y < 2, own_far, two_far)],
+        [near(up), near(far)],
         sizes,
     )
     return result

time: 161 us -> 141 us (0.88)
  waiting for transfers between devices: 54.8 us -> 33.5 us
  starting transfers between devices: 38.8 us -> 42.1 us
  Pallas kernels: 44.4 us -> 42.3 us
    ppermute x15 -> x14, waiting for transfers between devices: 51.4 us -> 33.3 us  [moved(): lax.ppermute(value, axis, [(s, (s + steps) % count) for s in range(count)])]
    ppermute x1, waiting for transfers between devices: 3.36 us -> 0.01 us  [shards(): own_far = lax.ppermute(after(own_down, token), 'y', [(3, 0), (0, 1)])]
    ppermute x0 -> x2, starting transfers between devices: none -> 2.57 us  [the longest x1 1.29 us: shards(): own_down = lax.ppermute(own, 'y', [(2, 3), (3, 0)])]
    pallas_call x6 -> x7, Pallas kernels: 41.6 us -> 39.5 us  [correlate(): pl.pallas_call(kernel, in_specs=[pl.BlockSpec(memory_space=pltpu.SMEM)] +...]
    ppermute x15 -> x14, starting transfers between devices: 32.5 us -> 32.7 us  [moved(): lax.ppermute(value, axis, [(s, (s + steps) % count) for s in range(count)])]
  transfers between devices with their start and end apart: 19 -> 20, of which waited for: 8 -> 9; matrix products, arithmetic and copies ran while one was open for 1% -> 1% of each run, Pallas kernels for 22% -> 24%
where the time goes in v3:
time: 141 us; the launch traced here: 140 us
  Pallas kernels  42.3 us (30%)
  starting transfers between devices  42.1 us (30%)
  waiting for transfers between devices  33.5 us (24%)
  blocking collectives  15 us (11%)
  local copies, waits for them, and re-layouts  5.14 us (4%)
  other arithmetic  1.46 us (1%)
    pallas_call x7, Pallas kernels, correlate(): pl.pallas_call(kernel, in_specs=[pl.BlockSpec(memory_space=pltpu.SMEM)] +...  39.5 us
    ppermute x14, waiting for transfers between devices, moved(): lax.ppermute(value, axis, [(s, (s + steps) % count) for s in range(count)])  33.3 us
    ppermute x14, starting transfers between devices, moved(): lax.ppermute(value, axis, [(s, (s + steps) % count) for s in range(count)])  32.7 us
    all_to_all x1, blocking collectives, shards(): lax.all_to_all(outgoing, 'chan', split_axis=0, concat_axis=0, tiled=True)  15 us
    ppermute x3, starting transfers between devices, down_x(): return lax.ppermute(value, ('x', 'y'), pairs)  3.88 us
    unnamed x8, local copies, waits for them, and re-layouts  3 us
    ppermute x1, starting transfers between devices, shards(): own_far = lax.ppermute(after(own_down, token), 'y', [(3, 0), (0, 1)])  2.96 us
  transfers between devices with their start and end apart: 20, of which 9 were waited for; matrix products, arithmetic and copies ran while one was open for 1% of the time, Pallas kernels for 24%

profile of v3, /device:TPU:0, one launch (start us, length us, event | category | flops | bytes accessed | tf_op | source)
XLA Modules:
  0.0 140.0 jit_solution(8480029767262737981)
XLA Ops:
  4.9 2.8 %channelize.1 = bf16[4,24,4224]{2,1,0:T(8,128)(2,1)S(1)} custom-call(bf16[128,4336]{1,0:T(8,128)(2,1)S(1)} %reshape.6.refs_0_, s32[1,4,24]{2,1,0:T(4,128)S(1)} %copy-done.1, s32[2,32]{1,0:T(2,128)S(1)} %bitcast.26, f32[16,16]{1,0:T(8,128)S(1)} %copy-done, f32[2,256,128]{2,1,0:T(8,128)S(1)} %copy-done.3), custom_call_target="tpu_custom_call" | custom-call | flops 4000000000 | bytes 3000000 | tf_op jit(solution)/shard_map/channelize/pallas_call | solution.py:138
  7.7 15.0 %all_to_all.5 = bf16[4,24,4224]{2,1,0:T(8,128)(2,1)S(1)} all-to-all(bf16[4,24,4224]{2,1,0:T(8,128)(2,1)S(1)} %channelize.1), channel_id=1, replica_groups=mesh['chan'=4,'x'=4,'zh'=2,'y'=4] {'chan'}, dimensions={0} | all-to-all | bytes 1622016 | tf_op jit(solution)/shard_map/all_to_all | solution.py:281
  22.7 3.6 %collective-permute-start.6 = (bf16[96,4224]{1,0:T(8,128)(2,1)S(1)}, bf16[96,4224]{1,0:T(8,128)(2,1)}, u32[]{:S(2)}, u32[]{:S(2)}) collective-permute-start(bf16[96,4224]{1,0:T(8,128)(2,1)S(1)} %bitcast.21), channel_id=1, source_target_pairs={{0,4},{4,0},{1,5},{5,1},{2,6},{6,2},{3,7},{7,3},{8,12},{12,8},{9,1... | collective-permute-start | bytes 2433032 | tf_op jit(solution)/shard_map/ppermute | solution.py:260
  26.3 2.8 %collective-permute-start = (bf16[96,4224]{1,0:T(8,128)(2,1)S(1)}, bf16[96,4224]{1,0:T(8,128)(2,1)}, u32[]{:S(2)}, u32[]{:S(2)}) collective-permute-start(bf16[96,4224]{1,0:T(8,128)(2,1)S(1)} %bitcast.22), channel_id=1, source_target_pairs={{0,24},{8,0},{16,8},{24,16},{1,25},{9,1},{17,9},{25,17},{2,26},{10... | collective-permute-start | bytes 2433032 | tf_op jit(solution)/shard_map/ppermute | solution.py:260
  31.7 2.6 %own_block.1 = (f32[2,8,128,2176]{3,2,1,0:T(8,128)}, bf16[128,4096]{1,0:T(8,128)(2,1)S(1)}) custom-call(s32[2]{0:T(128)S(1)} %broadcast_3_refs_0_.2.refs_0_, bf16[96,4224]{1,0:T(8,128)(2,1)S(1)} %bitcast.25), custom_call_target="tpu_custom_call" | custom-call | flops 100000000 | bytes 100000 | tf_op jit(solution)/shard_map/own_block/pallas_call | solution.py:239
  34.3 10.4 %collective-permute-done.6 = bf16[96,4224]{1,0:T(8,128)(2,1)} collective-permute-done((bf16[96,4224]{1,0:T(8,128)(2,1)S(1)}, bf16[96,4224]{1,0:T(8,128)(2,1)}, u32[]{:S(2)}, u32[]{:S(2)}) %collective-permute-start.6) | collective-permute-done | bytes 811040 | tf_op jit(solution)/shard_map/ppermute | solution.py:260
  44.6 3.0 %collective-permute-start.7 = (bf16[96,4224]{1,0:T(8,128)(2,1)}, bf16[96,4224]{1,0:T(8,128)(2,1)}, u32[]{:S(2)}, u32[]{:S(2)}) collective-permute-start(bf16[96,4224]{1,0:T(8,128)(2,1)} %collective-permute-done.6), channel_id=1, source_target_pairs={{0,16},{8,24},{16,0},{24,8},{1,17},{9,25},{17,1},{25,9},{2,18},{10... | collective-permute-start | bytes 2433032 | tf_op jit(solution)/shard_map/ppermute | solution.py:260
  47.7 3.3 %collective-permute-start.11 = (bf16[96,4224]{1,0:T(8,128)(2,1)}, bf16[96,4224]{1,0:T(8,128)(2,1)}, u32[]{:S(2)}, u32[]{:S(2)}) collective-permute-start(bf16[96,4224]{1,0:T(8,128)(2,1)} %collective-permute-done.refs_2_), channel_id=1, source_target_pairs={{0,4},{4,0},{1,5},{5,1},{2,6},{6,2},{3,7},{7,3},{8,12},{12,8},{9,1... | collective-permute-start | bytes 2433032 | tf_op jit(solution)/shard_map/ppermute | solution.py:260
  54.5 4.9 %pair_blocks.6 = (f32[2,8,128,2176]{3,2,1,0:T(8,128)}, f32[8,128]{1,0:T(8,128)}) custom-call(s32[2]{0:T(128)S(1)} %pad_add_fusion.1.refs_0_, bf16[128,4096]{1,0:T(8,128)(2,1)S(1)} %get-tuple-element.30.refs_1_, bf16[96,4224]{1,0:T(8,128)(2,1)} %collective-permute-done.refs_2_, ...), custom_call_target="tpu_custom_call", output_to_operand_aliasing={{0}: (3, {})} | custom-call | flops 100000000 | bytes 100000 | tf_op jit(solution)/shard_map/pair_blocks/pallas_call | solution.py:239
  59.4 6.5 %collective-permute-done.7 = bf16[96,4224]{1,0:T(8,128)(2,1)} collective-permute-done((bf16[96,4224]{1,0:T(8,128)(2,1)}, bf16[96,4224]{1,0:T(8,128)(2,1)}, u32[]{:S(2)}, u32[]{:S(2)}) %collective-permute-start.7) | collective-permute-done | bytes 811040 | tf_op jit(solution)/shard_map/ppermute | solution.py:260
  68.7 2.3 %collective-permute-done.1.refs_2_ = bf16[96,4224]{1,0:T(8,128)(2,1)S(1)} collective-permute-done((bf16[96,4224]{1,0:T(8,128)(2,1)}, bf16[96,4224]{1,0:T(8,128)(2,1)S(1)}, u32[]{:S(2)}, u32[]{:S(2)}) %collective-permute-start.1) | collective-permute-done | bytes 811040 | tf_op jit(solution)/shard_map/ppermute | solution.py:260
  71.0 2.9 %collective-permute-start.9 = (bf16[96,4224]{1,0:T(8,128)(2,1)S(1)}, bf16[96,4224]{1,0:T(8,128)(2,1)}, u32[]{:S(2)}, u32[]{:S(2)}) collective-permute-start(bf16[96,4224]{1,0:T(8,128)(2,1)S(1)} %collective-permute-done.1.refs_2_), channel_id=1, source_target_pairs={{0,3},{1,0},{2,1},{3,2},{4,7},{5,4},{6,5},{7,6},{8,11},{9,8},{10,9... | collective-permute-start | bytes 2433032 | tf_op jit(solution)/shard_map/ppermute | solution.py:260
  76.3 6.8 %pair_blocks.7 = (f32[2,8,128,2176]{3,2,1,0:T(8,128)}, f32[8,128]{1,0:T(8,128)}) custom-call(s32[8]{0:T(128)S(1)} %stack.104.refs_0_, bf16[128,4096]{1,0:T(8,128)(2,1)S(1)} %get-tuple-element.30.refs_1_, bf16[96,4224]{1,0:T(8,128)(2,1)S(1)} %collective-permute-done.1.refs_2_, ...), custom_call_target="tpu_custom_call", output_to_operand_aliasing={{0}: (6, {})} | custom-call | flops 400000000 | bytes 400000 | tf_op jit(solution)/shard_map/pair_blocks/pallas_call | solution.py:239
  83.1 3.9 %collective-permute-start.17 = (bf16[96,4224]{1,0:T(8,128)(2,1)S(1)}, bf16[96,4224]{1,0:T(8,128)(2,1)}, u32[]{:S(2)}, u32[]{:S(2)}) collective-permute-start(bf16[96,4224]{1,0:T(8,128)(2,1)S(1)} %broadcast_select_fusion.refs_5_), channel_id=1, source_target_pairs={{0,3},{1,0},{2,1},{3,2},{4,7},{5,4},{6,5},{7,6},{8,11},{9,8},{10,9... | collective-permute-start | bytes 2433032 | tf_op jit(solution)/shard_map/ppermute | solution.py:260
  86.9 2.0 %collective-permute-done.8.refs_4_ = bf16[96,4224]{1,0:T(8,128)(2,1)} collective-permute-done((bf16[96,4224]{1,0:T(8,128)(2,1)S(1)}, bf16[96,4224]{1,0:T(8,128)(2,1)}, u32[]{:S(2)}, u32[]{:S(2)}) %collective-permute-start.8) | collective-permute-done | bytes 811040 | tf_op jit(solution)/shard_map/ppermute | solution.py:260
  88.9 3.6 %collective-permute-done.9.refs_5_ = bf16[96,4224]{1,0:T(8,128)(2,1)} collective-permute-done((bf16[96,4224]{1,0:T(8,128)(2,1)S(1)}, bf16[96,4224]{1,0:T(8,128)(2,1)}, u32[]{:S(2)}, u32[]{:S(2)}) %collective-permute-start.9) | collective-permute-done | bytes 811040 | tf_op jit(solution)/shard_map/ppermute | solution.py:260
  94.8 7.5 %pair_blocks.8 = (f32[2,8,128,2176]{3,2,1,0:T(8,128)}, f32[8,128]{1,0:T(8,128)}) custom-call(s32[8]{0:T(128)S(1)} %stack.97.refs_0_, bf16[128,4096]{1,0:T(8,128)(2,1)S(1)} %get-tuple-element.30.refs_1_, bf16[96,4224]{1,0:T(8,128)(2,1)} %collective-permute-done.2.refs_2_, ...), custom_call_target="tpu_custom_call", output_to_operand_aliasing={{0}: (7, {})} | custom-call | flops 400000000 | bytes 400000 | tf_op jit(solution)/shard_map/pair_blocks/pallas_call | solution.py:239
  102.3 6.3 %collective-permute-start.15 = (bf16[96,4224]{1,0:T(8,128)(2,1)}, bf16[96,4224]{1,0:T(8,128)(2,1)}, u32[]{:S(2)}, u32[]{:S(2)}) collective-permute-start(bf16[96,4224]{1,0:T(8,128)(2,1)} %collective-permute-done.11.refs_4_), channel_id=1, source_target_pairs={{0,3},{1,0},{2,1},{3,2},{4,7},{5,4},{6,5},{7,6},{8,11},{9,8},{10,9... | collective-permute-start | bytes 2433032 | tf_op jit(solution)/shard_map/ppermute | solution.py:260
  111.4 3.0 %collective-permute-start.13 = (bf16[96,4224]{1,0:T(8,128)(2,1)}, bf16[96,4224]{1,0:T(8,128)(2,1)}, u32[]{:S(2)}, u32[]{:S(2)}) collective-permute-start(bf16[96,4224]{1,0:T(8,128)(2,1)} %collective-permute-done.2.refs_2_), channel_id=1, source_target_pairs={{3,0},{0,1},{7,4},{4,5},{11,8},{8,9},{15,12},{12,13},{19,16},{16,1... | collective-permute-start | bytes 2433032 | tf_op jit(solution)/shard_map/ppermute | solution.py:334
  114.8 6.4 %pair_blocks.9 = (f32[2,8,128,2176]{3,2,1,0:T(8,128)}, f32[8,128]{1,0:T(8,128)}) custom-call(s32[6]{0:T(128)S(1)} %stack.111.refs_0_, bf16[128,4096]{1,0:T(8,128)(2,1)S(1)} %get-tuple-element.30.refs_1_, bf16[96,4224]{1,0:T(8,128)(2,1)} %collective-permute-done.17.refs_2_, ...), custom_call_target="tpu_custom_call", output_to_operand_aliasing={{0}: (5, {})} | custom-call | flops 300000000 | bytes 300000 | tf_op jit(solution)/shard_map/pair_blocks/pallas_call | solution.py:239
  121.3 2.6 %collective-permute-done.15.refs_2_ = bf16[96,4224]{1,0:T(8,128)(2,1)} collective-permute-done((bf16[96,4224]{1,0:T(8,128)(2,1)}, bf16[96,4224]{1,0:T(8,128)(2,1)}, u32[]{:S(2)}, u32[]{:S(2)}) %collective-permute-start.15) | collective-permute-done | bytes 811040 | tf_op jit(solution)/shard_map/ppermute | solution.py:260
  123.9 4.7 %collective-permute-done.16.refs_3_ = bf16[96,4224]{1,0:T(8,128)(2,1)} collective-permute-done((bf16[96,4224]{1,0:T(8,128)(2,1)}, bf16[96,4224]{1,0:T(8,128)(2,1)}, u32[]{:S(2)}, u32[]{:S(2)}) %collective-permute-start.16) | collective-permute-done | bytes 811040 | tf_op jit(solution)/shard_map/ppermute | solution.py:260
  128.5 5.6 %pair_blocks.10 = (f32[2,8,128,2176]{3,2,1,0:T(8,128)}, f32[8,128]{1,0:T(8,128)}) custom-call(s32[4]{0:T(128)S(1)} %pad_add_fusion.2.refs_0_, bf16[128,4096]{1,0:T(8,128)(2,1)S(1)} %get-tuple-element.30.refs_1_, bf16[96,4224]{1,0:T(8,128)(2,1)} %collective-permute-done.15.refs_2_, ...), custom_call_target="tpu_custom_call", output_to_operand_aliasing={{0}: (4, {})} | custom-call | flops 200000000 | bytes 200000 | tf_op jit(solution)/shard_map/pair_blocks/pallas_call | solution.py:239
  134.2 5.7 %pair_blocks.11 = (f32[2,8,128,2176]{3,2,1,0:T(8,128)}, f32[8,128]{1,0:T(8,128)}) custom-call(s32[4]{0:T(128)S(1)} %pad_add_fusion.refs_0_, bf16[128,4096]{1,0:T(8,128)(2,1)S(1)} %get-tuple-element.30.refs_1_, bf16[96,4224]{1,0:T(8,128)(2,1)S(1)} %collective-permute-done.12.refs_2_, ...), custom_call_target="tpu_custom_call", output_to_operand_aliasing={{0}: (6, {})} | custom-call | flops 200000000 | bytes 200000 | tf_op jit(solution)/shard_map/pair_blocks/pallas_call | solution.py:239
  (43 shorter events, 21.6 us)
Async XLA Ops:
  1.9 0.7 copy-start
  2.6 0.7 copy-start.1
  3.3 0.7 copy-start.2
  4.0 0.9 copy-start.3
  22.7 21.9 %collective-permute-start.6 = (bf16[96,4224]{1,0:T(8,128)(2,1)S(1)}, bf16[96,4224]{1,0:T(8,128)(2,1)}, u32[]{:S(2)}, u32[]{:S(2)}) collective-permute-start(bf16[96,4224]{1,0:T(8,128)(2,1)S(1)} %bitcast.21), channel_id=1, source_target_pairs={{0,4},{4,0},{1,5},{5,1},{2,6},{6,2},{3,7},{7,3},{8,12},{12,8},{9,1... | collective-permute-start | bytes 2433032 | tf_op jit(solution)/shard_map/ppermute | solution.py:260
  26.3 21.4 %collective-permute-start = (bf16[96,4224]{1,0:T(8,128)(2,1)S(1)}, bf16[96,4224]{1,0:T(8,128)(2,1)}, u32[]{:S(2)}, u32[]{:S(2)}) collective-permute-start(bf16[96,4224]{1,0:T(8,128)(2,1)S(1)} %bitcast.22), channel_id=1, source_target_pairs={{0,24},{8,0},{16,8},{24,16},{1,25},{9,1},{17,9},{25,17},{2,26},{10... | collective-permute-start | bytes 2433032 | tf_op jit(solution)/shard_map/ppermute | solution.py:260
  29.1 23.5 %collective-permute-start.4 = (bf16[96,4224]{1,0:T(8,128)(2,1)S(1)}, bf16[96,4224]{1,0:T(8,128)(2,1)S(1)}, u32[]{:S(2)}, u32[]{:S(2)}) collective-permute-start(bf16[96,4224]{1,0:T(8,128)(2,1)S(1)} %bitcast.23), channel_id=1, source_target_pairs={{1,0},{2,1},{3,2},{5,4},{6,5},{7,6},{9,8},{10,9},{11,10},{13,12},{... | collective-permute-start | bytes 2433032 | tf_op jit(solution)/shard_map/ppermute | solution.py:301
  30.3 24.1 %collective-permute-start.2 = (bf16[96,4224]{1,0:T(8,128)(2,1)S(1)}, bf16[96,4224]{1,0:T(8,128)(2,1)}, u32[]{:S(2)}, u32[]{:S(2)}) collective-permute-start(bf16[96,4224]{1,0:T(8,128)(2,1)S(1)} %bitcast.24), channel_id=1, source_target_pairs={{2,3},{3,0},{6,7},{7,4},{10,11},{11,8},{14,15},{15,12},{18,19},{19... | collective-permute-start | bytes 2433032 | tf_op jit(solution)/shard_map/ppermute | solution.py:302
  44.6 21.2 %collective-permute-start.7 = (bf16[96,4224]{1,0:T(8,128)(2,1)}, bf16[96,4224]{1,0:T(8,128)(2,1)}, u32[]{:S(2)}, u32[]{:S(2)}) collective-permute-start(bf16[96,4224]{1,0:T(8,128)(2,1)} %collective-permute-done.6), channel_id=1, source_target_pairs={{0,16},{8,24},{16,0},{24,8},{1,17},{9,25},{17,1},{25,9},{2,18},{10... | collective-permute-start | bytes 2433032 | tf_op jit(solution)/shard_map/ppermute | solution.py:260
  47.7 28.6 %collective-permute-start.11 = (bf16[96,4224]{1,0:T(8,128)(2,1)}, bf16[96,4224]{1,0:T(8,128)(2,1)}, u32[]{:S(2)}, u32[]{:S(2)}) collective-permute-start(bf16[96,4224]{1,0:T(8,128)(2,1)} %collective-permute-done.refs_2_), channel_id=1, source_target_pairs={{0,4},{4,0},{1,5},{5,1},{2,6},{6,2},{3,7},{7,3},{8,12},{12,8},{9,1... | collective-permute-start | bytes 2433032 | tf_op jit(solution)/shard_map/ppermute | solution.py:260
  51.0 23.0 %collective-permute-start.3 = (bf16[96,4224]{1,0:T(8,128)(2,1)}, bf16[96,4224]{1,0:T(8,128)(2,1)}, u32[]{:S(2)}, u32[]{:S(2)}) collective-permute-start(bf16[96,4224]{1,0:T(8,128)(2,1)} %collective-permute-done.refs_2_), channel_id=1, source_target_pairs={{0,1},{1,2},{2,3},{3,0},{4,5},{5,6},{6,7},{7,4},{8,9},{9,10},{10,1... | collective-permute-start | bytes 2433032 | tf_op jit(solution)/shard_map/ppermute | solution.py:260
  52.6 18.5 %collective-permute-start.1 = (bf16[96,4224]{1,0:T(8,128)(2,1)}, bf16[96,4224]{1,0:T(8,128)(2,1)S(1)}, u32[]{:S(2)}, u32[]{:S(2)}) collective-permute-start(bf16[96,4224]{1,0:T(8,128)(2,1)} %collective-permute-done.refs_2_), channel_id=1, source_target_pairs={{0,3},{1,0},{2,1},{3,2},{4,7},{5,4},{6,5},{7,6},{8,11},{9,8},{10,9... | collective-permute-start | bytes 2433032 | tf_op jit(solution)/shard_map/ppermute | solution.py:260
  67.1 21.8 %collective-permute-start.8 = (bf16[96,4224]{1,0:T(8,128)(2,1)S(1)}, bf16[96,4224]{1,0:T(8,128)(2,1)}, u32[]{:S(2)}, u32[]{:S(2)}) collective-permute-start(bf16[96,4224]{1,0:T(8,128)(2,1)S(1)} %broadcast_select_fusion.refs_5_), channel_id=1, source_target_pairs={{0,1},{1,2},{2,3},{3,0},{4,5},{5,6},{6,7},{7,4},{8,9},{9,10},{10,1... | collective-permute-start | bytes 2433032 | tf_op jit(solution)/shard_map/ppermute | solution.py:260
  71.0 21.5 %collective-permute-start.9 = (bf16[96,4224]{1,0:T(8,128)(2,1)S(1)}, bf16[96,4224]{1,0:T(8,128)(2,1)}, u32[]{:S(2)}, u32[]{:S(2)}) collective-permute-start(bf16[96,4224]{1,0:T(8,128)(2,1)S(1)} %collective-permute-done.1.refs_2_), channel_id=1, source_target_pairs={{0,3},{1,0},{2,1},{3,2},{4,7},{5,4},{6,5},{7,6},{8,11},{9,8},{10,9... | collective-permute-start | bytes 2433032 | tf_op jit(solution)/shard_map/ppermute | solution.py:260
  74.0 20.2 %collective-permute-start.10 = (bf16[96,4224]{1,0:T(8,128)(2,1)}, bf16[96,4224]{1,0:T(8,128)(2,1)}, u32[]{:S(2)}, u32[]{:S(2)}) collective-permute-start(bf16[96,4224]{1,0:T(8,128)(2,1)} %collective-permute-done.3.refs_3_), channel_id=1, source_target_pairs={{0,4},{4,0},{1,5},{5,1},{2,6},{6,2},{3,7},{7,3},{8,12},{12,8},{9,1... | collective-permute-start | bytes 2433032 | tf_op jit(solution)/shard_map/ppermute | solution.py:260
  74.6 20.2 %collective-permute-start.5 = (bf16[96,4224]{1,0:T(8,128)(2,1)}, bf16[96,4224]{1,0:T(8,128)(2,1)}, u32[]{:S(2)}, u32[]{:S(2)}) collective-permute-start(bf16[96,4224]{1,0:T(8,128)(2,1)} %collective-permute-done.3.refs_3_), channel_id=1, source_target_pairs={{1,25},{2,26},{3,27},{9,1},{10,2},{11,3},{17,9},{18,10},{19,11},{2... | collective-permute-start | bytes 2433032 | tf_op jit(solution)/shard_map/ppermute | solution.py:266
  83.1 26.8 %collective-permute-start.17 = (bf16[96,4224]{1,0:T(8,128)(2,1)S(1)}, bf16[96,4224]{1,0:T(8,128)(2,1)}, u32[]{:S(2)}, u32[]{:S(2)}) collective-permute-start(bf16[96,4224]{1,0:T(8,128)(2,1)S(1)} %broadcast_select_fusion.refs_5_), channel_id=1, source_target_pairs={{0,3},{1,0},{2,1},{3,2},{4,7},{5,4},{6,5},{7,6},{8,11},{9,8},{10,9... | collective-permute-start | bytes 2433032 | tf_op jit(solution)/shard_map/ppermute | solution.py:260
  88.9 21.8 %collective-permute-start.18 = (bf16[96,4224]{1,0:T(8,128)(2,1)}, bf16[96,4224]{1,0:T(8,128)(2,1)}, u32[]{:S(2)}, u32[]{:S(2)}) collective-permute-start(bf16[96,4224]{1,0:T(8,128)(2,1)} %collective-permute-done.8.refs_4_), channel_id=1, source_target_pairs={{0,1},{1,2},{2,3},{3,0},{4,5},{5,6},{6,7},{7,4},{8,9},{9,10},{10,1... | collective-permute-start | bytes 2433032 | tf_op jit(solution)/shard_map/ppermute | solution.py:260
  92.5 18.9 %collective-permute-start.14 = (bf16[96,4224]{1,0:T(8,128)(2,1)}, bf16[96,4224]{1,0:T(8,128)(2,1)}, u32[]{:S(2)}, u32[]{:S(2)}) collective-permute-start(bf16[96,4224]{1,0:T(8,128)(2,1)} %collective-permute-done.9.refs_5_), channel_id=1, source_target_pairs={{2,26},{3,27},{10,2},{11,3},{18,10},{19,11},{26,18},{27,19},{6,30}... | collective-permute-start | bytes 2433032 | tf_op jit(solution)/shard_map/ppermute | solution.py:266
  94.1 20.7 %collective-permute-start.19 = (bf16[96,4224]{1,0:T(8,128)(2,1)}, bf16[96,4224]{1,0:T(8,128)(2,1)}, u32[]{:S(2)}, u32[]{:S(2)}) collective-permute-start(bf16[96,4224]{1,0:T(8,128)(2,1)} %collective-permute-done.9.refs_5_), channel_id=1, source_target_pairs={{0,4},{4,0},{1,5},{5,1},{2,6},{6,2},{3,7},{7,3},{8,12},{12,8},{9,1... | collective-permute-start | bytes 2433032 | tf_op jit(solution)/shard_map/ppermute | solution.py:260
  102.3 21.6 %collective-permute-start.15 = (bf16[96,4224]{1,0:T(8,128)(2,1)}, bf16[96,4224]{1,0:T(8,128)(2,1)}, u32[]{:S(2)}, u32[]{:S(2)}) collective-permute-start(bf16[96,4224]{1,0:T(8,128)(2,1)} %collective-permute-done.11.refs_4_), channel_id=1, source_target_pairs={{0,3},{1,0},{2,1},{3,2},{4,7},{5,4},{6,5},{7,6},{8,11},{9,8},{10,9... | collective-permute-start | bytes 2433032 | tf_op jit(solution)/shard_map/ppermute | solution.py:260
  109.9 18.6 %collective-permute-start.16 = (bf16[96,4224]{1,0:T(8,128)(2,1)}, bf16[96,4224]{1,0:T(8,128)(2,1)}, u32[]{:S(2)}, u32[]{:S(2)}) collective-permute-start(bf16[96,4224]{1,0:T(8,128)(2,1)} %collective-permute-done.7), channel_id=1, source_target_pairs={{0,4},{4,0},{1,5},{5,1},{2,6},{6,2},{3,7},{7,3},{8,12},{12,8},{9,1... | collective-permute-start | bytes 2433032 | tf_op jit(solution)/shard_map/ppermute | solution.py:260
  110.7 23.5 %collective-permute-start.12 = (bf16[96,4224]{1,0:T(8,128)(2,1)S(1)}, bf16[96,4224]{1,0:T(8,128)(2,1)S(1)}, u32[]{:S(2)}, u32[]{:S(2)}) collective-permute-start(bf16[96,4224]{1,0:T(8,128)(2,1)S(1)} %collective-permute-done.1.refs_2_), channel_id=1, source_target_pairs={{3,27},{11,3},{19,11},{27,19},{7,31},{15,7},{23,15},{31,23},{35,59... | collective-permute-start | bytes 2433032 | tf_op jit(solution)/shard_map/ppermute | solution.py:266
  111.4 22.8 %collective-permute-start.13 = (bf16[96,4224]{1,0:T(8,128)(2,1)}, bf16[96,4224]{1,0:T(8,128)(2,1)}, u32[]{:S(2)}, u32[]{:S(2)}) collective-permute-start(bf16[96,4224]{1,0:T(8,128)(2,1)} %collective-permute-done.2.refs_2_), channel_id=1, source_target_pairs={{3,0},{0,1},{7,4},{4,5},{11,8},{8,9},{15,12},{12,13},{19,16},{16,1... | collective-permute-start | bytes 2433032 | tf_op jit(solution)/shard_map/ppermute | solution.py:334

commit v4 on v3

--- a/solution.py
+++ b/solution.py
@@ -191,7 +191,7 @@
             return jnp.where(spots[count + n] == 1, arrays[n][0][:, lanes], arrays[n][1][:, lanes])
         return arrays[n][0][:, lanes]
 
-    copies = []
+    copies, part = [], fine // 2
     for n in range(count):
         told = rows(n, slice(fine * width, fine * width + LANES))
         spread = row_places(told, in_count, cap, 0)
@@ -208,10 +208,12 @@
         for n in range(count):
             buf[n, 0, f] = got[0:LANES, n * LANES : (n + 1) * LANES]
             buf[n, 1, f] = got[LANES : 2 * LANES, n * LANES : (n + 1) * LANES]
-            column = pl.ds(pl.multiple_of(spots[n] * LANES, LANES), LANES)
-            copy = pltpu.make_async_copy(buf.at[n, :, f], out.at[:, f, :, column], sems.at[n, f])
-            copy.start()
-            copies.append(copy)
+            if f % part == part - 1:
+                now = pl.ds(f - part + 1, part)
+                column = pl.ds(pl.multiple_of(spots[n] * LANES, LANES), LANES)
+                copy = pltpu.make_async_copy(buf.at[n, :, now], out.at[:, now, :, column], sems.at[n, f // part])
+                copy.start()
+                copies.append(copy)
     if not first:
         token[...] = jnp.zeros(token.shape, token.dtype)
     for copy in copies:
@@ -246,7 +248,7 @@
         scratch_shapes=[
             pltpu.VMEM((count * LANES, width), jnp.bfloat16),
             pltpu.VMEM((count, 2, fine, LANES, LANES), jnp.float32),
-            pltpu.SemaphoreType.DMA((count, fine)),
+            pltpu.SemaphoreType.DMA((count, 2)),
         ],
         input_output_aliases={} if first else {len(operands) - 1: 0},
         compiler_params=pltpu.CompilerParams(vmem_limit_bytes=24 * 1024 * 1024),

time: 141 us -> 139 us (0.986)
  Pallas kernels: 42.3 us -> 36.9 us
  waiting for transfers between devices: 33.5 us -> 36.7 us
    pallas_call x7, Pallas kernels: 39.5 us -> 34.1 us  [correlate(): pl.pallas_call(kernel, in_specs=[pl.BlockSpec(memory_space=pltpu.SMEM)] +...]
    ppermute x14, waiting for transfers between devices: 33.3 us -> 36.5 us  [moved(): lax.ppermute(value, axis, [(s, (s + steps) % count) for s in range(count)])]
  transfers between devices with their start and end apart: 20 -> 20, of which waited for: 9 -> 9; matrix products, arithmetic and copies ran while one was open for 1% -> 1% of each run, Pallas kernels for 24% -> 21%
where the time goes in v4:
time: 139 us; the launch traced here: 138 us
  starting transfers between devices  42.1 us (30%)
  Pallas kernels  36.9 us (27%)
  waiting for transfers between devices  36.7 us (26%)
  blocking collectives  15 us (11%)
  local copies, waits for them, and re-layouts  5.14 us (4%)
  other arithmetic  1.46 us (1%)
    ppermute x14, waiting for transfers between devices, moved(): lax.ppermute(value, axis, [(s, (s + steps) % count) for s in range(count)])  36.5 us
    pallas_call x7, Pallas kernels, correlate(): pl.pallas_call(kernel, in_specs=[pl.BlockSpec(memory_space=pltpu.SMEM)] +...  34.1 us
    ppermute x14, starting transfers between devices, moved(): lax.ppermute(value, axis, [(s, (s + steps) % count) for s in range(count)])  32.5 us
    all_to_all x1, blocking collectives, shards(): lax.all_to_all(outgoing, 'chan', split_axis=0, concat_axis=0, tiled=True)  15 us
    ppermute x3, starting transfers between devices, down_x(): return lax.ppermute(value, ('x', 'y'), pairs)  3.88 us
    ppermute x1, starting transfers between devices, shards(): own_far = lax.ppermute(after(own_down, token), 'y', [(3, 0), (0, 1)])  3.17 us
    unnamed x8, local copies, waits for them, and re-layouts  3 us
    pallas_call x1, Pallas kernels, channelize(): pl.pallas_call(kernel, out_shape=jax.ShapeDtypeStruct((groups, cap, row_w...  2.81 us
  transfers between devices with their start and end apart: 20, of which 9 were waited for; matrix products, arithmetic and copies ran while one was open for 1% of the time, Pallas kernels for 21%

profile of v4, /device:TPU:0, one launch (start us, length us, event | category | flops | bytes accessed | tf_op | source)
XLA Modules:
  0.0 137.9 jit_solution(1276131306860083018)
XLA Ops:
  4.9 2.8 %channelize.1 = bf16[4,24,4224]{2,1,0:T(8,128)(2,1)S(1)} custom-call(bf16[128,4336]{1,0:T(8,128)(2,1)S(1)} %reshape.6.refs_0_, s32[1,4,24]{2,1,0:T(4,128)S(1)} %copy-done.1, s32[2,32]{1,0:T(2,128)S(1)} %bitcast.26, f32[16,16]{1,0:T(8,128)S(1)} %copy-done, f32[2,256,128]{2,1,0:T(8,128)S(1)} %copy-done.3), custom_call_target="tpu_custom_call" | custom-call | flops 4000000000 | bytes 3000000 | tf_op jit(solution)/shard_map/channelize/pallas_call | solution.py:138
  7.7 15.0 %all_to_all.5 = bf16[4,24,4224]{2,1,0:T(8,128)(2,1)S(1)} all-to-all(bf16[4,24,4224]{2,1,0:T(8,128)(2,1)S(1)} %channelize.1), channel_id=1, replica_groups=mesh['chan'=4,'x'=4,'zh'=2,'y'=4] {'chan'}, dimensions={0} | all-to-all | bytes 1622016 | tf_op jit(solution)/shard_map/all_to_all | solution.py:283
  22.7 3.6 %collective-permute-start.6 = (bf16[96,4224]{1,0:T(8,128)(2,1)S(1)}, bf16[96,4224]{1,0:T(8,128)(2,1)}, u32[]{:S(2)}, u32[]{:S(2)}) collective-permute-start(bf16[96,4224]{1,0:T(8,128)(2,1)S(1)} %bitcast.21), channel_id=1, source_target_pairs={{0,4},{4,0},{1,5},{5,1},{2,6},{6,2},{3,7},{7,3},{8,12},{12,8},{9,1... | collective-permute-start | bytes 2433032 | tf_op jit(solution)/shard_map/ppermute | solution.py:262
  26.3 2.8 %collective-permute-start = (bf16[96,4224]{1,0:T(8,128)(2,1)S(1)}, bf16[96,4224]{1,0:T(8,128)(2,1)}, u32[]{:S(2)}, u32[]{:S(2)}) collective-permute-start(bf16[96,4224]{1,0:T(8,128)(2,1)S(1)} %bitcast.22), channel_id=1, source_target_pairs={{0,24},{8,0},{16,8},{24,16},{1,25},{9,1},{17,9},{25,17},{2,26},{10... | collective-permute-start | bytes 2433032 | tf_op jit(solution)/shard_map/ppermute | solution.py:262
  31.7 2.5 %own_block.1 = (f32[2,8,128,2176]{3,2,1,0:T(8,128)}, bf16[128,4096]{1,0:T(8,128)(2,1)S(1)}) custom-call(s32[2]{0:T(128)S(1)} %broadcast_3_refs_0_.2.refs_0_, bf16[96,4224]{1,0:T(8,128)(2,1)S(1)} %bitcast.25), custom_call_target="tpu_custom_call" | custom-call | flops 100000000 | bytes 100000 | tf_op jit(solution)/shard_map/own_block/pallas_call | solution.py:241
  34.2 10.4 %collective-permute-done.6 = bf16[96,4224]{1,0:T(8,128)(2,1)} collective-permute-done((bf16[96,4224]{1,0:T(8,128)(2,1)S(1)}, bf16[96,4224]{1,0:T(8,128)(2,1)}, u32[]{:S(2)}, u32[]{:S(2)}) %collective-permute-start.6) | collective-permute-done | bytes 811040 | tf_op jit(solution)/shard_map/ppermute | solution.py:262
  44.6 3.0 %collective-permute-start.7 = (bf16[96,4224]{1,0:T(8,128)(2,1)}, bf16[96,4224]{1,0:T(8,128)(2,1)}, u32[]{:S(2)}, u32[]{:S(2)}) collective-permute-start(bf16[96,4224]{1,0:T(8,128)(2,1)} %collective-permute-done.6), channel_id=1, source_target_pairs={{0,16},{8,24},{16,0},{24,8},{1,17},{9,25},{17,1},{25,9},{2,18},{10... | collective-permute-start | bytes 2433032 | tf_op jit(solution)/shard_map/ppermute | solution.py:262
  47.7 3.3 %collective-permute-start.11 = (bf16[96,4224]{1,0:T(8,128)(2,1)}, bf16[96,4224]{1,0:T(8,128)(2,1)}, u32[]{:S(2)}, u32[]{:S(2)}) collective-permute-start(bf16[96,4224]{1,0:T(8,128)(2,1)} %collective-permute-done.refs_2_), channel_id=1, source_target_pairs={{0,4},{4,0},{1,5},{5,1},{2,6},{6,2},{3,7},{7,3},{8,12},{12,8},{9,1... | collective-permute-start | bytes 2433032 | tf_op jit(solution)/shard_map/ppermute | solution.py:262
  54.5 3.8 %pair_blocks.6 = (f32[2,8,128,2176]{3,2,1,0:T(8,128)}, f32[8,128]{1,0:T(8,128)}) custom-call(s32[2]{0:T(128)S(1)} %pad_add_fusion.1.refs_0_, bf16[128,4096]{1,0:T(8,128)(2,1)S(1)} %get-tuple-element.30.refs_1_, bf16[96,4224]{1,0:T(8,128)(2,1)} %collective-permute-done.refs_2_, ...), custom_call_target="tpu_custom_call", output_to_operand_aliasing={{0}: (3, {})} | custom-call | flops 100000000 | bytes 100000 | tf_op jit(solution)/shard_map/pair_blocks/pallas_call | solution.py:241
  58.3 7.6 %collective-permute-done.7 = bf16[96,4224]{1,0:T(8,128)(2,1)} collective-permute-done((bf16[96,4224]{1,0:T(8,128)(2,1)}, bf16[96,4224]{1,0:T(8,128)(2,1)}, u32[]{:S(2)}, u32[]{:S(2)}) %collective-permute-start.7) | collective-permute-done | bytes 811040 | tf_op jit(solution)/shard_map/ppermute | solution.py:262
  68.7 2.3 %collective-permute-done.1.refs_2_ = bf16[96,4224]{1,0:T(8,128)(2,1)S(1)} collective-permute-done((bf16[96,4224]{1,0:T(8,128)(2,1)}, bf16[96,4224]{1,0:T(8,128)(2,1)S(1)}, u32[]{:S(2)}, u32[]{:S(2)}) %collective-permute-start.1) | collective-permute-done | bytes 811040 | tf_op jit(solution)/shard_map/ppermute | solution.py:262
  71.0 2.9 %collective-permute-start.9 = (bf16[96,4224]{1,0:T(8,128)(2,1)S(1)}, bf16[96,4224]{1,0:T(8,128)(2,1)}, u32[]{:S(2)}, u32[]{:S(2)}) collective-permute-start(bf16[96,4224]{1,0:T(8,128)(2,1)S(1)} %collective-permute-done.1.refs_2_), channel_id=1, source_target_pairs={{0,3},{1,0},{2,1},{3,2},{4,7},{5,4},{6,5},{7,6},{8,11},{9,8},{10,9... | collective-permute-start | bytes 2433032 | tf_op jit(solution)/shard_map/ppermute | solution.py:262
  76.3 6.1 %pair_blocks.7 = (f32[2,8,128,2176]{3,2,1,0:T(8,128)}, f32[8,128]{1,0:T(8,128)}) custom-call(s32[8]{0:T(128)S(1)} %stack.104.refs_0_, bf16[128,4096]{1,0:T(8,128)(2,1)S(1)} %get-tuple-element.30.refs_1_, bf16[96,4224]{1,0:T(8,128)(2,1)S(1)} %collective-permute-done.1.refs_2_, ...), custom_call_target="tpu_custom_call", output_to_operand_aliasing={{0}: (6, {})} | custom-call | flops 400000000 | bytes 400000 | tf_op jit(solution)/shard_map/pair_blocks/pallas_call | solution.py:241
  82.4 3.7 %collective-permute-start.17 = (bf16[96,4224]{1,0:T(8,128)(2,1)S(1)}, bf16[96,4224]{1,0:T(8,128)(2,1)}, u32[]{:S(2)}, u32[]{:S(2)}) collective-permute-start(bf16[96,4224]{1,0:T(8,128)(2,1)S(1)} %broadcast_select_fusion.refs_5_), channel_id=1, source_target_pairs={{0,3},{1,0},{2,1},{3,2},{4,7},{5,4},{6,5},{7,6},{8,11},{9,8},{10,9... | collective-permute-start | bytes 2433032 | tf_op jit(solution)/shard_map/ppermute | solution.py:262
  86.1 2.9 %collective-permute-done.8.refs_4_ = bf16[96,4224]{1,0:T(8,128)(2,1)} collective-permute-done((bf16[96,4224]{1,0:T(8,128)(2,1)S(1)}, bf16[96,4224]{1,0:T(8,128)(2,1)}, u32[]{:S(2)}, u32[]{:S(2)}) %collective-permute-start.8) | collective-permute-done | bytes 811040 | tf_op jit(solution)/shard_map/ppermute | solution.py:262
  88.9 3.6 %collective-permute-done.9.refs_5_ = bf16[96,4224]{1,0:T(8,128)(2,1)} collective-permute-done((bf16[96,4224]{1,0:T(8,128)(2,1)S(1)}, bf16[96,4224]{1,0:T(8,128)(2,1)}, u32[]{:S(2)}, u32[]{:S(2)}) %collective-permute-start.9) | collective-permute-done | bytes 811040 | tf_op jit(solution)/shard_map/ppermute | solution.py:262
  95.0 6.8 %pair_blocks.8 = (f32[2,8,128,2176]{3,2,1,0:T(8,128)}, f32[8,128]{1,0:T(8,128)}) custom-call(s32[8]{0:T(128)S(1)} %stack.97.refs_0_, bf16[128,4096]{1,0:T(8,128)(2,1)S(1)} %get-tuple-element.30.refs_1_, bf16[96,4224]{1,0:T(8,128)(2,1)} %collective-permute-done.2.refs_2_, ...), custom_call_target="tpu_custom_call", output_to_operand_aliasing={{0}: (7, {})} | custom-call | flops 400000000 | bytes 400000 | tf_op jit(solution)/shard_map/pair_blocks/pallas_call | solution.py:241
  101.8 6.3 %collective-permute-start.15 = (bf16[96,4224]{1,0:T(8,128)(2,1)}, bf16[96,4224]{1,0:T(8,128)(2,1)}, u32[]{:S(2)}, u32[]{:S(2)}) collective-permute-start(bf16[96,4224]{1,0:T(8,128)(2,1)} %collective-permute-done.11.refs_4_), channel_id=1, source_target_pairs={{0,3},{1,0},{2,1},{3,2},{4,7},{5,4},{6,5},{7,6},{8,11},{9,8},{10,9... | collective-permute-start | bytes 2433032 | tf_op jit(solution)/shard_map/ppermute | solution.py:262
  111.2 3.2 %collective-permute-start.13 = (bf16[96,4224]{1,0:T(8,128)(2,1)}, bf16[96,4224]{1,0:T(8,128)(2,1)}, u32[]{:S(2)}, u32[]{:S(2)}) collective-permute-start(bf16[96,4224]{1,0:T(8,128)(2,1)} %collective-permute-done.2.refs_2_), channel_id=1, source_target_pairs={{3,0},{0,1},{7,4},{4,5},{11,8},{8,9},{15,12},{12,13},{19,16},{16,1... | collective-permute-start | bytes 2433032 | tf_op jit(solution)/shard_map/ppermute | solution.py:336
  114.8 5.8 %pair_blocks.9 = (f32[2,8,128,2176]{3,2,1,0:T(8,128)}, f32[8,128]{1,0:T(8,128)}) custom-call(s32[6]{0:T(128)S(1)} %stack.111.refs_0_, bf16[128,4096]{1,0:T(8,128)(2,1)S(1)} %get-tuple-element.30.refs_1_, bf16[96,4224]{1,0:T(8,128)(2,1)} %collective-permute-done.17.refs_2_, ...), custom_call_target="tpu_custom_call", output_to_operand_aliasing={{0}: (5, {})} | custom-call | flops 300000000 | bytes 300000 | tf_op jit(solution)/shard_map/pair_blocks/pallas_call | solution.py:241
  120.6 3.2 %collective-permute-done.15.refs_2_ = bf16[96,4224]{1,0:T(8,128)(2,1)} collective-permute-done((bf16[96,4224]{1,0:T(8,128)(2,1)}, bf16[96,4224]{1,0:T(8,128)(2,1)}, u32[]{:S(2)}, u32[]{:S(2)}) %collective-permute-start.15) | collective-permute-done | bytes 811040 | tf_op jit(solution)/shard_map/ppermute | solution.py:262
  123.9 4.7 %collective-permute-done.16.refs_3_ = bf16[96,4224]{1,0:T(8,128)(2,1)} collective-permute-done((bf16[96,4224]{1,0:T(8,128)(2,1)}, bf16[96,4224]{1,0:T(8,128)(2,1)}, u32[]{:S(2)}, u32[]{:S(2)}) %collective-permute-start.16) | collective-permute-done | bytes 811040 | tf_op jit(solution)/shard_map/ppermute | solution.py:262
  128.5 4.6 %pair_blocks.10 = (f32[2,8,128,2176]{3,2,1,0:T(8,128)}, f32[8,128]{1,0:T(8,128)}) custom-call(s32[4]{0:T(128)S(1)} %pad_add_fusion.2.refs_0_, bf16[128,4096]{1,0:T(8,128)(2,1)S(1)} %get-tuple-element.30.refs_1_, bf16[96,4224]{1,0:T(8,128)(2,1)} %collective-permute-done.15.refs_2_, ...), custom_call_target="tpu_custom_call", output_to_operand_aliasing={{0}: (4, {})} | custom-call | flops 200000000 | bytes 200000 | tf_op jit(solution)/shard_map/pair_blocks/pallas_call | solution.py:241
  133.1 4.6 %pair_blocks.11 = (f32[2,8,128,2176]{3,2,1,0:T(8,128)}, f32[8,128]{1,0:T(8,128)}) custom-call(s32[4]{0:T(128)S(1)} %pad_add_fusion.refs_0_, bf16[128,4096]{1,0:T(8,128)(2,1)S(1)} %get-tuple-element.30.refs_1_, bf16[96,4224]{1,0:T(8,128)(2,1)S(1)} %collective-permute-done.12.refs_2_, ...), custom_call_target="tpu_custom_call", output_to_operand_aliasing={{0}: (6, {})} | custom-call | flops 200000000 | bytes 200000 | tf_op jit(solution)/shard_map/pair_blocks/pallas_call | solution.py:241
  (43 shorter events, 22.0 us)
Async XLA Ops:
  1.9 0.7 copy-start
  2.6 0.7 copy-start.1
  3.3 0.7 copy-start.2
  4.0 0.9 copy-start.3
  22.7 21.9 %collective-permute-start.6 = (bf16[96,4224]{1,0:T(8,128)(2,1)S(1)}, bf16[96,4224]{1,0:T(8,128)(2,1)}, u32[]{:S(2)}, u32[]{:S(2)}) collective-permute-start(bf16[96,4224]{1,0:T(8,128)(2,1)S(1)} %bitcast.21), channel_id=1, source_target_pairs={{0,4},{4,0},{1,5},{5,1},{2,6},{6,2},{3,7},{7,3},{8,12},{12,8},{9,1... | collective-permute-start | bytes 2433032 | tf_op jit(solution)/shard_map/ppermute | solution.py:262
  26.3 21.4 %collective-permute-start = (bf16[96,4224]{1,0:T(8,128)(2,1)S(1)}, bf16[96,4224]{1,0:T(8,128)(2,1)}, u32[]{:S(2)}, u32[]{:S(2)}) collective-permute-start(bf16[96,4224]{1,0:T(8,128)(2,1)S(1)} %bitcast.22), channel_id=1, source_target_pairs={{0,24},{8,0},{16,8},{24,16},{1,25},{9,1},{17,9},{25,17},{2,26},{10... | collective-permute-start | bytes 2433032 | tf_op jit(solution)/shard_map/ppermute | solution.py:262
  29.1 23.5 %collective-permute-start.4 = (bf16[96,4224]{1,0:T(8,128)(2,1)S(1)}, bf16[96,4224]{1,0:T(8,128)(2,1)S(1)}, u32[]{:S(2)}, u32[]{:S(2)}) collective-permute-start(bf16[96,4224]{1,0:T(8,128)(2,1)S(1)} %bitcast.23), channel_id=1, source_target_pairs={{1,0},{2,1},{3,2},{5,4},{6,5},{7,6},{9,8},{10,9},{11,10},{13,12},{... | collective-permute-start | bytes 2433032 | tf_op jit(solution)/shard_map/ppermute | solution.py:303
  30.3 24.1 %collective-permute-start.2 = (bf16[96,4224]{1,0:T(8,128)(2,1)S(1)}, bf16[96,4224]{1,0:T(8,128)(2,1)}, u32[]{:S(2)}, u32[]{:S(2)}) collective-permute-start(bf16[96,4224]{1,0:T(8,128)(2,1)S(1)} %bitcast.24), channel_id=1, source_target_pairs={{2,3},{3,0},{6,7},{7,4},{10,11},{11,8},{14,15},{15,12},{18,19},{19... | collective-permute-start | bytes 2433032 | tf_op jit(solution)/shard_map/ppermute | solution.py:304
  44.6 21.2 %collective-permute-start.7 = (bf16[96,4224]{1,0:T(8,128)(2,1)}, bf16[96,4224]{1,0:T(8,128)(2,1)}, u32[]{:S(2)}, u32[]{:S(2)}) collective-permute-start(bf16[96,4224]{1,0:T(8,128)(2,1)} %collective-permute-done.6), channel_id=1, source_target_pairs={{0,16},{8,24},{16,0},{24,8},{1,17},{9,25},{17,1},{25,9},{2,18},{10... | collective-permute-start | bytes 2433032 | tf_op jit(solution)/shard_map/ppermute | solution.py:262
  47.7 28.6 %collective-permute-start.11 = (bf16[96,4224]{1,0:T(8,128)(2,1)}, bf16[96,4224]{1,0:T(8,128)(2,1)}, u32[]{:S(2)}, u32[]{:S(2)}) collective-permute-start(bf16[96,4224]{1,0:T(8,128)(2,1)} %collective-permute-done.refs_2_), channel_id=1, source_target_pairs={{0,4},{4,0},{1,5},{5,1},{2,6},{6,2},{3,7},{7,3},{8,12},{12,8},{9,1... | collective-permute-start | bytes 2433032 | tf_op jit(solution)/shard_map/ppermute | solution.py:262
  51.0 23.0 %collective-permute-start.3 = (bf16[96,4224]{1,0:T(8,128)(2,1)}, bf16[96,4224]{1,0:T(8,128)(2,1)}, u32[]{:S(2)}, u32[]{:S(2)}) collective-permute-start(bf16[96,4224]{1,0:T(8,128)(2,1)} %collective-permute-done.refs_2_), channel_id=1, source_target_pairs={{0,1},{1,2},{2,3},{3,0},{4,5},{5,6},{6,7},{7,4},{8,9},{9,10},{10,1... | collective-permute-start | bytes 2433032 | tf_op jit(solution)/shard_map/ppermute | solution.py:262
  52.6 18.5 %collective-permute-start.1 = (bf16[96,4224]{1,0:T(8,128)(2,1)}, bf16[96,4224]{1,0:T(8,128)(2,1)S(1)}, u32[]{:S(2)}, u32[]{:S(2)}) collective-permute-start(bf16[96,4224]{1,0:T(8,128)(2,1)} %collective-permute-done.refs_2_), channel_id=1, source_target_pairs={{0,3},{1,0},{2,1},{3,2},{4,7},{5,4},{6,5},{7,6},{8,11},{9,8},{10,9... | collective-permute-start | bytes 2433032 | tf_op jit(solution)/shard_map/ppermute | solution.py:262
  67.1 21.8 %collective-permute-start.8 = (bf16[96,4224]{1,0:T(8,128)(2,1)S(1)}, bf16[96,4224]{1,0:T(8,128)(2,1)}, u32[]{:S(2)}, u32[]{:S(2)}) collective-permute-start(bf16[96,4224]{1,0:T(8,128)(2,1)S(1)} %broadcast_select_fusion.refs_5_), channel_id=1, source_target_pairs={{0,1},{1,2},{2,3},{3,0},{4,5},{5,6},{6,7},{7,4},{8,9},{9,10},{10,1... | collective-permute-start | bytes 2433032 | tf_op jit(solution)/shard_map/ppermute | solution.py:262
  71.0 21.5 %collective-permute-start.9 = (bf16[96,4224]{1,0:T(8,128)(2,1)S(1)}, bf16[96,4224]{1,0:T(8,128)(2,1)}, u32[]{:S(2)}, u32[]{:S(2)}) collective-permute-start(bf16[96,4224]{1,0:T(8,128)(2,1)S(1)} %collective-permute-done.1.refs_2_), channel_id=1, source_target_pairs={{0,3},{1,0},{2,1},{3,2},{4,7},{5,4},{6,5},{7,6},{8,11},{9,8},{10,9... | collective-permute-start | bytes 2433032 | tf_op jit(solution)/shard_map/ppermute | solution.py:262
  74.0 20.2 %collective-permute-start.10 = (bf16[96,4224]{1,0:T(8,128)(2,1)}, bf16[96,4224]{1,0:T(8,128)(2,1)}, u32[]{:S(2)}, u32[]{:S(2)}) collective-permute-start(bf16[96,4224]{1,0:T(8,128)(2,1)} %collective-permute-done.3.refs_3_), channel_id=1, source_target_pairs={{0,4},{4,0},{1,5},{5,1},{2,6},{6,2},{3,7},{7,3},{8,12},{12,8},{9,1... | collective-permute-start | bytes 2433032 | tf_op jit(solution)/shard_map/ppermute | solution.py:262
  74.6 20.4 %collective-permute-start.5 = (bf16[96,4224]{1,0:T(8,128)(2,1)}, bf16[96,4224]{1,0:T(8,128)(2,1)}, u32[]{:S(2)}, u32[]{:S(2)}) collective-permute-start(bf16[96,4224]{1,0:T(8,128)(2,1)} %collective-permute-done.3.refs_3_), channel_id=1, source_target_pairs={{1,25},{2,26},{3,27},{9,1},{10,2},{11,3},{17,9},{18,10},{19,11},{2... | collective-permute-start | bytes 2433032 | tf_op jit(solution)/shard_map/ppermute | solution.py:268
  82.4 27.5 %collective-permute-start.17 = (bf16[96,4224]{1,0:T(8,128)(2,1)S(1)}, bf16[96,4224]{1,0:T(8,128)(2,1)}, u32[]{:S(2)}, u32[]{:S(2)}) collective-permute-start(bf16[96,4224]{1,0:T(8,128)(2,1)S(1)} %broadcast_select_fusion.refs_5_), channel_id=1, source_target_pairs={{0,3},{1,0},{2,1},{3,2},{4,7},{5,4},{6,5},{7,6},{8,11},{9,8},{10,9... | collective-permute-start | bytes 2433032 | tf_op jit(solution)/shard_map/ppermute | solution.py:262
  88.9 21.6 %collective-permute-start.18 = (bf16[96,4224]{1,0:T(8,128)(2,1)}, bf16[96,4224]{1,0:T(8,128)(2,1)}, u32[]{:S(2)}, u32[]{:S(2)}) collective-permute-start(bf16[96,4224]{1,0:T(8,128)(2,1)} %collective-permute-done.8.refs_4_), channel_id=1, source_target_pairs={{0,1},{1,2},{2,3},{3,0},{4,5},{5,6},{6,7},{7,4},{8,9},{9,10},{10,1... | collective-permute-start | bytes 2433032 | tf_op jit(solution)/shard_map/ppermute | solution.py:262
  92.5 18.7 %collective-permute-start.14 = (bf16[96,4224]{1,0:T(8,128)(2,1)}, bf16[96,4224]{1,0:T(8,128)(2,1)}, u32[]{:S(2)}, u32[]{:S(2)}) collective-permute-start(bf16[96,4224]{1,0:T(8,128)(2,1)} %collective-permute-done.9.refs_5_), channel_id=1, source_target_pairs={{2,26},{3,27},{10,2},{11,3},{18,10},{19,11},{26,18},{27,19},{6,30}... | collective-permute-start | bytes 2433032 | tf_op jit(solution)/shard_map/ppermute | solution.py:268
  94.1 20.7 %collective-permute-start.19 = (bf16[96,4224]{1,0:T(8,128)(2,1)}, bf16[96,4224]{1,0:T(8,128)(2,1)}, u32[]{:S(2)}, u32[]{:S(2)}) collective-permute-start(bf16[96,4224]{1,0:T(8,128)(2,1)} %collective-permute-done.9.refs_5_), channel_id=1, source_target_pairs={{0,4},{4,0},{1,5},{5,1},{2,6},{6,2},{3,7},{7,3},{8,12},{12,8},{9,1... | collective-permute-start | bytes 2433032 | tf_op jit(solution)/shard_map/ppermute | solution.py:262
  101.8 22.1 %collective-permute-start.15 = (bf16[96,4224]{1,0:T(8,128)(2,1)}, bf16[96,4224]{1,0:T(8,128)(2,1)}, u32[]{:S(2)}, u32[]{:S(2)}) collective-permute-start(bf16[96,4224]{1,0:T(8,128)(2,1)} %collective-permute-done.11.refs_4_), channel_id=1, source_target_pairs={{0,3},{1,0},{2,1},{3,2},{4,7},{5,4},{6,5},{7,6},{8,11},{9,8},{10,9... | collective-permute-start | bytes 2433032 | tf_op jit(solution)/shard_map/ppermute | solution.py:262
  109.9 18.6 %collective-permute-start.16 = (bf16[96,4224]{1,0:T(8,128)(2,1)}, bf16[96,4224]{1,0:T(8,128)(2,1)}, u32[]{:S(2)}, u32[]{:S(2)}) collective-permute-start(bf16[96,4224]{1,0:T(8,128)(2,1)} %collective-permute-done.7), channel_id=1, source_target_pairs={{0,4},{4,0},{1,5},{5,1},{2,6},{6,2},{3,7},{7,3},{8,12},{12,8},{9,1... | collective-permute-start | bytes 2433032 | tf_op jit(solution)/shard_map/ppermute | solution.py:262
  110.5 22.6 %collective-permute-start.12 = (bf16[96,4224]{1,0:T(8,128)(2,1)S(1)}, bf16[96,4224]{1,0:T(8,128)(2,1)S(1)}, u32[]{:S(2)}, u32[]{:S(2)}) collective-permute-start(bf16[96,4224]{1,0:T(8,128)(2,1)S(1)} %collective-permute-done.1.refs_2_), channel_id=1, source_target_pairs={{3,27},{11,3},{19,11},{27,19},{7,31},{15,7},{23,15},{31,23},{35,59... | collective-permute-start | bytes 2433032 | tf_op jit(solution)/shard_map/ppermute | solution.py:268
  111.2 21.9 %collective-permute-start.13 = (bf16[96,4224]{1,0:T(8,128)(2,1)}, bf16[96,4224]{1,0:T(8,128)(2,1)}, u32[]{:S(2)}, u32[]{:S(2)}) collective-permute-start(bf16[96,4224]{1,0:T(8,128)(2,1)} %collective-permute-done.2.refs_2_), channel_id=1, source_target_pairs={{3,0},{0,1},{7,4},{4,5},{11,8},{8,9},{15,12},{12,13},{19,16},{16,1... | collective-permute-start | bytes 2433032 | tf_op jit(solution)/shard_map/ppermute | solution.py:336

commit v5 on v4

--- a/solution.py
+++ b/solution.py
@@ -2,7 +2,6 @@
 
 import jax
 import jax.numpy as jnp
-import numpy as np
 from jax import lax
 from jax.experimental import pallas as pl
 from jax.experimental.pallas import tpu as pltpu
@@ -17,36 +16,34 @@
 UNUSED = 512
 
 
-def trig_table():
-    table = np.zeros((2, 2, LANES, 8, 2, STEP), np.float64)
-    point = np.arange(LANES) % FFT
-    for half in range(2):
-        for fine in range(8):
-            angle = 2.0 * math.pi * ((8 * half + fine) * point % FFT) / FFT
-            cosine, sine = np.cos(angle)[:, None], np.sin(angle)[:, None]
-            table[half, 0, :, fine, 0] = cosine
-            table[half, 0, :, fine, 1] = -sine
-            table[half, 1, :, fine, 0] = sine
-            table[half, 1, :, fine, 1] = cosine
-    return table.reshape(2, 2 * LANES, LANES).astype(np.float32)
-
-
-def channelize_kernel(spectra_len, cap, volt, lists_far, counts_far, taps_far, trig_far, out, *scratch):
-    lists, counts, taps, trig, sems, square, frames, weights = scratch
-    fars, nears = (lists_far, counts_far, taps_far, trig_far), (lists, counts, taps, trig)
-    copies = [pltpu.make_async_copy(f, n, sems.at[i]) for i, (f, n) in enumerate(zip(fars, nears))]
-    for copy in copies:
-        copy.start()
-    for copy in copies:
-        copy.wait()
+def trig_factors(half):
+    shape = (2 * LANES, LANES)
+    row = lax.broadcasted_iota(jnp.int32, shape, 0)
+    lane = lax.broadcasted_iota(jnp.int32, shape, 1)
+    part_in, part_out = row // LANES, lane // STEP % 2
+    turn = (8 * half + lane // (2 * STEP)) * (row % FFT) + 4 * (part_out - part_in) + FFT
+    turn = turn % FFT
+    turn = jnp.minimum(turn, FFT - turn)
+    value = jnp.full(shape, 1.0, jnp.float32)
+    for step in range(1, FFT // 2 + 1):
+        cosine = 0.0 if 4 * step == FFT else math.cos(2.0 * math.pi * step / FFT)
+        value = jnp.where(turn == step, jnp.float32(cosine), value)
+    return value
+
+
+def channelize_kernel(spectra_len, cap, volt, small, out, square, frames, weights):
+    groups, coarse, in_count = 4, 2, volt.shape[0] // 4
+    lists = small[0:groups, 0:cap]
+    counts = small[groups : groups + coarse, 0:in_count]
+    taps = small[groups + coarse : groups + coarse + TAPS, 0:FFT]
+    trig = [trig_factors(half) for half in range(2)]
     samples = volt.shape[1]
-    in_count = counts.shape[1]
     tiles = -(-samples // LANES)
     listed = 2 * cap
     point_row = lax.broadcasted_iota(jnp.int32, (LANES, LANES), 0) // FFT
     spec_lane = lax.broadcasted_iota(jnp.int32, (LANES, LANES), 1) % STEP
     lag = point_row - spec_lane
-    by_row = jnp.concatenate([taps[...]] * (LANES // FFT), axis=1).T
+    by_row = jnp.concatenate([taps] * (LANES // FFT), axis=1).T
     column = [jnp.broadcast_to(by_row[:, m : m + 1], (LANES, LANES)) for m in range(TAPS)]
     for part in range(3):
         shaped = jnp.zeros((LANES, LANES), jnp.float32)
@@ -60,10 +57,10 @@
             weights[half, part, :, 0:LANES] = high
             weights[half, part, :, LANES : 2 * LANES] = low
     square[...] = jnp.zeros(square.shape, square.dtype)
-    square[0:4, 0:cap] = lists[0].astype(jnp.float32)
+    square[0:4, 0:cap] = lists
     by_slot = square[...].T
     entry = [by_slot[0:cap, g : g + 1].astype(jnp.int32) for g in range(4)]
-    gains = jnp.sqrt(samples / (FFT * counts[...].astype(jnp.float32)))
+    gains = jnp.sqrt(samples / (FFT * counts))
     inputs = lax.broadcasted_iota(jnp.int32, (cap, in_count), 1)
     lanes = lax.broadcasted_iota(jnp.int32, (cap, LANES), 1)
     picks = []
@@ -129,6 +126,8 @@
     in_count, coarse, _, samples = voltages.shape
     groups, cap = keep_list.shape[1:]
     volt = voltages.reshape(in_count * coarse * 2, samples)
+    parts = (keep_list[0].astype(jnp.float32), sample_counts.T.astype(jnp.float32), filter_taps)
+    small = jnp.concatenate([jnp.pad(p, ((0, 0), (0, LANES - p.shape[1]))) for p in parts], axis=0)
     row_width = 8 * 2 * spectra_len + LANES
     tiles = -(-samples // LANES)
 
@@ -138,13 +137,7 @@
     return pl.pallas_call(
         kernel,
         out_shape=jax.ShapeDtypeStruct((groups, cap, row_width), jnp.bfloat16),
-        in_specs=[pl.BlockSpec(memory_space=pltpu.VMEM)] + [pl.BlockSpec(memory_space=pl.ANY)] * 4,
         scratch_shapes=[
-            pltpu.VMEM(keep_list.shape, jnp.int32),
-            pltpu.VMEM((coarse, in_count), jnp.int32),
-            pltpu.VMEM(filter_taps.shape, jnp.float32),
-            pltpu.VMEM((2, 2 * LANES, LANES), jnp.float32),
-            pltpu.SemaphoreType.DMA((4,)),
             pltpu.VMEM((LANES, LANES), jnp.float32),
             pltpu.VMEM((2, tiles * 2 * cap, 2 * LANES), jnp.bfloat16),
             pltpu.VMEM((2, 3, 2 * LANES, 2 * LANES), jnp.bfloat16),
@@ -152,7 +145,7 @@
         compiler_params=pltpu.CompilerParams(vmem_limit_bytes=32 * 1024 * 1024),
         cost_estimate=pl.CostEstimate(flops=4 * 10**9, bytes_accessed=3 * 10**6, transcendentals=0),
         name="channelize",
-    )(volt, keep_list, sample_counts.T, filter_taps, trig_table())
+    )(volt, small)
 
 
 def row_places(block, in_count, cap, width):

time: 139 us -> 138 us (level)
  local copies, waits for them, and re-layouts: 5.14 us -> 2.14 us
  other arithmetic: 1.46 us -> 3.53 us
    unnamed x8 -> x0, local copies, waits for them, and re-layouts: 3 us -> none
  transfers between devices with their start and end apart: 20 -> 20, of which waited for: 9 -> 9; matrix products, arithmetic and copies ran while one was open for 1% -> 1% of each run, Pallas kernels for 21% -> 22%
where the time goes in v5:
time: 138 us; the launch traced here: 137 us
  starting transfers between devices  42.1 us (31%)
  Pallas kernels  36.9 us (27%)
  waiting for transfers between devices  36.7 us (27%)
  blocking collectives  15 us (11%)
  other arithmetic  3.53 us (3%)
  local copies, waits for them, and re-layouts  2.14 us (2%)
    ppermute x14, waiting for transfers between devices, moved(): lax.ppermute(value, axis, [(s, (s + steps) % count) for s in range(count)])  36.5 us
    pallas_call x7, Pallas kernels, correlate(): pl.pallas_call(kernel, in_specs=[pl.BlockSpec(memory_space=pltpu.SMEM)] +...  34.1 us
    ppermute x14, starting transfers between devices, moved(): lax.ppermute(value, axis, [(s, (s + steps) % count) for s in range(count)])  32.5 us
    all_to_all x1, blocking collectives, shards(): lax.all_to_all(outgoing, 'chan', split_axis=0, concat_axis=0, tiled=True)  15 us
    ppermute x3, starting transfers between devices, down_x(): return lax.ppermute(value, ('x', 'y'), pairs)  3.88 us
    ppermute x1, starting transfers between devices, shards(): own_far = lax.ppermute(after(own_down, token), 'y', [(3, 0), (0, 1)])  3.17 us
    pallas_call x1, Pallas kernels, channelize(): pl.pallas_call(kernel, out_shape=jax.ShapeDtypeStruct((groups, cap, row_w...  2.79 us
  transfers between devices with their start and end apart: 20, of which 9 were waited for; matrix products, arithmetic and copies ran while one was open for 1% of the time, Pallas kernels for 22%

profile of v5, /device:TPU:0, one launch (start us, length us, event | category | flops | bytes accessed | tf_op | source)
XLA Modules:
  0.0 136.9 jit_solution(653229050852902463)
XLA Ops:
  4.0 2.8 %channelize.1 = bf16[4,24,4224]{2,1,0:T(8,128)(2,1)S(1)} custom-call(bf16[128,4336]{1,0:T(8,128)(2,1)S(1)} %reshape.7.refs_0_, f32[22,128]{1,0:T(8,128)S(1)} %select_maximum_fusion.refs_1_), custom_call_target="tpu_custom_call" | custom-call | flops 4000000000 | bytes 3000000 | tf_op jit(solution)/shard_map/channelize/pallas_call | solution.py:137
  6.8 15.0 %all_to_all.5 = bf16[4,24,4224]{2,1,0:T(8,128)(2,1)S(1)} all-to-all(bf16[4,24,4224]{2,1,0:T(8,128)(2,1)S(1)} %channelize.1), channel_id=1, replica_groups=mesh['chan'=4,'x'=4,'zh'=2,'y'=4] {'chan'}, dimensions={0} | all-to-all | bytes 1622016 | tf_op jit(solution)/shard_map/all_to_all | solution.py:276
  21.7 3.6 %collective-permute-start.6 = (bf16[96,4224]{1,0:T(8,128)(2,1)S(1)}, bf16[96,4224]{1,0:T(8,128)(2,1)}, u32[]{:S(2)}, u32[]{:S(2)}) collective-permute-start(bf16[96,4224]{1,0:T(8,128)(2,1)S(1)} %bitcast.24), channel_id=1, source_target_pairs={{0,4},{4,0},{1,5},{5,1},{2,6},{6,2},{3,7},{7,3},{8,12},{12,8},{9,1... | collective-permute-start | bytes 2433032 | tf_op jit(solution)/shard_map/ppermute | solution.py:255
  25.3 2.8 %collective-permute-start = (bf16[96,4224]{1,0:T(8,128)(2,1)S(1)}, bf16[96,4224]{1,0:T(8,128)(2,1)}, u32[]{:S(2)}, u32[]{:S(2)}) collective-permute-start(bf16[96,4224]{1,0:T(8,128)(2,1)S(1)} %bitcast.25), channel_id=1, source_target_pairs={{0,24},{8,0},{16,8},{24,16},{1,25},{9,1},{17,9},{25,17},{2,26},{10... | collective-permute-start | bytes 2433032 | tf_op jit(solution)/shard_map/ppermute | solution.py:255
  30.7 2.5 %own_block.1 = (f32[2,8,128,2176]{3,2,1,0:T(8,128)}, bf16[128,4096]{1,0:T(8,128)(2,1)S(1)}) custom-call(s32[2]{0:T(128)S(1)} %broadcast_3_refs_0_.2.refs_0_, bf16[96,4224]{1,0:T(8,128)(2,1)S(1)} %bitcast.28), custom_call_target="tpu_custom_call" | custom-call | flops 100000000 | bytes 100000 | tf_op jit(solution)/shard_map/own_block/pallas_call | solution.py:234
  33.2 10.4 %collective-permute-done.6 = bf16[96,4224]{1,0:T(8,128)(2,1)} collective-permute-done((bf16[96,4224]{1,0:T(8,128)(2,1)S(1)}, bf16[96,4224]{1,0:T(8,128)(2,1)}, u32[]{:S(2)}, u32[]{:S(2)}) %collective-permute-start.6) | collective-permute-done | bytes 811040 | tf_op jit(solution)/shard_map/ppermute | solution.py:255
  43.6 3.0 %collective-permute-start.7 = (bf16[96,4224]{1,0:T(8,128)(2,1)}, bf16[96,4224]{1,0:T(8,128)(2,1)}, u32[]{:S(2)}, u32[]{:S(2)}) collective-permute-start(bf16[96,4224]{1,0:T(8,128)(2,1)} %collective-permute-done.6), channel_id=1, source_target_pairs={{0,16},{8,24},{16,0},{24,8},{1,17},{9,25},{17,1},{25,9},{2,18},{10... | collective-permute-start | bytes 2433032 | tf_op jit(solution)/shard_map/ppermute | solution.py:255
  46.7 3.3 %collective-permute-start.11 = (bf16[96,4224]{1,0:T(8,128)(2,1)}, bf16[96,4224]{1,0:T(8,128)(2,1)}, u32[]{:S(2)}, u32[]{:S(2)}) collective-permute-start(bf16[96,4224]{1,0:T(8,128)(2,1)} %collective-permute-done.refs_2_), channel_id=1, source_target_pairs={{0,4},{4,0},{1,5},{5,1},{2,6},{6,2},{3,7},{7,3},{8,12},{12,8},{9,1... | collective-permute-start | bytes 2433032 | tf_op jit(solution)/shard_map/ppermute | solution.py:255
  53.5 3.8 %pair_blocks.6 = (f32[2,8,128,2176]{3,2,1,0:T(8,128)}, f32[8,128]{1,0:T(8,128)}) custom-call(s32[2]{0:T(128)S(1)} %pad_add_fusion.1.refs_0_, bf16[128,4096]{1,0:T(8,128)(2,1)S(1)} %get-tuple-element.30.refs_1_, bf16[96,4224]{1,0:T(8,128)(2,1)} %collective-permute-done.refs_2_, ...), custom_call_target="tpu_custom_call", output_to_operand_aliasing={{0}: (3, {})} | custom-call | flops 100000000 | bytes 100000 | tf_op jit(solution)/shard_map/pair_blocks/pallas_call | solution.py:234
  57.3 7.6 %collective-permute-done.7 = bf16[96,4224]{1,0:T(8,128)(2,1)} collective-permute-done((bf16[96,4224]{1,0:T(8,128)(2,1)}, bf16[96,4224]{1,0:T(8,128)(2,1)}, u32[]{:S(2)}, u32[]{:S(2)}) %collective-permute-start.7) | collective-permute-done | bytes 811040 | tf_op jit(solution)/shard_map/ppermute | solution.py:255
  67.8 2.3 %collective-permute-done.1.refs_2_ = bf16[96,4224]{1,0:T(8,128)(2,1)S(1)} collective-permute-done((bf16[96,4224]{1,0:T(8,128)(2,1)}, bf16[96,4224]{1,0:T(8,128)(2,1)S(1)}, u32[]{:S(2)}, u32[]{:S(2)}) %collective-permute-start.1) | collective-permute-done | bytes 811040 | tf_op jit(solution)/shard_map/ppermute | solution.py:255
  70.1 2.9 %collective-permute-start.9 = (bf16[96,4224]{1,0:T(8,128)(2,1)S(1)}, bf16[96,4224]{1,0:T(8,128)(2,1)}, u32[]{:S(2)}, u32[]{:S(2)}) collective-permute-start(bf16[96,4224]{1,0:T(8,128)(2,1)S(1)} %collective-permute-done.1.refs_2_), channel_id=1, source_target_pairs={{0,3},{1,0},{2,1},{3,2},{4,7},{5,4},{6,5},{7,6},{8,11},{9,8},{10,9... | collective-permute-start | bytes 2433032 | tf_op jit(solution)/shard_map/ppermute | solution.py:255
  75.3 6.1 %pair_blocks.7 = (f32[2,8,128,2176]{3,2,1,0:T(8,128)}, f32[8,128]{1,0:T(8,128)}) custom-call(s32[8]{0:T(128)S(1)} %stack.104.refs_0_, bf16[128,4096]{1,0:T(8,128)(2,1)S(1)} %get-tuple-element.30.refs_1_, bf16[96,4224]{1,0:T(8,128)(2,1)S(1)} %collective-permute-done.1.refs_2_, ...), custom_call_target="tpu_custom_call", output_to_operand_aliasing={{0}: (6, {})} | custom-call | flops 400000000 | bytes 400000 | tf_op jit(solution)/shard_map/pair_blocks/pallas_call | solution.py:234
  81.4 3.7 %collective-permute-start.17 = (bf16[96,4224]{1,0:T(8,128)(2,1)S(1)}, bf16[96,4224]{1,0:T(8,128)(2,1)}, u32[]{:S(2)}, u32[]{:S(2)}) collective-permute-start(bf16[96,4224]{1,0:T(8,128)(2,1)S(1)} %broadcast_select_fusion.refs_5_), channel_id=1, source_target_pairs={{0,3},{1,0},{2,1},{3,2},{4,7},{5,4},{6,5},{7,6},{8,11},{9,8},{10,9... | collective-permute-start | bytes 2433032 | tf_op jit(solution)/shard_map/ppermute | solution.py:255
  85.1 2.8 %collective-permute-done.8.refs_4_ = bf16[96,4224]{1,0:T(8,128)(2,1)} collective-permute-done((bf16[96,4224]{1,0:T(8,128)(2,1)S(1)}, bf16[96,4224]{1,0:T(8,128)(2,1)}, u32[]{:S(2)}, u32[]{:S(2)}) %collective-permute-start.8) | collective-permute-done | bytes 811040 | tf_op jit(solution)/shard_map/ppermute | solution.py:255
  87.9 3.6 %collective-permute-done.9.refs_5_ = bf16[96,4224]{1,0:T(8,128)(2,1)} collective-permute-done((bf16[96,4224]{1,0:T(8,128)(2,1)S(1)}, bf16[96,4224]{1,0:T(8,128)(2,1)}, u32[]{:S(2)}, u32[]{:S(2)}) %collective-permute-start.9) | collective-permute-done | bytes 811040 | tf_op jit(solution)/shard_map/ppermute | solution.py:255
  94.0 6.8 %pair_blocks.8 = (f32[2,8,128,2176]{3,2,1,0:T(8,128)}, f32[8,128]{1,0:T(8,128)}) custom-call(s32[8]{0:T(128)S(1)} %stack.97.refs_0_, bf16[128,4096]{1,0:T(8,128)(2,1)S(1)} %get-tuple-element.30.refs_1_, bf16[96,4224]{1,0:T(8,128)(2,1)} %collective-permute-done.2.refs_2_, ...), custom_call_target="tpu_custom_call", output_to_operand_aliasing={{0}: (7, {})} | custom-call | flops 400000000 | bytes 400000 | tf_op jit(solution)/shard_map/pair_blocks/pallas_call | solution.py:234
  100.8 6.3 %collective-permute-start.15 = (bf16[96,4224]{1,0:T(8,128)(2,1)}, bf16[96,4224]{1,0:T(8,128)(2,1)}, u32[]{:S(2)}, u32[]{:S(2)}) collective-permute-start(bf16[96,4224]{1,0:T(8,128)(2,1)} %collective-permute-done.11.refs_4_), channel_id=1, source_target_pairs={{0,3},{1,0},{2,1},{3,2},{4,7},{5,4},{6,5},{7,6},{8,11},{9,8},{10,9... | collective-permute-start | bytes 2433032 | tf_op jit(solution)/shard_map/ppermute | solution.py:255
  110.2 3.2 %collective-permute-start.13 = (bf16[96,4224]{1,0:T(8,128)(2,1)}, bf16[96,4224]{1,0:T(8,128)(2,1)}, u32[]{:S(2)}, u32[]{:S(2)}) collective-permute-start(bf16[96,4224]{1,0:T(8,128)(2,1)} %collective-permute-done.2.refs_2_), channel_id=1, source_target_pairs={{3,0},{0,1},{7,4},{4,5},{11,8},{8,9},{15,12},{12,13},{19,16},{16,1... | collective-permute-start | bytes 2433032 | tf_op jit(solution)/shard_map/ppermute | solution.py:329
  113.9 5.8 %pair_blocks.9 = (f32[2,8,128,2176]{3,2,1,0:T(8,128)}, f32[8,128]{1,0:T(8,128)}) custom-call(s32[6]{0:T(128)S(1)} %stack.111.refs_0_, bf16[128,4096]{1,0:T(8,128)(2,1)S(1)} %get-tuple-element.30.refs_1_, bf16[96,4224]{1,0:T(8,128)(2,1)} %collective-permute-done.17.refs_2_, ...), custom_call_target="tpu_custom_call", output_to_operand_aliasing={{0}: (5, {})} | custom-call | flops 300000000 | bytes 300000 | tf_op jit(solution)/shard_map/pair_blocks/pallas_call | solution.py:234
  119.7 3.2 %collective-permute-done.15.refs_2_ = bf16[96,4224]{1,0:T(8,128)(2,1)} collective-permute-done((bf16[96,4224]{1,0:T(8,128)(2,1)}, bf16[96,4224]{1,0:T(8,128)(2,1)}, u32[]{:S(2)}, u32[]{:S(2)}) %collective-permute-start.15) | collective-permute-done | bytes 811040 | tf_op jit(solution)/shard_map/ppermute | solution.py:255
  122.9 4.7 %collective-permute-done.16.refs_3_ = bf16[96,4224]{1,0:T(8,128)(2,1)} collective-permute-done((bf16[96,4224]{1,0:T(8,128)(2,1)}, bf16[96,4224]{1,0:T(8,128)(2,1)}, u32[]{:S(2)}, u32[]{:S(2)}) %collective-permute-start.16) | collective-permute-done | bytes 811040 | tf_op jit(solution)/shard_map/ppermute | solution.py:255
  127.6 4.6 %pair_blocks.10 = (f32[2,8,128,2176]{3,2,1,0:T(8,128)}, f32[8,128]{1,0:T(8,128)}) custom-call(s32[4]{0:T(128)S(1)} %pad_add_fusion.2.refs_0_, bf16[128,4096]{1,0:T(8,128)(2,1)S(1)} %get-tuple-element.30.refs_1_, bf16[96,4224]{1,0:T(8,128)(2,1)} %collective-permute-done.15.refs_2_, ...), custom_call_target="tpu_custom_call", output_to_operand_aliasing={{0}: (4, {})} | custom-call | flops 200000000 | bytes 200000 | tf_op jit(solution)/shard_map/pair_blocks/pallas_call | solution.py:234
  132.2 4.6 %pair_blocks.11 = (f32[2,8,128,2176]{3,2,1,0:T(8,128)}, f32[8,128]{1,0:T(8,128)}) custom-call(s32[4]{0:T(128)S(1)} %pad_add_fusion.refs_0_, bf16[128,4096]{1,0:T(8,128)(2,1)S(1)} %get-tuple-element.30.refs_1_, bf16[96,4224]{1,0:T(8,128)(2,1)S(1)} %collective-permute-done.12.refs_2_, ...), custom_call_target="tpu_custom_call", output_to_operand_aliasing={{0}: (6, {})} | custom-call | flops 200000000 | bytes 200000 | tf_op jit(solution)/shard_map/pair_blocks/pallas_call | solution.py:234
  (38 shorter events, 21.1 us)
Async XLA Ops:
  21.7 21.9 %collective-permute-start.6 = (bf16[96,4224]{1,0:T(8,128)(2,1)S(1)}, bf16[96,4224]{1,0:T(8,128)(2,1)}, u32[]{:S(2)}, u32[]{:S(2)}) collective-permute-start(bf16[96,4224]{1,0:T(8,128)(2,1)S(1)} %bitcast.24), channel_id=1, source_target_pairs={{0,4},{4,0},{1,5},{5,1},{2,6},{6,2},{3,7},{7,3},{8,12},{12,8},{9,1... | collective-permute-start | bytes 2433032 | tf_op jit(solution)/shard_map/ppermute | solution.py:255
  25.3 21.4 %collective-permute-start = (bf16[96,4224]{1,0:T(8,128)(2,1)S(1)}, bf16[96,4224]{1,0:T(8,128)(2,1)}, u32[]{:S(2)}, u32[]{:S(2)}) collective-permute-start(bf16[96,4224]{1,0:T(8,128)(2,1)S(1)} %bitcast.25), channel_id=1, source_target_pairs={{0,24},{8,0},{16,8},{24,16},{1,25},{9,1},{17,9},{25,17},{2,26},{10... | collective-permute-start | bytes 2433032 | tf_op jit(solution)/shard_map/ppermute | solution.py:255
  28.1 23.5 %collective-permute-start.4 = (bf16[96,4224]{1,0:T(8,128)(2,1)S(1)}, bf16[96,4224]{1,0:T(8,128)(2,1)S(1)}, u32[]{:S(2)}, u32[]{:S(2)}) collective-permute-start(bf16[96,4224]{1,0:T(8,128)(2,1)S(1)} %bitcast.26), channel_id=1, source_target_pairs={{1,0},{2,1},{3,2},{5,4},{6,5},{7,6},{9,8},{10,9},{11,10},{13,12},{... | collective-permute-start | bytes 2433032 | tf_op jit(solution)/shard_map/ppermute | solution.py:296
  29.4 24.1 %collective-permute-start.2 = (bf16[96,4224]{1,0:T(8,128)(2,1)S(1)}, bf16[96,4224]{1,0:T(8,128)(2,1)}, u32[]{:S(2)}, u32[]{:S(2)}) collective-permute-start(bf16[96,4224]{1,0:T(8,128)(2,1)S(1)} %bitcast.27), channel_id=1, source_target_pairs={{2,3},{3,0},{6,7},{7,4},{10,11},{11,8},{14,15},{15,12},{18,19},{19... | collective-permute-start | bytes 2433032 | tf_op jit(solution)/shard_map/ppermute | solution.py:297
  43.6 21.2 %collective-permute-start.7 = (bf16[96,4224]{1,0:T(8,128)(2,1)}, bf16[96,4224]{1,0:T(8,128)(2,1)}, u32[]{:S(2)}, u32[]{:S(2)}) collective-permute-start(bf16[96,4224]{1,0:T(8,128)(2,1)} %collective-permute-done.6), channel_id=1, source_target_pairs={{0,16},{8,24},{16,0},{24,8},{1,17},{9,25},{17,1},{25,9},{2,18},{10... | collective-permute-start | bytes 2433032 | tf_op jit(solution)/shard_map/ppermute | solution.py:255
  46.7 28.6 %collective-permute-start.11 = (bf16[96,4224]{1,0:T(8,128)(2,1)}, bf16[96,4224]{1,0:T(8,128)(2,1)}, u32[]{:S(2)}, u32[]{:S(2)}) collective-permute-start(bf16[96,4224]{1,0:T(8,128)(2,1)} %collective-permute-done.refs_2_), channel_id=1, source_target_pairs={{0,4},{4,0},{1,5},{5,1},{2,6},{6,2},{3,7},{7,3},{8,12},{12,8},{9,1... | collective-permute-start | bytes 2433032 | tf_op jit(solution)/shard_map/ppermute | solution.py:255
  50.0 23.0 %collective-permute-start.3 = (bf16[96,4224]{1,0:T(8,128)(2,1)}, bf16[96,4224]{1,0:T(8,128)(2,1)}, u32[]{:S(2)}, u32[]{:S(2)}) collective-permute-start(bf16[96,4224]{1,0:T(8,128)(2,1)} %collective-permute-done.refs_2_), channel_id=1, source_target_pairs={{0,1},{1,2},{2,3},{3,0},{4,5},{5,6},{6,7},{7,4},{8,9},{9,10},{10,1... | collective-permute-start | bytes 2433032 | tf_op jit(solution)/shard_map/ppermute | solution.py:255
  51.6 18.5 %collective-permute-start.1 = (bf16[96,4224]{1,0:T(8,128)(2,1)}, bf16[96,4224]{1,0:T(8,128)(2,1)S(1)}, u32[]{:S(2)}, u32[]{:S(2)}) collective-permute-start(bf16[96,4224]{1,0:T(8,128)(2,1)} %collective-permute-done.refs_2_), channel_id=1, source_target_pairs={{0,3},{1,0},{2,1},{3,2},{4,7},{5,4},{6,5},{7,6},{8,11},{9,8},{10,9... | collective-permute-start | bytes 2433032 | tf_op jit(solution)/shard_map/ppermute | solution.py:255
  66.1 21.8 %collective-permute-start.8 = (bf16[96,4224]{1,0:T(8,128)(2,1)S(1)}, bf16[96,4224]{1,0:T(8,128)(2,1)}, u32[]{:S(2)}, u32[]{:S(2)}) collective-permute-start(bf16[96,4224]{1,0:T(8,128)(2,1)S(1)} %broadcast_select_fusion.refs_5_), channel_id=1, source_target_pairs={{0,1},{1,2},{2,3},{3,0},{4,5},{5,6},{6,7},{7,4},{8,9},{9,10},{10,1... | collective-permute-start | bytes 2433032 | tf_op jit(solution)/shard_map/ppermute | solution.py:255
  70.1 21.5 %collective-permute-start.9 = (bf16[96,4224]{1,0:T(8,128)(2,1)S(1)}, bf16[96,4224]{1,0:T(8,128)(2,1)}, u32[]{:S(2)}, u32[]{:S(2)}) collective-permute-start(bf16[96,4224]{1,0:T(8,128)(2,1)S(1)} %collective-permute-done.1.refs_2_), channel_id=1, source_target_pairs={{0,3},{1,0},{2,1},{3,2},{4,7},{5,4},{6,5},{7,6},{8,11},{9,8},{10,9... | collective-permute-start | bytes 2433032 | tf_op jit(solution)/shard_map/ppermute | solution.py:255
  73.0 20.2 %collective-permute-start.10 = (bf16[96,4224]{1,0:T(8,128)(2,1)}, bf16[96,4224]{1,0:T(8,128)(2,1)}, u32[]{:S(2)}, u32[]{:S(2)}) collective-permute-start(bf16[96,4224]{1,0:T(8,128)(2,1)} %collective-permute-done.3.refs_3_), channel_id=1, source_target_pairs={{0,4},{4,0},{1,5},{5,1},{2,6},{6,2},{3,7},{7,3},{8,12},{12,8},{9,1... | collective-permute-start | bytes 2433032 | tf_op jit(solution)/shard_map/ppermute | solution.py:255
  73.6 20.4 %collective-permute-start.5 = (bf16[96,4224]{1,0:T(8,128)(2,1)}, bf16[96,4224]{1,0:T(8,128)(2,1)}, u32[]{:S(2)}, u32[]{:S(2)}) collective-permute-start(bf16[96,4224]{1,0:T(8,128)(2,1)} %collective-permute-done.3.refs_3_), channel_id=1, source_target_pairs={{1,25},{2,26},{3,27},{9,1},{10,2},{11,3},{17,9},{18,10},{19,11},{2... | collective-permute-start | bytes 2433032 | tf_op jit(solution)/shard_map/ppermute | solution.py:261
  81.4 27.5 %collective-permute-start.17 = (bf16[96,4224]{1,0:T(8,128)(2,1)S(1)}, bf16[96,4224]{1,0:T(8,128)(2,1)}, u32[]{:S(2)}, u32[]{:S(2)}) collective-permute-start(bf16[96,4224]{1,0:T(8,128)(2,1)S(1)} %broadcast_select_fusion.refs_5_), channel_id=1, source_target_pairs={{0,3},{1,0},{2,1},{3,2},{4,7},{5,4},{6,5},{7,6},{8,11},{9,8},{10,9... | collective-permute-start | bytes 2433032 | tf_op jit(solution)/shard_map/ppermute | solution.py:255
  87.9 21.6 %collective-permute-start.18 = (bf16[96,4224]{1,0:T(8,128)(2,1)}, bf16[96,4224]{1,0:T(8,128)(2,1)}, u32[]{:S(2)}, u32[]{:S(2)}) collective-permute-start(bf16[96,4224]{1,0:T(8,128)(2,1)} %collective-permute-done.8.refs_4_), channel_id=1, source_target_pairs={{0,1},{1,2},{2,3},{3,0},{4,5},{5,6},{6,7},{7,4},{8,9},{9,10},{10,1... | collective-permute-start | bytes 2433032 | tf_op jit(solution)/shard_map/ppermute | solution.py:255
  91.5 18.7 %collective-permute-start.14 = (bf16[96,4224]{1,0:T(8,128)(2,1)}, bf16[96,4224]{1,0:T(8,128)(2,1)}, u32[]{:S(2)}, u32[]{:S(2)}) collective-permute-start(bf16[96,4224]{1,0:T(8,128)(2,1)} %collective-permute-done.9.refs_5_), channel_id=1, source_target_pairs={{2,26},{3,27},{10,2},{11,3},{18,10},{19,11},{26,18},{27,19},{6,30}... | collective-permute-start | bytes 2433032 | tf_op jit(solution)/shard_map/ppermute | solution.py:261
  93.2 20.7 %collective-permute-start.19 = (bf16[96,4224]{1,0:T(8,128)(2,1)}, bf16[96,4224]{1,0:T(8,128)(2,1)}, u32[]{:S(2)}, u32[]{:S(2)}) collective-permute-start(bf16[96,4224]{1,0:T(8,128)(2,1)} %collective-permute-done.9.refs_5_), channel_id=1, source_target_pairs={{0,4},{4,0},{1,5},{5,1},{2,6},{6,2},{3,7},{7,3},{8,12},{12,8},{9,1... | collective-permute-start | bytes 2433032 | tf_op jit(solution)/shard_map/ppermute | solution.py:255
  100.8 22.1 %collective-permute-start.15 = (bf16[96,4224]{1,0:T(8,128)(2,1)}, bf16[96,4224]{1,0:T(8,128)(2,1)}, u32[]{:S(2)}, u32[]{:S(2)}) collective-permute-start(bf16[96,4224]{1,0:T(8,128)(2,1)} %collective-permute-done.11.refs_4_), channel_id=1, source_target_pairs={{0,3},{1,0},{2,1},{3,2},{4,7},{5,4},{6,5},{7,6},{8,11},{9,8},{10,9... | collective-permute-start | bytes 2433032 | tf_op jit(solution)/shard_map/ppermute | solution.py:255
  108.9 18.7 %collective-permute-start.16 = (bf16[96,4224]{1,0:T(8,128)(2,1)}, bf16[96,4224]{1,0:T(8,128)(2,1)}, u32[]{:S(2)}, u32[]{:S(2)}) collective-permute-start(bf16[96,4224]{1,0:T(8,128)(2,1)} %collective-permute-done.7), channel_id=1, source_target_pairs={{0,4},{4,0},{1,5},{5,1},{2,6},{6,2},{3,7},{7,3},{8,12},{12,8},{9,1... | collective-permute-start | bytes 2433032 | tf_op jit(solution)/shard_map/ppermute | solution.py:255
  109.5 22.6 %collective-permute-start.12 = (bf16[96,4224]{1,0:T(8,128)(2,1)S(1)}, bf16[96,4224]{1,0:T(8,128)(2,1)S(1)}, u32[]{:S(2)}, u32[]{:S(2)}) collective-permute-start(bf16[96,4224]{1,0:T(8,128)(2,1)S(1)} %collective-permute-done.1.refs_2_), channel_id=1, source_target_pairs={{3,27},{11,3},{19,11},{27,19},{7,31},{15,7},{23,15},{31,23},{35,59... | collective-permute-start | bytes 2433032 | tf_op jit(solution)/shard_map/ppermute | solution.py:261
  110.2 21.9 %collective-permute-start.13 = (bf16[96,4224]{1,0:T(8,128)(2,1)}, bf16[96,4224]{1,0:T(8,128)(2,1)}, u32[]{:S(2)}, u32[]{:S(2)}) collective-permute-start(bf16[96,4224]{1,0:T(8,128)(2,1)} %collective-permute-done.2.refs_2_), channel_id=1, source_target_pairs={{3,0},{0,1},{7,4},{4,5},{11,8},{8,9},{15,12},{12,13},{19,16},{16,1... | collective-permute-start | bytes 2433032 | tf_op jit(solution)/shard_map/ppermute | solution.py:329

commit v6 on v5

--- a/solution.py
+++ b/solution.py
@@ -339,15 +339,8 @@
     result, token = correlate(
         result,
         side,
-        [onez_up, two],
-        [offset(1, flip, up), offset(2, z, y)],
-        sizes,
-    )
-    result, token = correlate(
-        result,
-        side,
-        [(y == y_count - 1, two_up, own_up), (y < 2, own_far, two_far)],
-        [near(up), near(far)],
+        [onez_up, two, (y == y_count - 1, two_up, own_up), (y < 2, own_far, two_far)],
+        [offset(1, flip, up), offset(2, z, y), near(up), near(far)],
         sizes,
     )
     return result

time: 138 us -> 137 us (level)
  starting transfers between devices: 42.1 us -> 47.1 us
  Pallas kernels: 36.9 us -> 34.3 us
  waiting for transfers between devices: 36.7 us -> 34.4 us
    ppermute x14, waiting for transfers between devices: 36.5 us -> 30.8 us  [moved(): lax.ppermute(value, axis, [(s, (s + steps) % count) for s in range(count)])]
    ppermute x14, starting transfers between devices: 32.5 us -> 36.4 us  [moved(): lax.ppermute(value, axis, [(s, (s + steps) % count) for s in range(count)])]
    ppermute x1, waiting for transfers between devices: 0.01 us -> 2.95 us  [shards(): own_far = lax.ppermute(after(own_down, token), 'y', [(3, 0), (0, 1)])]
    pallas_call x7 -> x6, Pallas kernels: 34.1 us -> 31.6 us  [correlate(): pl.pallas_call(kernel, in_specs=[pl.BlockSpec(memory_space=pltpu.SMEM)] +...]
  transfers between devices with their start and end apart: 20 -> 20, of which waited for: 9 -> 11; matrix products, arithmetic and copies ran while one was open for 1% -> 1% of each run, Pallas kernels for 22% -> 18%
where the time goes in v6:
time: 137 us
  starting transfers between devices  47.1 us (34%)
  waiting for transfers between devices  34.4 us (25%)
  Pallas kernels  34.3 us (25%)
  blocking collectives  15 us (11%)
  other arithmetic  3.38 us (2%)
  local copies, waits for them, and re-layouts  2.22 us (2%)
    ppermute x14, starting transfers between devices, moved(): lax.ppermute(value, axis, [(s, (s + steps) % count) for s in range(count)])  36.4 us
    pallas_call x6, Pallas kernels, correlate(): pl.pallas_call(kernel, in_specs=[pl.BlockSpec(memory_space=pltpu.SMEM)] +...  31.6 us
    ppermute x14, waiting for transfers between devices, moved(): lax.ppermute(value, axis, [(s, (s + steps) % count) for s in range(count)])  30.8 us
    all_to_all x1, blocking collectives, shards(): lax.all_to_all(outgoing, 'chan', split_axis=0, concat_axis=0, tiled=True)  15 us
    ppermute x3, starting transfers between devices, down_x(): return lax.ppermute(value, ('x', 'y'), pairs)  4.7 us
    ppermute x1, starting transfers between devices, shards(): own_far = lax.ppermute(after(own_down, token), 'y', [(3, 0), (0, 1)])  3.47 us
    ppermute x1, waiting for transfers between devices, shards(): own_far = lax.ppermute(after(own_down, token), 'y', [(3, 0), (0, 1)])  2.95 us
    pallas_call x1, Pallas kernels, channelize(): pl.pallas_call(kernel, out_shape=jax.ShapeDtypeStruct((groups, cap, row_w...  2.79 us
  transfers between devices with their start and end apart: 20, of which 11 were waited for; matrix products, arithmetic and copies ran while one was open for 1% of the time, Pallas kernels for 18%

profile of v6, /device:TPU:0, one launch (start us, length us, event | category | flops | bytes accessed | tf_op | source)
XLA Modules:
  0.0 136.9 jit_solution(15375723335004554587)
XLA Ops:
  4.0 2.8 %channelize.1 = bf16[4,24,4224]{2,1,0:T(8,128)(2,1)S(1)} custom-call(bf16[128,4336]{1,0:T(8,128)(2,1)S(1)} %reshape.7.refs_0_, f32[22,128]{1,0:T(8,128)S(1)} %select_maximum_fusion.refs_1_), custom_call_target="tpu_custom_call" | custom-call | flops 4000000000 | bytes 3000000 | tf_op jit(solution)/shard_map/channelize/pallas_call | solution.py:137
  6.8 15.0 %all_to_all.5 = bf16[4,24,4224]{2,1,0:T(8,128)(2,1)S(1)} all-to-all(bf16[4,24,4224]{2,1,0:T(8,128)(2,1)S(1)} %channelize.1), channel_id=1, replica_groups=mesh['chan'=4,'x'=4,'zh'=2,'y'=4] {'chan'}, dimensions={0} | all-to-all | bytes 1622016 | tf_op jit(solution)/shard_map/all_to_all | solution.py:276
  21.7 3.6 %collective-permute-start.6 = (bf16[96,4224]{1,0:T(8,128)(2,1)S(1)}, bf16[96,4224]{1,0:T(8,128)(2,1)}, u32[]{:S(2)}, u32[]{:S(2)}) collective-permute-start(bf16[96,4224]{1,0:T(8,128)(2,1)S(1)} %bitcast.24), channel_id=1, source_target_pairs={{0,4},{4,0},{1,5},{5,1},{2,6},{6,2},{3,7},{7,3},{8,12},{12,8},{9,1... | collective-permute-start | bytes 2433032 | tf_op jit(solution)/shard_map/ppermute | solution.py:255
  25.3 2.8 %collective-permute-start = (bf16[96,4224]{1,0:T(8,128)(2,1)S(1)}, bf16[96,4224]{1,0:T(8,128)(2,1)}, u32[]{:S(2)}, u32[]{:S(2)}) collective-permute-start(bf16[96,4224]{1,0:T(8,128)(2,1)S(1)} %bitcast.25), channel_id=1, source_target_pairs={{0,24},{8,0},{16,8},{24,16},{1,25},{9,1},{17,9},{25,17},{2,26},{10... | collective-permute-start | bytes 2433032 | tf_op jit(solution)/shard_map/ppermute | solution.py:255
  30.7 2.5 %own_block.1 = (f32[2,8,128,2176]{3,2,1,0:T(8,128)}, bf16[128,4096]{1,0:T(8,128)(2,1)S(1)}) custom-call(s32[2]{0:T(128)S(1)} %broadcast_3_refs_0_.2.refs_0_, bf16[96,4224]{1,0:T(8,128)(2,1)S(1)} %bitcast.28), custom_call_target="tpu_custom_call" | custom-call | flops 100000000 | bytes 100000 | tf_op jit(solution)/shard_map/own_block/pallas_call | solution.py:234
  33.2 10.4 %collective-permute-done.6 = bf16[96,4224]{1,0:T(8,128)(2,1)} collective-permute-done((bf16[96,4224]{1,0:T(8,128)(2,1)S(1)}, bf16[96,4224]{1,0:T(8,128)(2,1)}, u32[]{:S(2)}, u32[]{:S(2)}) %collective-permute-start.6) | collective-permute-done | bytes 811040 | tf_op jit(solution)/shard_map/ppermute | solution.py:255
  43.6 3.0 %collective-permute-start.7 = (bf16[96,4224]{1,0:T(8,128)(2,1)}, bf16[96,4224]{1,0:T(8,128)(2,1)}, u32[]{:S(2)}, u32[]{:S(2)}) collective-permute-start(bf16[96,4224]{1,0:T(8,128)(2,1)} %collective-permute-done.6), channel_id=1, source_target_pairs={{0,16},{8,24},{16,0},{24,8},{1,17},{9,25},{17,1},{25,9},{2,18},{10... | collective-permute-start | bytes 2433032 | tf_op jit(solution)/shard_map/ppermute | solution.py:255
  46.7 3.0 %collective-permute-start.9 = (bf16[96,4224]{1,0:T(8,128)(2,1)}, bf16[96,4224]{1,0:T(8,128)(2,1)S(1)}, u32[]{:S(2)}, u32[]{:S(2)}) collective-permute-start(bf16[96,4224]{1,0:T(8,128)(2,1)} %collective-permute-done.refs_2_), channel_id=1, source_target_pairs={{0,3},{1,0},{2,1},{3,2},{4,7},{5,4},{6,5},{7,6},{8,11},{9,8},{10,9... | collective-permute-start | bytes 2433032 | tf_op jit(solution)/shard_map/ppermute | solution.py:255
  49.9 3.1 %collective-permute-start.1 = (bf16[96,4224]{1,0:T(8,128)(2,1)}, bf16[96,4224]{1,0:T(8,128)(2,1)}, u32[]{:S(2)}, u32[]{:S(2)}) collective-permute-start(bf16[96,4224]{1,0:T(8,128)(2,1)} %collective-permute-done.refs_2_), channel_id=1, source_target_pairs={{0,4},{4,0},{1,5},{5,1},{2,6},{6,2},{3,7},{7,3},{8,12},{12,8},{9,1... | collective-permute-start | bytes 2433032 | tf_op jit(solution)/shard_map/ppermute | solution.py:255
  53.5 3.8 %pair_blocks.5 = (f32[2,8,128,2176]{3,2,1,0:T(8,128)}, f32[8,128]{1,0:T(8,128)}) custom-call(s32[2]{0:T(128)S(1)} %pad_add_fusion.refs_0_, bf16[128,4096]{1,0:T(8,128)(2,1)S(1)} %get-tuple-element.29.refs_1_, bf16[96,4224]{1,0:T(8,128)(2,1)} %collective-permute-done.refs_2_, ...), custom_call_target="tpu_custom_call", output_to_operand_aliasing={{0}: (3, {})} | custom-call | flops 100000000 | bytes 100000 | tf_op jit(solution)/shard_map/pair_blocks/pallas_call | solution.py:234
  57.3 7.6 %collective-permute-done.7 = bf16[96,4224]{1,0:T(8,128)(2,1)} collective-permute-done((bf16[96,4224]{1,0:T(8,128)(2,1)}, bf16[96,4224]{1,0:T(8,128)(2,1)}, u32[]{:S(2)}, u32[]{:S(2)}) %collective-permute-start.7) | collective-permute-done | bytes 811040 | tf_op jit(solution)/shard_map/ppermute | solution.py:255
  67.8 2.6 %collective-permute-start.10 = (bf16[96,4224]{1,0:T(8,128)(2,1)S(1)}, bf16[96,4224]{1,0:T(8,128)(2,1)}, u32[]{:S(2)}, u32[]{:S(2)}) collective-permute-start(bf16[96,4224]{1,0:T(8,128)(2,1)S(1)} %collective-permute-done.9.refs_2_), channel_id=1, source_target_pairs={{0,3},{1,0},{2,1},{3,2},{4,7},{5,4},{6,5},{7,6},{8,11},{9,8},{10,9... | collective-permute-start | bytes 2433032 | tf_op jit(solution)/shard_map/ppermute | solution.py:255
  76.5 6.1 %pair_blocks.6 = (f32[2,8,128,2176]{3,2,1,0:T(8,128)}, f32[8,128]{1,0:T(8,128)}) custom-call(s32[8]{0:T(128)S(1)} %stack.103.refs_0_, bf16[128,4096]{1,0:T(8,128)(2,1)S(1)} %get-tuple-element.29.refs_1_, bf16[96,4224]{1,0:T(8,128)(2,1)S(1)} %collective-permute-done.9.refs_2_, ...), custom_call_target="tpu_custom_call", output_to_operand_aliasing={{0}: (6, {})} | custom-call | flops 400000000 | bytes 400000 | tf_op jit(solution)/shard_map/pair_blocks/pallas_call | solution.py:234
  82.6 2.5 %collective-permute-start.17 = (bf16[96,4224]{1,0:T(8,128)(2,1)S(1)}, bf16[96,4224]{1,0:T(8,128)(2,1)}, u32[]{:S(2)}, u32[]{:S(2)}) collective-permute-start(bf16[96,4224]{1,0:T(8,128)(2,1)S(1)} %broadcast_select_fusion.refs_5_), channel_id=1, source_target_pairs={{0,3},{1,0},{2,1},{3,2},{4,7},{5,4},{6,5},{7,6},{8,11},{9,8},{10,9... | collective-permute-start | bytes 2433032 | tf_op jit(solution)/shard_map/ppermute | solution.py:255
  85.1 2.9 %collective-permute-done.8.refs_4_ = bf16[96,4224]{1,0:T(8,128)(2,1)} collective-permute-done((bf16[96,4224]{1,0:T(8,128)(2,1)S(1)}, bf16[96,4224]{1,0:T(8,128)(2,1)}, u32[]{:S(2)}, u32[]{:S(2)}) %collective-permute-start.8) | collective-permute-done | bytes 811040 | tf_op jit(solution)/shard_map/ppermute | solution.py:255
  90.7 3.0 %collective-permute-start.19 = (bf16[96,4224]{1,0:T(8,128)(2,1)}, bf16[96,4224]{1,0:T(8,128)(2,1)}, u32[]{:S(2)}, u32[]{:S(2)}) collective-permute-start(bf16[96,4224]{1,0:T(8,128)(2,1)} %collective-permute-done.10.refs_5_), channel_id=1, source_target_pairs={{0,4},{4,0},{1,5},{5,1},{2,6},{6,2},{3,7},{7,3},{8,12},{12,8},{9,1... | collective-permute-start | bytes 2433032 | tf_op jit(solution)/shard_map/ppermute | solution.py:255
  93.7 6.8 %pair_blocks.7 = (f32[2,8,128,2176]{3,2,1,0:T(8,128)}, f32[8,128]{1,0:T(8,128)}) custom-call(s32[8]{0:T(128)S(1)} %stack.96.refs_0_, bf16[128,4096]{1,0:T(8,128)(2,1)S(1)} %get-tuple-element.29.refs_1_, bf16[96,4224]{1,0:T(8,128)(2,1)} %collective-permute-done.2.refs_2_, ...), custom_call_target="tpu_custom_call", output_to_operand_aliasing={{0}: (7, {})} | custom-call | flops 400000000 | bytes 400000 | tf_op jit(solution)/shard_map/pair_blocks/pallas_call | solution.py:234
  100.5 6.2 %collective-permute-start.12 = (bf16[96,4224]{1,0:T(8,128)(2,1)}, bf16[96,4224]{1,0:T(8,128)(2,1)}, u32[]{:S(2)}, u32[]{:S(2)}) collective-permute-start(bf16[96,4224]{1,0:T(8,128)(2,1)} %collective-permute-done.1.refs_4_), channel_id=1, source_target_pairs={{0,3},{1,0},{2,1},{3,2},{4,7},{5,4},{6,5},{7,6},{8,11},{9,8},{10,9... | collective-permute-start | bytes 2433032 | tf_op jit(solution)/shard_map/ppermute | solution.py:255
  106.7 2.5 %collective-permute-start.13 = (bf16[96,4224]{1,0:T(8,128)(2,1)}, bf16[96,4224]{1,0:T(8,128)(2,1)S(1)}, u32[]{:S(2)}, u32[]{:S(2)}) collective-permute-start(bf16[96,4224]{1,0:T(8,128)(2,1)} %collective-permute-done.7), channel_id=1, source_target_pairs={{0,4},{4,0},{1,5},{5,1},{2,6},{6,2},{3,7},{7,3},{8,12},{12,8},{9,1... | collective-permute-start | bytes 2433032 | tf_op jit(solution)/shard_map/ppermute | solution.py:255
  110.8 3.5 %collective-permute-start.15 = (bf16[96,4224]{1,0:T(8,128)(2,1)}, bf16[96,4224]{1,0:T(8,128)(2,1)}, u32[]{:S(2)}, u32[]{:S(2)}) collective-permute-start(bf16[96,4224]{1,0:T(8,128)(2,1)} %collective-permute-done.2.refs_2_), channel_id=1, source_target_pairs={{3,0},{0,1},{7,4},{4,5},{11,8},{8,9},{15,12},{12,13},{19,16},{16,1... | collective-permute-start | bytes 2433032 | tf_op jit(solution)/shard_map/ppermute | solution.py:329
  114.6 5.8 %pair_blocks.8 = (f32[2,8,128,2176]{3,2,1,0:T(8,128)}, f32[8,128]{1,0:T(8,128)}) custom-call(s32[6]{0:T(128)S(1)} %stack.107.refs_0_, bf16[128,4096]{1,0:T(8,128)(2,1)S(1)} %get-tuple-element.29.refs_1_, bf16[96,4224]{1,0:T(8,128)(2,1)} %collective-permute-done.17.refs_2_, ...), custom_call_target="tpu_custom_call", output_to_operand_aliasing={{0}: (5, {})} | custom-call | flops 300000000 | bytes 300000 | tf_op jit(solution)/shard_map/pair_blocks/pallas_call | solution.py:234
  121.0 6.2 %collective-permute-done.13.refs_3_ = bf16[96,4224]{1,0:T(8,128)(2,1)S(1)} collective-permute-done((bf16[96,4224]{1,0:T(8,128)(2,1)}, bf16[96,4224]{1,0:T(8,128)(2,1)S(1)}, u32[]{:S(2)}, u32[]{:S(2)}) %collective-permute-start.13) | collective-permute-done | bytes 811040 | tf_op jit(solution)/shard_map/ppermute | solution.py:255
  127.3 3.0 %collective-permute-done.15.refs_6_ = bf16[96,4224]{1,0:T(8,128)(2,1)} collective-permute-done((bf16[96,4224]{1,0:T(8,128)(2,1)}, bf16[96,4224]{1,0:T(8,128)(2,1)}, u32[]{:S(2)}, u32[]{:S(2)}) %collective-permute-start.15) | collective-permute-done | bytes 811040 | tf_op jit(solution)/shard_map/ppermute | solution.py:329
  130.2 6.6 %pair_blocks.9 = (f32[2,8,128,2176]{3,2,1,0:T(8,128)}, f32[8,128]{1,0:T(8,128)}) custom-call(s32[8]{0:T(128)S(1)} %stack.89.refs_0_, bf16[128,4096]{1,0:T(8,128)(2,1)S(1)} %get-tuple-element.29.refs_1_, bf16[96,4224]{1,0:T(8,128)(2,1)} %collective-permute-done.12.refs_2_, ...), custom_call_target="tpu_custom_call", output_to_operand_aliasing={{0}: (8, {})} | custom-call | flops 400000000 | bytes 400000 | tf_op jit(solution)/shard_map/pair_blocks/pallas_call | solution.py:234
  (36 shorter events, 21.4 us)
Async XLA Ops:
  21.7 21.9 %collective-permute-start.6 = (bf16[96,4224]{1,0:T(8,128)(2,1)S(1)}, bf16[96,4224]{1,0:T(8,128)(2,1)}, u32[]{:S(2)}, u32[]{:S(2)}) collective-permute-start(bf16[96,4224]{1,0:T(8,128)(2,1)S(1)} %bitcast.24), channel_id=1, source_target_pairs={{0,4},{4,0},{1,5},{5,1},{2,6},{6,2},{3,7},{7,3},{8,12},{12,8},{9,1... | collective-permute-start | bytes 2433032 | tf_op jit(solution)/shard_map/ppermute | solution.py:255
  25.3 21.4 %collective-permute-start = (bf16[96,4224]{1,0:T(8,128)(2,1)S(1)}, bf16[96,4224]{1,0:T(8,128)(2,1)}, u32[]{:S(2)}, u32[]{:S(2)}) collective-permute-start(bf16[96,4224]{1,0:T(8,128)(2,1)S(1)} %bitcast.25), channel_id=1, source_target_pairs={{0,24},{8,0},{16,8},{24,16},{1,25},{9,1},{17,9},{25,17},{2,26},{10... | collective-permute-start | bytes 2433032 | tf_op jit(solution)/shard_map/ppermute | solution.py:255
  28.1 21.8 %collective-permute-start.4 = (bf16[96,4224]{1,0:T(8,128)(2,1)S(1)}, bf16[96,4224]{1,0:T(8,128)(2,1)S(1)}, u32[]{:S(2)}, u32[]{:S(2)}) collective-permute-start(bf16[96,4224]{1,0:T(8,128)(2,1)S(1)} %bitcast.26), channel_id=1, source_target_pairs={{1,0},{2,1},{3,2},{5,4},{6,5},{7,6},{9,8},{10,9},{11,10},{13,12},{... | collective-permute-start | bytes 2433032 | tf_op jit(solution)/shard_map/ppermute | solution.py:296
  29.4 24.1 %collective-permute-start.2 = (bf16[96,4224]{1,0:T(8,128)(2,1)S(1)}, bf16[96,4224]{1,0:T(8,128)(2,1)}, u32[]{:S(2)}, u32[]{:S(2)}) collective-permute-start(bf16[96,4224]{1,0:T(8,128)(2,1)S(1)} %bitcast.27), channel_id=1, source_target_pairs={{2,3},{3,0},{6,7},{7,4},{10,11},{11,8},{14,15},{15,12},{18,19},{19... | collective-permute-start | bytes 2433032 | tf_op jit(solution)/shard_map/ppermute | solution.py:297
  43.6 21.2 %collective-permute-start.7 = (bf16[96,4224]{1,0:T(8,128)(2,1)}, bf16[96,4224]{1,0:T(8,128)(2,1)}, u32[]{:S(2)}, u32[]{:S(2)}) collective-permute-start(bf16[96,4224]{1,0:T(8,128)(2,1)} %collective-permute-done.6), channel_id=1, source_target_pairs={{0,16},{8,24},{16,0},{24,8},{1,17},{9,25},{17,1},{25,9},{2,18},{10... | collective-permute-start | bytes 2433032 | tf_op jit(solution)/shard_map/ppermute | solution.py:255
  46.7 21.0 %collective-permute-start.9 = (bf16[96,4224]{1,0:T(8,128)(2,1)}, bf16[96,4224]{1,0:T(8,128)(2,1)S(1)}, u32[]{:S(2)}, u32[]{:S(2)}) collective-permute-start(bf16[96,4224]{1,0:T(8,128)(2,1)} %collective-permute-done.refs_2_), channel_id=1, source_target_pairs={{0,3},{1,0},{2,1},{3,2},{4,7},{5,4},{6,5},{7,6},{8,11},{9,8},{10,9... | collective-permute-start | bytes 2433032 | tf_op jit(solution)/shard_map/ppermute | solution.py:255
  49.8 22.5 %collective-permute-start.3 = (bf16[96,4224]{1,0:T(8,128)(2,1)}, bf16[96,4224]{1,0:T(8,128)(2,1)}, u32[]{:S(2)}, u32[]{:S(2)}) collective-permute-start(bf16[96,4224]{1,0:T(8,128)(2,1)} %collective-permute-done.refs_2_), channel_id=1, source_target_pairs={{0,1},{1,2},{2,3},{3,0},{4,5},{5,6},{6,7},{7,4},{8,9},{9,10},{10,1... | collective-permute-start | bytes 2433032 | tf_op jit(solution)/shard_map/ppermute | solution.py:255
  49.9 26.6 %collective-permute-start.1 = (bf16[96,4224]{1,0:T(8,128)(2,1)}, bf16[96,4224]{1,0:T(8,128)(2,1)}, u32[]{:S(2)}, u32[]{:S(2)}) collective-permute-start(bf16[96,4224]{1,0:T(8,128)(2,1)} %collective-permute-done.refs_2_), channel_id=1, source_target_pairs={{0,4},{4,0},{1,5},{5,1},{2,6},{6,2},{3,7},{7,3},{8,12},{12,8},{9,1... | collective-permute-start | bytes 2433032 | tf_op jit(solution)/shard_map/ppermute | solution.py:255
  66.1 21.8 %collective-permute-start.8 = (bf16[96,4224]{1,0:T(8,128)(2,1)S(1)}, bf16[96,4224]{1,0:T(8,128)(2,1)}, u32[]{:S(2)}, u32[]{:S(2)}) collective-permute-start(bf16[96,4224]{1,0:T(8,128)(2,1)S(1)} %broadcast_select_fusion.refs_5_), channel_id=1, source_target_pairs={{0,1},{1,2},{2,3},{3,0},{4,5},{5,6},{6,7},{7,4},{8,9},{9,10},{10,1... | collective-permute-start | bytes 2433032 | tf_op jit(solution)/shard_map/ppermute | solution.py:255
  67.8 21.1 %collective-permute-start.10 = (bf16[96,4224]{1,0:T(8,128)(2,1)S(1)}, bf16[96,4224]{1,0:T(8,128)(2,1)}, u32[]{:S(2)}, u32[]{:S(2)}) collective-permute-start(bf16[96,4224]{1,0:T(8,128)(2,1)S(1)} %collective-permute-done.9.refs_2_), channel_id=1, source_target_pairs={{0,3},{1,0},{2,1},{3,2},{4,7},{5,4},{6,5},{7,6},{8,11},{9,8},{10,9... | collective-permute-start | bytes 2433032 | tf_op jit(solution)/shard_map/ppermute | solution.py:255
  72.3 18.4 %collective-permute-start.11 = (bf16[96,4224]{1,0:T(8,128)(2,1)}, bf16[96,4224]{1,0:T(8,128)(2,1)}, u32[]{:S(2)}, u32[]{:S(2)}) collective-permute-start(bf16[96,4224]{1,0:T(8,128)(2,1)} %collective-permute-done.3.refs_3_), channel_id=1, source_target_pairs={{0,4},{4,0},{1,5},{5,1},{2,6},{6,2},{3,7},{7,3},{8,12},{12,8},{9,1... | collective-permute-start | bytes 2433032 | tf_op jit(solution)/shard_map/ppermute | solution.py:255
  74.8 18.9 %collective-permute-start.5 = (bf16[96,4224]{1,0:T(8,128)(2,1)}, bf16[96,4224]{1,0:T(8,128)(2,1)}, u32[]{:S(2)}, u32[]{:S(2)}) collective-permute-start(bf16[96,4224]{1,0:T(8,128)(2,1)} %collective-permute-done.3.refs_3_), channel_id=1, source_target_pairs={{1,25},{2,26},{3,27},{9,1},{10,2},{11,3},{17,9},{18,10},{19,11},{2... | collective-permute-start | bytes 2433032 | tf_op jit(solution)/shard_map/ppermute | solution.py:261
  82.6 24.1 %collective-permute-start.17 = (bf16[96,4224]{1,0:T(8,128)(2,1)S(1)}, bf16[96,4224]{1,0:T(8,128)(2,1)}, u32[]{:S(2)}, u32[]{:S(2)}) collective-permute-start(bf16[96,4224]{1,0:T(8,128)(2,1)S(1)} %broadcast_select_fusion.refs_5_), channel_id=1, source_target_pairs={{0,3},{1,0},{2,1},{3,2},{4,7},{5,4},{6,5},{7,6},{8,11},{9,8},{10,9... | collective-permute-start | bytes 2433032 | tf_op jit(solution)/shard_map/ppermute | solution.py:255
  87.9 21.3 %collective-permute-start.18 = (bf16[96,4224]{1,0:T(8,128)(2,1)}, bf16[96,4224]{1,0:T(8,128)(2,1)}, u32[]{:S(2)}, u32[]{:S(2)}) collective-permute-start(bf16[96,4224]{1,0:T(8,128)(2,1)} %collective-permute-done.8.refs_4_), channel_id=1, source_target_pairs={{0,1},{1,2},{2,3},{3,0},{4,5},{5,6},{6,7},{7,4},{8,9},{9,10},{10,1... | collective-permute-start | bytes 2433032 | tf_op jit(solution)/shard_map/ppermute | solution.py:255
  88.9 21.9 %collective-permute-start.16 = (bf16[96,4224]{1,0:T(8,128)(2,1)}, bf16[96,4224]{1,0:T(8,128)(2,1)}, u32[]{:S(2)}, u32[]{:S(2)}) collective-permute-start(bf16[96,4224]{1,0:T(8,128)(2,1)} %collective-permute-done.10.refs_5_), channel_id=1, source_target_pairs={{2,26},{3,27},{10,2},{11,3},{18,10},{19,11},{26,18},{27,19},{6,30}... | collective-permute-start | bytes 2433032 | tf_op jit(solution)/shard_map/ppermute | solution.py:261
  90.7 23.9 %collective-permute-start.19 = (bf16[96,4224]{1,0:T(8,128)(2,1)}, bf16[96,4224]{1,0:T(8,128)(2,1)}, u32[]{:S(2)}, u32[]{:S(2)}) collective-permute-start(bf16[96,4224]{1,0:T(8,128)(2,1)} %collective-permute-done.10.refs_5_), channel_id=1, source_target_pairs={{0,4},{4,0},{1,5},{5,1},{2,6},{6,2},{3,7},{7,3},{8,12},{12,8},{9,1... | collective-permute-start | bytes 2433032 | tf_op jit(solution)/shard_map/ppermute | solution.py:255
  100.5 20.5 %collective-permute-start.12 = (bf16[96,4224]{1,0:T(8,128)(2,1)}, bf16[96,4224]{1,0:T(8,128)(2,1)}, u32[]{:S(2)}, u32[]{:S(2)}) collective-permute-start(bf16[96,4224]{1,0:T(8,128)(2,1)} %collective-permute-done.1.refs_4_), channel_id=1, source_target_pairs={{0,3},{1,0},{2,1},{3,2},{4,7},{5,4},{6,5},{7,6},{8,11},{9,8},{10,9... | collective-permute-start | bytes 2433032 | tf_op jit(solution)/shard_map/ppermute | solution.py:255
  106.7 20.6 %collective-permute-start.13 = (bf16[96,4224]{1,0:T(8,128)(2,1)}, bf16[96,4224]{1,0:T(8,128)(2,1)S(1)}, u32[]{:S(2)}, u32[]{:S(2)}) collective-permute-start(bf16[96,4224]{1,0:T(8,128)(2,1)} %collective-permute-done.7), channel_id=1, source_target_pairs={{0,4},{4,0},{1,5},{5,1},{2,6},{6,2},{3,7},{7,3},{8,12},{12,8},{9,1... | collective-permute-start | bytes 2433032 | tf_op jit(solution)/shard_map/ppermute | solution.py:255
  109.2 18.1 %collective-permute-start.14 = (bf16[96,4224]{1,0:T(8,128)(2,1)S(1)}, bf16[96,4224]{1,0:T(8,128)(2,1)}, u32[]{:S(2)}, u32[]{:S(2)}) collective-permute-start(bf16[96,4224]{1,0:T(8,128)(2,1)S(1)} %collective-permute-done.9.refs_2_), channel_id=1, source_target_pairs={{3,27},{11,3},{19,11},{27,19},{7,31},{15,7},{23,15},{31,23},{35,59... | collective-permute-start | bytes 2433032 | tf_op jit(solution)/shard_map/ppermute | solution.py:261
  110.8 19.4 %collective-permute-start.15 = (bf16[96,4224]{1,0:T(8,128)(2,1)}, bf16[96,4224]{1,0:T(8,128)(2,1)}, u32[]{:S(2)}, u32[]{:S(2)}) collective-permute-start(bf16[96,4224]{1,0:T(8,128)(2,1)} %collective-permute-done.2.refs_2_), channel_id=1, source_target_pairs={{3,0},{0,1},{7,4},{4,5},{11,8},{8,9},{15,12},{12,13},{19,16},{16,1... | collective-permute-start | bytes 2433032 | tf_op jit(solution)/shard_map/ppermute | solution.py:329
